TPU v7x, 128 devices: a whole 4x4x4 slice. The times are simulated.
128 devices in a mesh: dp: 32 (over y, x, core), tensor: 4 (over z).
Axes of the slice: x: 4, y: 4, z: 4, core: 2. Of those that a mesh axis runs over, the one named last changes fastest.
Arguments:
- residual: bfloat16 [2048, 4608], P(('dp', 'tensor')), may hold values from -5.4 to 5.4
- queries: bfloat16 [2048, 2560], P('dp', 'tensor'), may hold values from -30 to 30
- new_keys: bfloat16 [2048, 2560], P('dp', 'tensor'), may hold values from -6 to 6
- new_values: bfloat16 [2048, 2560], P('dp', 'tensor'), may hold values from -6 to 6
- cache_keys: bfloat16 [32768, 2560], P('dp', 'tensor'), may hold values from -6 to 6
- cache_values: bfloat16 [32768, 2560], P('dp', 'tensor'), may hold values from -6 to 6
- out_weight: bfloat16 [2560, 4608], P('tensor', 'dp'), may hold values from -0.125 to 0.125
- norm_gain: float32 [4608], replicated, may hold values from 0.1 to 1.9
- route_ids: int32 [2048, 2], P(('dp', 'tensor')), may hold values from 0 to 7, all different within a row; in each aligned block of 16 rows (0 to 15, 16 to 31, ...) at most 5 rows name the same one
- route_weight: float32 [2048, 2], P(('dp', 'tensor')), may hold values from 0.2 to 1
- gate_weight: bfloat16 [4608, 98304], P(None, ('dp', 'tensor')), may hold values from -0.09375 to 0.09375
- up_weight: bfloat16 [4608, 98304], P(None, ('dp', 'tensor')), may hold values from -0.09375 to 0.09375
- down_weight: bfloat16 [98304, 4608], P(('dp', 'tensor')), may hold values from -0.0546875 to 0.0546875
Outputs:
- layer_out: bfloat16 [2048, 4608], P(('dp', 'tensor'))
Inputs may be any that keep to these rules, and one draw needn't show every extreme that they name: `route_ids`: within each aligned block of 16 rows (the tokens of one device of dp+tensor), no expert is named more than 5 times, a bound that some block reaches; the 2 experts of a row differ.
All inputs are finite; a program needn't handle non-finite values.
Results may differ from a plain program's by a relative error of at most 0.02055.
Values may be sent and summed in bfloat16 or wider, within the bound.
No kernel may reach another device: no remote copies, remote signals or barrier semaphores. Data moves between devices by JAX's collectives and lax.ppermute only.
A program may use at most 128 MiB of HBM per device.

v0:
```python
import math

import jax
import jax.numpy as jnp
from jax import lax
from jax.sharding import PartitionSpec as P

D = 4608
HD = 128
E = 8
TOP = 2


norm_eps = 1e-06
big_negative = -1e30


def from_behind(block, axis, distance):
    devices = range(lax.axis_size(axis))
    route = [((i - distance) % len(devices), i) for i in devices]
    return lax.ppermute(block, axis, route)


def body(
    residual,
    queries,
    new_keys,
    new_values,
    cache_keys,
    cache_values,
    out_weight,
    norm_gain,
    route_ids,
    route_weight,
    gate_weight,
    up_weight,
    down_weight,
):
    query_rows = queries.shape[0]
    cache_rows = cache_keys.shape[0]
    head_width = queries.shape[1]
    head_count = head_width // HD
    data_count = lax.axis_size("dp")
    tensor_count = lax.axis_size("tensor")
    data_index = lax.axis_index("dp")
    context_total = cache_rows * data_count
    local_keys = jnp.concatenate([cache_keys, new_keys], axis=0)
    local_values = jnp.concatenate([cache_values, new_values], axis=0)
    local_rows = local_keys.shape[0]
    row_index = jnp.arange(local_rows, dtype=jnp.int32)
    key_pos = jnp.where(
        row_index < cache_rows,
        data_index * cache_rows + row_index,
        context_total + data_index * query_rows + row_index - cache_rows,
    )
    key_heads = local_keys.reshape(local_rows, head_count, HD)
    value_heads = local_values.reshape(local_rows, head_count, HD)
    score_scale = 1.0 / math.sqrt(HD)

    def fold_keys(running, query_block, query_pos):
        block_rows = query_block.shape[0]
        query_heads = query_block.reshape(block_rows, head_count, HD)
        allowed = (key_pos[None, :] <= query_pos[:, None])[:, None, :]
        scores = (
            jnp.einsum("qhc,khc->qhk", query_heads, key_heads, preferred_element_type=jnp.float32)
            * score_scale
        )
        scores = jnp.where(allowed, scores, big_negative)
        old_max, old_sum, old_acc = running
        new_max = jnp.maximum(old_max, jnp.max(scores, axis=2))
        rescale = jnp.exp(old_max - new_max)
        weights = jnp.where(allowed, jnp.exp(scores - new_max[:, :, None]), 0.0)
        new_sum = old_sum * rescale + jnp.sum(weights, axis=2)
        product = jnp.einsum(
            "qhk,khc->qhc",
            weights.astype(jnp.bfloat16),
            value_heads,
            preferred_element_type=jnp.float32,
        )
        new_acc = old_acc * rescale[:, :, None] + product
        return (new_max, new_sum, new_acc)

    def anchor_pos(anchor):
        return context_total + anchor * query_rows + jnp.arange(query_rows, dtype=jnp.int32)

    own_state = fold_keys(
        (
            jnp.full((query_rows, head_count), big_negative, jnp.float32),
            jnp.zeros((query_rows, head_count), jnp.float32),
            jnp.zeros((query_rows, head_count, HD), jnp.float32),
        ),
        queries,
        anchor_pos(data_index),
    )

    def visit(step, carry):
        travelling, running = carry
        travelling = from_behind(travelling, "dp", 1)
        running = from_behind((running[0], running[1], running[2]), "dp", 1)
        anchor = (data_index - step - 1) % data_count
        return (travelling, fold_keys(running, travelling, anchor_pos(anchor)))

    last_queries, last_state = lax.fori_loop(0, data_count - 1, visit, (queries, own_state))
    final_max, final_sum, final_acc = from_behind(
        (last_state[0], last_state[1], last_state[2]), "dp", 1
    )
    attended = (
        (final_acc / final_sum[:, :, None]).reshape(query_rows, head_width).astype(jnp.bfloat16)
    )
    head_terms = jnp.dot(
        attended,
        lax.all_gather(out_weight, "dp", axis=1, tiled=True),
        preferred_element_type=jnp.float32,
    )
    own_rows = lax.psum_scatter(head_terms, "tensor", scatter_dimension=0, tiled=True)
    stream = (residual.astype(jnp.float32) + own_rows).astype(jnp.bfloat16)
    stream_f = stream.astype(jnp.float32)
    normed = (
        stream_f
        * lax.rsqrt(jnp.mean(stream_f * stream_f, axis=1, keepdims=True) + norm_eps)
        * norm_gain
    ).astype(jnp.bfloat16)
    tok_src = residual.shape[0]
    cap_rows = (9 * tok_src + 4 * E - 1) // (4 * E)
    slot_total = E * cap_rows
    route_flat = route_ids.reshape(-1)
    onehot = (route_flat[:, None] == jnp.arange(E, dtype=jnp.int32)[None, :]).astype(jnp.int32)
    before = jnp.cumsum(onehot, axis=0) - onehot
    slot_index = jnp.sum(before * onehot, axis=1)
    slot_rows = route_flat * cap_rows + slot_index
    matches = (
        slot_rows.reshape(tok_src, TOP)[:, :, None]
        == jnp.arange(slot_total, dtype=jnp.int32)[None, None, :]
    )
    placing = jnp.transpose(jnp.sum(matches, axis=1)).astype(jnp.bfloat16)
    combiner = jnp.sum(matches * route_weight[:, :, None], axis=1)
    packed = jnp.dot(placing, normed, preferred_element_type=jnp.float32).astype(jnp.bfloat16)
    device_count = data_count * tensor_count
    group_size = device_count // E
    copies = jnp.broadcast_to(
        packed.reshape(E, 1, cap_rows, D), (E, group_size, cap_rows, D)
    ).reshape(device_count * cap_rows, D)
    arrived = lax.all_to_all(copies, ("dp", "tensor"), split_axis=0, concat_axis=0, tiled=True)
    gate_val = jnp.dot(arrived, gate_weight, preferred_element_type=jnp.float32)
    up_val = jnp.dot(arrived, up_weight, preferred_element_type=jnp.float32)
    hidden = (jax.nn.silu(gate_val) * up_val).astype(jnp.bfloat16)
    partial_value = jnp.dot(hidden, down_weight, preferred_element_type=jnp.float32).astype(
        jnp.bfloat16
    )
    returned = lax.all_to_all(
        partial_value, ("dp", "tensor"), split_axis=0, concat_axis=0, tiled=True
    )
    expert_sums = jnp.sum(
        returned.reshape(E, group_size, cap_rows, D), axis=1, dtype=jnp.float32
    ).reshape(slot_total, D)
    moe_out = jnp.dot(
        combiner, expert_sums, precision=lax.Precision.HIGHEST, preferred_element_type=jnp.float32
    )
    return (stream_f + moe_out).astype(jnp.bfloat16)


def solution(mesh):
    placed = (
        P(("dp", "tensor"), None),
        P("dp", "tensor"),
        P("dp", "tensor"),
        P("dp", "tensor"),
        P("dp", "tensor"),
        P("dp", "tensor"),
        P("tensor", "dp"),
        P(),
        P(("dp", "tensor"), None),
        P(("dp", "tensor"), None),
        P(None, ("dp", "tensor")),
        P(None, ("dp", "tensor")),
        P(("dp", "tensor"), None),
    )
    return jax.shard_map(
        body, mesh=mesh, in_specs=placed, out_specs=P(("dp", "tensor"), None), check_vma=False
    )
```

profile of v0, /device:TPU:0, one launch (start us, length us, event | category | flops | bytes accessed | tf_op | source)
XLA Modules:
  0.0 660.4 jit_solution(15595093963371476847)
XLA Ops:
  22.0 305.9 %while.22 = (s32[]{:T(128)}, bf16[64,640]{1,0:T(8,128)(2,1)S(1)}, f32[64,5]{0,1:T(8,128)S(1)}, f32[64,5]{0,1:T(8,128)S(1)}, f32[64,5,128]{2,0,1:T(8,128)S(1)}, /...) while((s32[]{:T(128)}, bf16[64,640]{1,0:T(8,128)(2,1)S(1)}, ...), condition=%wide.region_5.6_spmd.clone, body=%wide.region_2.5_spmd.clone.sunk | while | flops 181549072 | bytes 8836070 | solution.py:103
  34.1 6.8 %collective-permute-done = bf16[64,640]{1,0:T(8,128)(2,1)S(1)} collective-permute-done((bf16[64,640]{1,0:T(8,128)(2,1)S(1)}, bf16[64,640]{1,0:T(8,128)(2,1)S(1)}, u32[]{:S(2)}, u32[]{:S(2)}) %collective-permute-start) | collective-permute-done | bytes 81952 | tf_op jit(solution)/shard_map/while/body/eval_jaxpr/ppermute | solution.py:21
  43.7 8.4 %collective-permute-done = bf16[64,640]{1,0:T(8,128)(2,1)S(1)} collective-permute-done((bf16[64,640]{1,0:T(8,128)(2,1)S(1)}, bf16[64,640]{1,0:T(8,128)(2,1)S(1)}, u32[]{:S(2)}, u32[]{:S(2)}) %collective-permute-start) | collective-permute-done | bytes 81952 | tf_op jit(solution)/shard_map/while/body/eval_jaxpr/ppermute | solution.py:21
  58.7 6.8 %collective-permute-done = bf16[64,640]{1,0:T(8,128)(2,1)S(1)} collective-permute-done((bf16[64,640]{1,0:T(8,128)(2,1)S(1)}, bf16[64,640]{1,0:T(8,128)(2,1)S(1)}, u32[]{:S(2)}, u32[]{:S(2)}) %collective-permute-start) | collective-permute-done | bytes 81952 | tf_op jit(solution)/shard_map/while/body/eval_jaxpr/ppermute | solution.py:21
  68.4 6.8 %collective-permute-done = bf16[64,640]{1,0:T(8,128)(2,1)S(1)} collective-permute-done((bf16[64,640]{1,0:T(8,128)(2,1)S(1)}, bf16[64,640]{1,0:T(8,128)(2,1)S(1)}, u32[]{:S(2)}, u32[]{:S(2)}) %collective-permute-start) | collective-permute-done | bytes 81952 | tf_op jit(solution)/shard_map/while/body/eval_jaxpr/ppermute | solution.py:21
  78.0 6.8 %collective-permute-done = bf16[64,640]{1,0:T(8,128)(2,1)S(1)} collective-permute-done((bf16[64,640]{1,0:T(8,128)(2,1)S(1)}, bf16[64,640]{1,0:T(8,128)(2,1)S(1)}, u32[]{:S(2)}, u32[]{:S(2)}) %collective-permute-start) | collective-permute-done | bytes 81952 | tf_op jit(solution)/shard_map/while/body/eval_jaxpr/ppermute | solution.py:21
  87.6 6.8 %collective-permute-done = bf16[64,640]{1,0:T(8,128)(2,1)S(1)} collective-permute-done((bf16[64,640]{1,0:T(8,128)(2,1)S(1)}, bf16[64,640]{1,0:T(8,128)(2,1)S(1)}, u32[]{:S(2)}, u32[]{:S(2)}) %collective-permute-start) | collective-permute-done | bytes 81952 | tf_op jit(solution)/shard_map/while/body/eval_jaxpr/ppermute | solution.py:21
  97.3 6.8 %collective-permute-done = bf16[64,640]{1,0:T(8,128)(2,1)S(1)} collective-permute-done((bf16[64,640]{1,0:T(8,128)(2,1)S(1)}, bf16[64,640]{1,0:T(8,128)(2,1)S(1)}, u32[]{:S(2)}, u32[]{:S(2)}) %collective-permute-start) | collective-permute-done | bytes 81952 | tf_op jit(solution)/shard_map/while/body/eval_jaxpr/ppermute | solution.py:21
  126.2 6.8 %collective-permute-done = bf16[64,640]{1,0:T(8,128)(2,1)S(1)} collective-permute-done((bf16[64,640]{1,0:T(8,128)(2,1)S(1)}, bf16[64,640]{1,0:T(8,128)(2,1)S(1)}, u32[]{:S(2)}, u32[]{:S(2)}) %collective-permute-start) | collective-permute-done | bytes 81952 | tf_op jit(solution)/shard_map/while/body/eval_jaxpr/ppermute | solution.py:21
  222.5 6.8 %collective-permute-done = bf16[64,640]{1,0:T(8,128)(2,1)S(1)} collective-permute-done((bf16[64,640]{1,0:T(8,128)(2,1)S(1)}, bf16[64,640]{1,0:T(8,128)(2,1)S(1)}, u32[]{:S(2)}, u32[]{:S(2)}) %collective-permute-start) | collective-permute-done | bytes 81952 | tf_op jit(solution)/shard_map/while/body/eval_jaxpr/ppermute | solution.py:21
  232.1 6.8 %collective-permute-done = bf16[64,640]{1,0:T(8,128)(2,1)S(1)} collective-permute-done((bf16[64,640]{1,0:T(8,128)(2,1)S(1)}, bf16[64,640]{1,0:T(8,128)(2,1)S(1)}, u32[]{:S(2)}, u32[]{:S(2)}) %collective-permute-start) | collective-permute-done | bytes 81952 | tf_op jit(solution)/shard_map/while/body/eval_jaxpr/ppermute | solution.py:21
  251.4 6.8 %collective-permute-done = bf16[64,640]{1,0:T(8,128)(2,1)S(1)} collective-permute-done((bf16[64,640]{1,0:T(8,128)(2,1)S(1)}, bf16[64,640]{1,0:T(8,128)(2,1)S(1)}, u32[]{:S(2)}, u32[]{:S(2)}) %collective-permute-start) | collective-permute-done | bytes 81952 | tf_op jit(solution)/shard_map/while/body/eval_jaxpr/ppermute | solution.py:21
  261.0 6.8 %collective-permute-done = bf16[64,640]{1,0:T(8,128)(2,1)S(1)} collective-permute-done((bf16[64,640]{1,0:T(8,128)(2,1)S(1)}, bf16[64,640]{1,0:T(8,128)(2,1)S(1)}, u32[]{:S(2)}, u32[]{:S(2)}) %collective-permute-start) | collective-permute-done | bytes 81952 | tf_op jit(solution)/shard_map/while/body/eval_jaxpr/ppermute | solution.py:21
  280.3 6.8 %collective-permute-done = bf16[64,640]{1,0:T(8,128)(2,1)S(1)} collective-permute-done((bf16[64,640]{1,0:T(8,128)(2,1)S(1)}, bf16[64,640]{1,0:T(8,128)(2,1)S(1)}, u32[]{:S(2)}, u32[]{:S(2)}) %collective-permute-start) | collective-permute-done | bytes 81952 | tf_op jit(solution)/shard_map/while/body/eval_jaxpr/ppermute | solution.py:21
  318.8 6.8 %collective-permute-done = bf16[64,640]{1,0:T(8,128)(2,1)S(1)} collective-permute-done((bf16[64,640]{1,0:T(8,128)(2,1)S(1)}, bf16[64,640]{1,0:T(8,128)(2,1)S(1)}, u32[]{:S(2)}, u32[]{:S(2)}) %collective-permute-start) | collective-permute-done | bytes 81952 | tf_op jit(solution)/shard_map/while/body/eval_jaxpr/ppermute | solution.py:21
  328.1 8.0 %collective-permute-done.5 = f32[64,5]{0,1:T(8,128)S(1)} collective-permute-done((f32[64,5]{0,1:T(8,128)S(1)}, f32[64,5]{0,1:T(8,128)S(1)}, u32[]{:S(2)}, u32[]{:S(2)}) %collective-permute-start.5) | collective-permute-done | bytes 1312 | tf_op jit(solution)/shard_map/ppermute | solution.py:21
  342.5 20.7 %reduce-scatter.2.cloned.1.call-done = f32[16,4608]{1,0:T(8,128)} async-done(((f32[64,4608]{1,0:T(8,128)}), f32[16,4608]{1,0:T(8,128)}) %reduce-scatter.2.cloned.1.call-update) | async-done | bytes 294928 | tf_op jit(solution)/shard_map/reduce_scatter | solution.py:115
  365.5 116.8 %all_to_all.21 = bf16[128,5,4608]{2,1,0:T(8,128)(2,1)} all-to-all(bf16[128,5,4608]{2,1,0:T(8,128)(2,1)S(1)} %bitcast.70), channel_id=1, replica_groups=mesh['dp'=32,'tensor'=4] {'dp','tensor'}, dimensions={0} | all-to-all | bytes 11796480 | tf_op jit(solution)/shard_map/all_to_all | solution.py:143
  482.3 9.3 %all_to_all.16 = bf16[640,4608]{1,0:T(8,128)(2,1)} reshape(bf16[128,5,4608]{2,1,0:T(8,128)(2,1)} %all_to_all.21) | data formatting | bytes 11796480 | tf_op jit(solution)/shard_map/all_to_all | solution.py:143
  491.6 9.0 %fusion.43 = f32[640,768]{1,0:T(8,128)S(1)} fusion(bf16[640,4608]{1,0:T(8,128)(2,1)} %all_to_all.16, bf16[4608,768]{1,0:T(8,128)(2,1)} %param.25), kind=kOutput, calls=%fused_computation.74 | convolution fusion | flops 4529848320 | bytes 14942208 | tf_op jit(solution)/shard_map/dot_general | solution.py:144
  500.6 7.9 %multiply_convert_fusion = bf16[640,768]{1,0:T(8,128)(2,1)S(1)} fusion(f32[640,768]{1,0:T(8,128)S(1)} %fusion.43, bf16[640,4608]{1,0:T(8,128)(2,1)S(1)} %copy-done.1, bf16[4608,768]{1,0:T(8,128)(2,1)} %param.26), kind=kOutput, calls=%fused_computation.29 | convolution fusion | flops 4532797440 | bytes 15925248 | tf_op jit(solution)/shard_map/dot_general | solution.py:145
  508.4 9.6 %convolution_convert_fusion = bf16[640,4608]{1,0:T(8,128)(2,1)} fusion(bf16[640,768]{1,0:T(8,128)(2,1)S(1)} %multiply_convert_fusion, bf16[768,4608]{1,0:T(8,128)(2,1)} %param.27), kind=kOutput, calls=%fused_computation.22 | convolution fusion | flops 4532797440 | bytes 13959168 | tf_op jit(solution)/shard_map/dot_general | solution.py:147
  518.0 9.0 %all_to_all.17 = bf16[128,5,4608]{2,1,0:T(8,128)(2,1)} reshape(bf16[640,4608]{1,0:T(8,128)(2,1)} %convolution_convert_fusion) | data formatting | bytes 11796480 | tf_op jit(solution)/shard_map/all_to_all | solution.py:150
  533.5 113.1 %all-to-all-done.1 = bf16[128,5,4608]{2,1,0:T(8,128)(2,1)} async-done(((bf16[128,5,4608]{2,1,0:T(8,128)(2,1)}), bf16[128,5,4608]{2,1,0:T(8,128)(2,1)}, u32[]{:S(2)}, u32[]{:S(2)}) %all-to-all-start.1) | async-done | bytes 5898272 | tf_op jit(solution)/shard_map/all_to_all | solution.py:150
  (572 shorter events, 243.2 us)
Async XLA Ops:
  6.5 329.6 %all-gather.2.cloned.1.call-start = ((), (), s32[]{:S(2)}) async-start(), calls=%async_computation.3 | async-start | bytes 6082560 | tf_op jit(solution)/shard_map/all_gather | solution.py:112
  7.4 355.7 %reduce-scatter.2.cloned.1.call-start = ((), (), s32[]{:S(2)}) async-start(), calls=%async_computation.4 | async-start | bytes 1474560 | tf_op jit(solution)/shard_map/reduce_scatter | solution.py:115
  23.9 9.2 %collective-permute-start.3 = (f32[64,5,128]{2,0,1:T(8,128)S(1)}, f32[64,5,128]{2,0,1:T(8,128)S(1)}, u32[]{:S(2)}, u32[]{:S(2)}) collective-permute-start(f32[64,5,128]{2,0,1:T(8,128)S(1)} %get-tuple-element.404), channel_id=1, source_target_pairs={{124,0},{0,4},{4,8},{8,12},{12,16},{16,20},{20,24},{24,28},{28,32}... | collective-permute-start | bytes 491528 | tf_op jit(solution)/shard_map/while/body/eval_jaxpr/ppermute | solution.py:21
  33.9 8.9 %collective-permute-start.3 = (f32[64,5,128]{2,0,1:T(8,128)S(1)}, f32[64,5,128]{2,0,1:T(8,128)S(1)}, u32[]{:S(2)}, u32[]{:S(2)}) collective-permute-start(f32[64,5,128]{2,0,1:T(8,128)S(1)} %get-tuple-element.404), channel_id=1, source_target_pairs={{124,0},{0,4},{4,8},{8,12},{12,16},{16,20},{20,24},{24,28},{28,32}... | collective-permute-start | bytes 491528 | tf_op jit(solution)/shard_map/while/body/eval_jaxpr/ppermute | solution.py:21
  43.3 8.9 %collective-permute-start = (bf16[64,640]{1,0:T(8,128)(2,1)S(1)}, bf16[64,640]{1,0:T(8,128)(2,1)S(1)}, u32[]{:S(2)}, u32[]{:S(2)}) collective-permute-start(bf16[64,640]{1,0:T(8,128)(2,1)S(1)} %get-tuple-element.401), channel_id=1, source_target_pairs={{124,0},{0,4},{4,8},{8,12},{12,16},{16,20},{20,24},{24,28},{28,32}... | collective-permute-start | bytes 245768 | tf_op jit(solution)/shard_map/while/body/eval_jaxpr/ppermute | solution.py:21
  43.3 9.5 %collective-permute-start.1 = (f32[64,5]{0,1:T(8,128)S(1)}, f32[64,5]{0,1:T(8,128)S(1)}, u32[]{:S(2)}, u32[]{:S(2)}) collective-permute-start(f32[64,5]{0,1:T(8,128)S(1)} %get-tuple-element.402), channel_id=1, source_target_pairs={{124,0},{0,4},{4,8},{8,12},{12,16},{16,20},{20,24},{24,28},{28,32}... | collective-permute-start | bytes 3848 | tf_op jit(solution)/shard_map/while/body/eval_jaxpr/ppermute | solution.py:21
  43.4 9.9 %collective-permute-start.2 = (f32[64,5]{0,1:T(8,128)S(1)}, f32[64,5]{0,1:T(8,128)S(1)}, u32[]{:S(2)}, u32[]{:S(2)}) collective-permute-start(f32[64,5]{0,1:T(8,128)S(1)} %get-tuple-element.403), channel_id=1, source_target_pairs={{124,0},{0,4},{4,8},{8,12},{12,16},{16,20},{20,24},{24,28},{28,32}... | collective-permute-start | bytes 3848 | tf_op jit(solution)/shard_map/while/body/eval_jaxpr/ppermute | solution.py:21
  43.5 14.2 %collective-permute-start.3 = (f32[64,5,128]{2,0,1:T(8,128)S(1)}, f32[64,5,128]{2,0,1:T(8,128)S(1)}, u32[]{:S(2)}, u32[]{:S(2)}) collective-permute-start(f32[64,5,128]{2,0,1:T(8,128)S(1)} %get-tuple-element.404), channel_id=1, source_target_pairs={{124,0},{0,4},{4,8},{8,12},{12,16},{16,20},{20,24},{24,28},{28,32}... | collective-permute-start | bytes 491528 | tf_op jit(solution)/shard_map/while/body/eval_jaxpr/ppermute | solution.py:21
  68.1 8.9 %collective-permute-start.3 = (f32[64,5,128]{2,0,1:T(8,128)S(1)}, f32[64,5,128]{2,0,1:T(8,128)S(1)}, u32[]{:S(2)}, u32[]{:S(2)}) collective-permute-start(f32[64,5,128]{2,0,1:T(8,128)S(1)} %get-tuple-element.404), channel_id=1, source_target_pairs={{124,0},{0,4},{4,8},{8,12},{12,16},{16,20},{20,24},{24,28},{28,32}... | collective-permute-start | bytes 491528 | tf_op jit(solution)/shard_map/while/body/eval_jaxpr/ppermute | solution.py:21
  77.7 8.9 %collective-permute-start.3 = (f32[64,5,128]{2,0,1:T(8,128)S(1)}, f32[64,5,128]{2,0,1:T(8,128)S(1)}, u32[]{:S(2)}, u32[]{:S(2)}) collective-permute-start(f32[64,5,128]{2,0,1:T(8,128)S(1)} %get-tuple-element.404), channel_id=1, source_target_pairs={{124,0},{0,4},{4,8},{8,12},{12,16},{16,20},{20,24},{24,28},{28,32}... | collective-permute-start | bytes 491528 | tf_op jit(solution)/shard_map/while/body/eval_jaxpr/ppermute | solution.py:21
  87.4 8.9 %collective-permute-start.3 = (f32[64,5,128]{2,0,1:T(8,128)S(1)}, f32[64,5,128]{2,0,1:T(8,128)S(1)}, u32[]{:S(2)}, u32[]{:S(2)}) collective-permute-start(f32[64,5,128]{2,0,1:T(8,128)S(1)} %get-tuple-element.404), channel_id=1, source_target_pairs={{124,0},{0,4},{4,8},{8,12},{12,16},{16,20},{20,24},{24,28},{28,32}... | collective-permute-start | bytes 491528 | tf_op jit(solution)/shard_map/while/body/eval_jaxpr/ppermute | solution.py:21
  97.0 8.9 %collective-permute-start.3 = (f32[64,5,128]{2,0,1:T(8,128)S(1)}, f32[64,5,128]{2,0,1:T(8,128)S(1)}, u32[]{:S(2)}, u32[]{:S(2)}) collective-permute-start(f32[64,5,128]{2,0,1:T(8,128)S(1)} %get-tuple-element.404), channel_id=1, source_target_pairs={{124,0},{0,4},{4,8},{8,12},{12,16},{16,20},{20,24},{24,28},{28,32}... | collective-permute-start | bytes 491528 | tf_op jit(solution)/shard_map/while/body/eval_jaxpr/ppermute | solution.py:21
  106.6 8.9 %collective-permute-start.3 = (f32[64,5,128]{2,0,1:T(8,128)S(1)}, f32[64,5,128]{2,0,1:T(8,128)S(1)}, u32[]{:S(2)}, u32[]{:S(2)}) collective-permute-start(f32[64,5,128]{2,0,1:T(8,128)S(1)} %get-tuple-element.404), channel_id=1, source_target_pairs={{124,0},{0,4},{4,8},{8,12},{12,16},{16,20},{20,24},{24,28},{28,32}... | collective-permute-start | bytes 491528 | tf_op jit(solution)/shard_map/while/body/eval_jaxpr/ppermute | solution.py:21
  116.3 8.9 %collective-permute-start.3 = (f32[64,5,128]{2,0,1:T(8,128)S(1)}, f32[64,5,128]{2,0,1:T(8,128)S(1)}, u32[]{:S(2)}, u32[]{:S(2)}) collective-permute-start(f32[64,5,128]{2,0,1:T(8,128)S(1)} %get-tuple-element.404), channel_id=1, source_target_pairs={{124,0},{0,4},{4,8},{8,12},{12,16},{16,20},{20,24},{24,28},{28,32}... | collective-permute-start | bytes 491528 | tf_op jit(solution)/shard_map/while/body/eval_jaxpr/ppermute | solution.py:21
  125.9 8.9 %collective-permute-start.3 = (f32[64,5,128]{2,0,1:T(8,128)S(1)}, f32[64,5,128]{2,0,1:T(8,128)S(1)}, u32[]{:S(2)}, u32[]{:S(2)}) collective-permute-start(f32[64,5,128]{2,0,1:T(8,128)S(1)} %get-tuple-element.404), channel_id=1, source_target_pairs={{124,0},{0,4},{4,8},{8,12},{12,16},{16,20},{20,24},{24,28},{28,32}... | collective-permute-start | bytes 491528 | tf_op jit(solution)/shard_map/while/body/eval_jaxpr/ppermute | solution.py:21
  164.4 8.9 %collective-permute-start.3 = (f32[64,5,128]{2,0,1:T(8,128)S(1)}, f32[64,5,128]{2,0,1:T(8,128)S(1)}, u32[]{:S(2)}, u32[]{:S(2)}) collective-permute-start(f32[64,5,128]{2,0,1:T(8,128)S(1)} %get-tuple-element.404), channel_id=1, source_target_pairs={{124,0},{0,4},{4,8},{8,12},{12,16},{16,20},{20,24},{24,28},{28,32}... | collective-permute-start | bytes 491528 | tf_op jit(solution)/shard_map/while/body/eval_jaxpr/ppermute | solution.py:21
  193.3 8.9 %collective-permute-start.3 = (f32[64,5,128]{2,0,1:T(8,128)S(1)}, f32[64,5,128]{2,0,1:T(8,128)S(1)}, u32[]{:S(2)}, u32[]{:S(2)}) collective-permute-start(f32[64,5,128]{2,0,1:T(8,128)S(1)} %get-tuple-element.404), channel_id=1, source_target_pairs={{124,0},{0,4},{4,8},{8,12},{12,16},{16,20},{20,24},{24,28},{28,32}... | collective-permute-start | bytes 491528 | tf_op jit(solution)/shard_map/while/body/eval_jaxpr/ppermute | solution.py:21
  212.6 8.9 %collective-permute-start.3 = (f32[64,5,128]{2,0,1:T(8,128)S(1)}, f32[64,5,128]{2,0,1:T(8,128)S(1)}, u32[]{:S(2)}, u32[]{:S(2)}) collective-permute-start(f32[64,5,128]{2,0,1:T(8,128)S(1)} %get-tuple-element.404), channel_id=1, source_target_pairs={{124,0},{0,4},{4,8},{8,12},{12,16},{16,20},{20,24},{24,28},{28,32}... | collective-permute-start | bytes 491528 | tf_op jit(solution)/shard_map/while/body/eval_jaxpr/ppermute | solution.py:21
  222.2 8.9 %collective-permute-start.3 = (f32[64,5,128]{2,0,1:T(8,128)S(1)}, f32[64,5,128]{2,0,1:T(8,128)S(1)}, u32[]{:S(2)}, u32[]{:S(2)}) collective-permute-start(f32[64,5,128]{2,0,1:T(8,128)S(1)} %get-tuple-element.404), channel_id=1, source_target_pairs={{124,0},{0,4},{4,8},{8,12},{12,16},{16,20},{20,24},{24,28},{28,32}... | collective-permute-start | bytes 491528 | tf_op jit(solution)/shard_map/while/body/eval_jaxpr/ppermute | solution.py:21
  231.9 8.9 %collective-permute-start.3 = (f32[64,5,128]{2,0,1:T(8,128)S(1)}, f32[64,5,128]{2,0,1:T(8,128)S(1)}, u32[]{:S(2)}, u32[]{:S(2)}) collective-permute-start(f32[64,5,128]{2,0,1:T(8,128)S(1)} %get-tuple-element.404), channel_id=1, source_target_pairs={{124,0},{0,4},{4,8},{8,12},{12,16},{16,20},{20,24},{24,28},{28,32}... | collective-permute-start | bytes 491528 | tf_op jit(solution)/shard_map/while/body/eval_jaxpr/ppermute | solution.py:21
  251.1 8.9 %collective-permute-start.3 = (f32[64,5,128]{2,0,1:T(8,128)S(1)}, f32[64,5,128]{2,0,1:T(8,128)S(1)}, u32[]{:S(2)}, u32[]{:S(2)}) collective-permute-start(f32[64,5,128]{2,0,1:T(8,128)S(1)} %get-tuple-element.404), channel_id=1, source_target_pairs={{124,0},{0,4},{4,8},{8,12},{12,16},{16,20},{20,24},{24,28},{28,32}... | collective-permute-start | bytes 491528 | tf_op jit(solution)/shard_map/while/body/eval_jaxpr/ppermute | solution.py:21
  260.7 8.9 %collective-permute-start.3 = (f32[64,5,128]{2,0,1:T(8,128)S(1)}, f32[64,5,128]{2,0,1:T(8,128)S(1)}, u32[]{:S(2)}, u32[]{:S(2)}) collective-permute-start(f32[64,5,128]{2,0,1:T(8,128)S(1)} %get-tuple-element.404), channel_id=1, source_target_pairs={{124,0},{0,4},{4,8},{8,12},{12,16},{16,20},{20,24},{24,28},{28,32}... | collective-permute-start | bytes 491528 | tf_op jit(solution)/shard_map/while/body/eval_jaxpr/ppermute | solution.py:21
  270.4 8.9 %collective-permute-start.3 = (f32[64,5,128]{2,0,1:T(8,128)S(1)}, f32[64,5,128]{2,0,1:T(8,128)S(1)}, u32[]{:S(2)}, u32[]{:S(2)}) collective-permute-start(f32[64,5,128]{2,0,1:T(8,128)S(1)} %get-tuple-element.404), channel_id=1, source_target_pairs={{124,0},{0,4},{4,8},{8,12},{12,16},{16,20},{20,24},{24,28},{28,32}... | collective-permute-start | bytes 491528 | tf_op jit(solution)/shard_map/while/body/eval_jaxpr/ppermute | solution.py:21
  527.0 119.6 %all-to-all-start.1 = ((bf16[128,5,4608]{2,1,0:T(8,128)(2,1)}), bf16[128,5,4608]{2,1,0:T(8,128)(2,1)}, u32[]{:S(2)}, u32[]{:S(2)}) async-start(bf16[128,5,4608]{2,1,0:T(8,128)(2,1)} %all_to_all.17), calls=%async_computation.2 | async-start | bytes 18874368 | tf_op jit(solution)/shard_map/all_to_all | solution.py:150
  (113 other events, 924.0 us)
Sparse Core Ops, SparseCore 0:
  9.7 52.7 all-gather.1
  341.9 21.2 reduce-scatter.1
where the time goes:
time: 665 us; the launch traced here: 660 us
  waiting for transfers between devices  377 us (57%)
  blocking collectives  117 us (18%)
  matrix products  72.9 us (11%)
  local copies, waits for them, and re-layouts  30 us (5%)
  other arithmetic  27.3 us (4%)
  starting transfers between devices  19 us (3%)
  between operations  13.6 us (2%)
    ppermute x126, waiting for transfers between devices, from_behind(): return lax.ppermute(block, axis, route)  243 us
    all_to_all x1, blocking collectives, body(): lax.all_to_all(copies, ('dp', 'tensor'), split_axis=0, concat_axis=0, til...  117 us
    all_to_all x1, waiting for transfers between devices, body(): lax.all_to_all(partial_value, ('dp', 'tensor'), split_axis=0, concat_axis...  113 us
    dot_general x32, matrix products, fold_keys(): jnp.einsum('qhc,khc->qhk', query_heads, key_heads, preferred_element_type...  21 us
    reduce_scatter x1, waiting for transfers between devices, body(): lax.psum_scatter(head_terms, 'tensor', scatter_dimension=0, tiled=True)  20.7 us
    dot_general x32, matrix products, fold_keys(): jnp.einsum('qhk,khc->qhc', weights.astype(jnp.bfloat16), value_heads, pre...  18.4 us
    reduce_sum x32, other arithmetic, fold_keys(): new_sum = old_sum * rescale + jnp.sum(weights, axis=2)  14.1 us
  transfers between devices with their start and end apart: 129, of which 65 were waited for; matrix products, arithmetic and copies ran while one was open for 10% of the time, Pallas kernels for 0%

commit v1 on v0

v1 whole, which is shorter than its diff:
```python
import functools
import math

import jax
import jax.numpy as jnp
from jax import lax
from jax.experimental import pallas as pl
from jax.experimental.pallas import tpu as pltpu
from jax.sharding import Mesh, PartitionSpec as P

D = 4608
HD = 128
HEADS = 5
E = 8
TOP = 2
CAP = 5
NZ = 4
PLANE = 16
Q_DEV = 64
SLICE = D // NZ
ROWS = 24
USED = NZ * CAP
PACK = 128
WIDE = HEADS * HD + PACK
NORM_EPS = 1e-06
NEGATIVE = -1e30
TO_BASE2 = math.log2(math.e) / math.sqrt(HD)

XY = ("y", "xh", "xl")
ZXY = ("z", "y", "xh", "xl")
F32 = jnp.float32
BF16 = jnp.bfloat16


def params(mib):
    return pltpu.CompilerParams(vmem_limit_bytes=mib * 2**20)


def exchange(block, axes):
    return lax.all_to_all(block, axes, split_axis=0, concat_axis=0, tiled=True)


def other_core(block):
    return lax.ppermute(block, "c", [(0, 1), (1, 0)])


def three_parts(value):
    high = value.astype(BF16).astype(F32)
    rest = value - high
    middle = rest.astype(BF16).astype(F32)
    return high, middle, (rest - middle).astype(BF16).astype(F32)


def dot_nt(a, b, **kw):
    return lax.dot_general(a, b, (((1,), (1,)), ((), ())), preferred_element_type=F32, **kw)


def dot_nn(a, b, **kw):
    return lax.dot_general(a, b, (((1,), (0,)), ((), ())), preferred_element_type=F32, **kw)


Q_BLOCK = 256


def attend_kernel(place_ref, q_ref, ka_ref, kb_ref, na_ref, nb_ref, va_ref, vb_ref, wa_ref, wb_ref, out_ref):
    core, mine = place_ref[0], place_ref[1]
    row = lax.broadcasted_iota(jnp.int32, (Q_BLOCK, HD), 0)
    lane = lax.broadcasted_iota(jnp.int32, (Q_BLOCK, HD), 1)
    block = pl.program_id(0) * (Q_BLOCK // Q_DEV) + row // Q_DEV
    q_pos = (block * 2 + core) * Q_DEV + row % Q_DEV
    k_pos = jnp.where(lane < Q_DEV, mine * Q_DEV + lane, (mine + 1 - 2 * core) * Q_DEV + lane - Q_DEV)
    allowed = k_pos <= q_pos
    pack = jnp.zeros((Q_BLOCK, PACK), F32)
    for h in range(HEADS):
        cols = slice(h * HD, (h + 1) * HD)
        q = q_ref[:, cols]
        s1 = dot_nt(q, ka_ref[:, cols])
        s2 = dot_nt(q, kb_ref[:, cols])
        fresh = jnp.concatenate([na_ref[:, cols], nb_ref[:, cols]], axis=0)
        s3 = jnp.where(allowed, dot_nt(q, fresh), NEGATIVE)
        top = jnp.maximum(
            jnp.maximum(jnp.max(s1, axis=1, keepdims=True), jnp.max(s2, axis=1, keepdims=True)),
            jnp.max(s3, axis=1, keepdims=True),
        ) * TO_BASE2
        w1 = jnp.exp2(s1 * TO_BASE2 - top)
        w2 = jnp.exp2(s2 * TO_BASE2 - top)
        w3 = jnp.exp2(s3 * TO_BASE2 - top)
        total = (
            jnp.sum(w1, axis=1, keepdims=True)
            + jnp.sum(w2, axis=1, keepdims=True)
            + jnp.sum(w3, axis=1, keepdims=True)
        )
        fresh_v = jnp.concatenate([wa_ref[:, cols], wb_ref[:, cols]], axis=0)
        acc = (
            dot_nn(w1.astype(BF16), va_ref[:, cols])
            + dot_nn(w2.astype(BF16), vb_ref[:, cols])
            + dot_nn(w3.astype(BF16), fresh_v)
        )
        out_ref[:, cols] = (acc / total).astype(BF16)
        for part, value in enumerate(three_parts(top + jnp.log2(total))):
            pack = jnp.where(lane == part * 8 + h, value, pack)
    out_ref[:, HEADS * HD :] = pack.astype(BF16)


def attend(place, q, ka, kb, na, nb, va, vb, wa, wb):
    rows = q.shape[0]
    whole = lambda a: pl.BlockSpec(a.shape, lambda i: (0, 0))
    keys = (ka, kb, na, nb, va, vb, wa, wb)
    return pl.pallas_call(
        attend_kernel,
        grid=(rows // Q_BLOCK,),
        out_shape=jax.ShapeDtypeStruct((rows, WIDE), BF16),
        in_specs=[
            pl.BlockSpec(memory_space=pltpu.SMEM),
            pl.BlockSpec((Q_BLOCK, HEADS * HD), lambda i: (i, 0)),
            *[whole(a) for a in keys],
        ],
        out_specs=pl.BlockSpec((Q_BLOCK, WIDE), lambda i: (i, 0)),
        compiler_params=params(56),
        cost_estimate=pl.CostEstimate(flops=11 * 10**9, bytes_accessed=8 * 10**6, transcendentals=11 * 10**6),
        name="attend",
    )(place, q, *keys)


def project_kernel(parts_ref, weight_ref, out_ref, attended_ref):
    @pl.when(pl.program_id(0) == 0)
    def _():
        count = parts_ref.shape[0]
        sums = [
            parts_ref[i, :, HEADS * HD :].astype(F32) for i in range(count)
        ]
        for h in range(HEADS):
            cols = slice(h * HD, (h + 1) * HD)
            logs = [
                s[:, h : h + 1] + s[:, 8 + h : 9 + h] + s[:, 16 + h : 17 + h] for s in sums
            ]
            top = functools.reduce(jnp.maximum, logs)
            shares = [jnp.exp2(v - top) for v in logs]
            total = functools.reduce(jnp.add, shares)
            acc = functools.reduce(
                jnp.add, [shares[i] * parts_ref[i, :, cols].astype(F32) for i in range(count)]
            )
            attended_ref[:, cols] = (acc / total).astype(BF16)

    out_ref[0] = dot_nt(attended_ref[...], weight_ref[...]).astype(BF16)


def project(parts, weight):
    return pl.pallas_call(
        project_kernel,
        grid=(NZ,),
        out_shape=jax.ShapeDtypeStruct((NZ, Q_DEV, SLICE), BF16),
        in_specs=[
            pl.BlockSpec(parts.shape, lambda i: (0, 0, 0)),
            pl.BlockSpec((SLICE, HEADS * HD), lambda i: (i, 0)),
        ],
        out_specs=pl.BlockSpec((1, Q_DEV, SLICE), lambda i: (i, 0, 0)),
        scratch_shapes=[pltpu.VMEM((Q_DEV, HEADS * HD), BF16)],
        compiler_params=params(40),
        cost_estimate=pl.CostEstimate(flops=4 * 10**8, bytes_accessed=8 * 10**6, transcendentals=0),
        name="project",
    )(parts, weight)


def earlier():
    i = lax.broadcasted_iota(jnp.int32, (Q_DEV, Q_DEV), 0)
    j = lax.broadcasted_iota(jnp.int32, (Q_DEV, Q_DEV), 1)
    return i, j


def pack_kernel(heads_ref, residual_ref, gain_ref, routes_ref, stream_ref, packed_ref):
    total = residual_ref[...].astype(F32)
    summed = heads_ref[0].astype(F32)
    for z in range(1, NZ):
        summed = summed + heads_ref[z].astype(F32)
    stream = (total + summed).astype(BF16)
    stream_ref[...] = stream
    stream_f = stream.astype(F32)
    squares = stream_f * stream_f
    scaled = (stream_f * gain_ref[...]).astype(BF16)
    first, second = routes_ref[0:1, :], routes_ref[1:2, :]
    expert = lax.broadcasted_iota(jnp.int32, (E, Q_DEV), 0).astype(F32)
    hot0 = jnp.where(expert == first, 1.0, 0.0)
    hot1 = jnp.where(expert == second, 1.0, 0.0)
    j, i = earlier()
    before_t = jnp.where((j < i) & (j // 16 == i // 16), 1.0, 0.0)
    counts = dot_nn((hot0 + hot1).astype(BF16), before_t.astype(BF16))
    base = (lax.broadcasted_iota(jnp.int32, (1, Q_DEV), 1) // 16 * CAP).astype(F32)
    slot0 = jnp.sum(counts * hot0, axis=0, keepdims=True) + base
    slot1 = jnp.sum(counts * hot1, axis=0, keepdims=True) + base
    sums_row = dot_nt(jnp.ones((8, SLICE), F32), squares, precision=lax.Precision.HIGHEST)
    slot = lax.broadcasted_iota(jnp.int32, (HD, Q_DEV), 0).astype(F32)
    row = lax.broadcasted_iota(jnp.int32, (ROWS, HD), 0)
    for e in range(E):
        placing = jnp.where(
            ((slot == slot0) & (first == e)) | ((slot == slot1) & (second == e)), 1.0, 0.0
        )
        block = dot_nn(placing[:ROWS].astype(BF16), scaled)
        placed = dot_nt(sums_row, placing, precision=lax.Precision.HIGHEST)[0:1, :]
        high, middle, low = three_parts(placed)
        extra = jnp.where(
            row == USED, high, jnp.where(row == USED + 1, middle, jnp.where(row == USED + 2, low, 0.0))
        )
        packed_ref[e, :, :HD] = (block[:, :HD] + extra).astype(BF16)
        packed_ref[e, :, HD:] = block[:, HD:].astype(BF16)


def pack(heads, residual, gain, routes):
    return pl.pallas_call(
        pack_kernel,
        out_shape=(
            jax.ShapeDtypeStruct((Q_DEV, SLICE), BF16),
            jax.ShapeDtypeStruct((E, ROWS, SLICE), BF16),
        ),
        compiler_params=params(40),
        cost_estimate=pl.CostEstimate(flops=3 * 10**7, bytes_accessed=2 * 10**6, transcendentals=0),
        name="pack",
    )(heads, residual, gain, routes)


RCV = PLANE * ROWS
F_BLOCK = 256


def hidden_kernel(steps, x_ref, ga_ref, gb_ref, ua_ref, ub_ref, out_ref, scale_ref):
    step = pl.program_id(0)

    @pl.when(step == 0)
    def _():
        row = lax.broadcasted_iota(jnp.int32, (ROWS, HD), 0)
        lane = lax.broadcasted_iota(jnp.int32, (ROWS, HD), 1)
        for i in range(PLANE):
            part = x_ref[0, i * ROWS : (i + 1) * ROWS, :HD].astype(F32)
            for z in range(1, NZ):
                part = part + x_ref[z, i * ROWS : (i + 1) * ROWS, :HD].astype(F32)
            sums = jnp.sum(jnp.where((row >= USED) & (row < USED + 3), part, 0.0), axis=0, keepdims=True)
            column = jnp.sum(jnp.where((lane == row) & (row < USED), sums, 0.0), axis=1, keepdims=True)
            valid = lax.broadcasted_iota(jnp.int32, (ROWS, 1), 0) < USED
            scale_ref[i * ROWS : (i + 1) * ROWS, :] = jnp.broadcast_to(
                jnp.where(valid, lax.rsqrt(column * (1.0 / D) + NORM_EPS), 0.0), (ROWS, HD)
            )

    def work(gate_ref, up_ref):
        gate = jnp.zeros((RCV, F_BLOCK), F32)
        up = jnp.zeros((RCV, F_BLOCK), F32)
        for z in range(NZ):
            x = x_ref[z]
            gate = gate + dot_nn(x, gate_ref[z * SLICE : (z + 1) * SLICE, :])
            up = up + dot_nn(x, up_ref[z * SLICE : (z + 1) * SLICE, :])
        scale = scale_ref[:, :1]
        gate = gate * scale
        up = up * scale
        out_ref[...] = (gate / (1.0 + jnp.exp(-gate)) * up).astype(BF16)

    pl.when(step < steps)(lambda: work(ga_ref, ua_ref))
    pl.when(step >= steps)(lambda: work(gb_ref, ub_ref))


def hidden_units(x, ga, gb, ua, ub):
    steps = ga.shape[1] // F_BLOCK
    near = pl.BlockSpec((D, F_BLOCK), lambda i: (0, jnp.minimum(i, steps - 1)))
    far = pl.BlockSpec((D, F_BLOCK), lambda i: (0, jnp.maximum(i - steps, 0)))
    return pl.pallas_call(
        functools.partial(hidden_kernel, steps),
        grid=(2 * steps,),
        out_shape=jax.ShapeDtypeStruct((RCV, 2 * ga.shape[1]), BF16),
        in_specs=[pl.BlockSpec(x.shape, lambda i: (0, 0, 0)), near, far, near, far],
        out_specs=pl.BlockSpec((RCV, F_BLOCK), lambda i: (0, i)),
        scratch_shapes=[pltpu.VMEM((RCV, HD), F32)],
        compiler_params=params(56),
        cost_estimate=pl.CostEstimate(flops=11 * 10**9, bytes_accessed=33 * 10**6, transcendentals=10**6),
        name="hidden_units",
    )(x, ga, gb, ua, ub)


def down_kernel(h_ref, da_ref, db_ref, out_ref):
    half = da_ref.shape[0]
    out_ref[0] = (
        dot_nn(h_ref[:, :half], da_ref[...]) + dot_nn(h_ref[:, half:], db_ref[...])
    ).astype(BF16)


def down_units(h, da, db):
    part = pl.BlockSpec((da.shape[0], SLICE), lambda i: (0, i))
    return pl.pallas_call(
        down_kernel,
        grid=(NZ,),
        out_shape=jax.ShapeDtypeStruct((NZ, RCV, SLICE), BF16),
        in_specs=[pl.BlockSpec(h.shape, lambda i: (0, 0)), part, part],
        out_specs=pl.BlockSpec((1, RCV, SLICE), lambda i: (i, 0, 0)),
        compiler_params=params(48),
        cost_estimate=pl.CostEstimate(flops=55 * 10**8, bytes_accessed=20 * 10**6, transcendentals=0),
        name="down_units",
    )(h, da, db)


C_BLOCK = 384


def combine_kernel(returned_ref, stream_ref, routes_ref, out_ref, mix_ref):
    width = NZ * RCV

    @pl.when(pl.program_id(0) == 0)
    def _():
        first, second = routes_ref[:, 0:1], routes_ref[:, 1:2]
        weight0 = routes_ref[:, 2:3] + routes_ref[:, 3:4] + routes_ref[:, 4:5]
        weight1 = routes_ref[:, 5:6] + routes_ref[:, 6:7] + routes_ref[:, 7:8]
        expert = lax.broadcasted_iota(jnp.int32, (Q_DEV, HD), 1).astype(F32)
        hot0 = jnp.where(expert == first, 1.0, 0.0)
        hot1 = jnp.where(expert == second, 1.0, 0.0)
        i, j = earlier()
        before = jnp.where((j < i) & (j // 16 == i // 16), 1.0, 0.0)
        counts = dot_nn(before.astype(BF16), (hot0 + hot1).astype(BF16))
        base = (lax.broadcasted_iota(jnp.int32, (Q_DEV, 1), 0) // 16 * CAP).astype(F32)
        slot0 = jnp.sum(counts * hot0, axis=1, keepdims=True) + base
        slot1 = jnp.sum(counts * hot1, axis=1, keepdims=True) + base
        col = lax.broadcasted_iota(jnp.int32, (Q_DEV, RCV), 1)
        slot = (col % ROWS).astype(F32)
        which = (col // (2 * ROWS)).astype(F32)
        mix = jnp.where((slot == slot0) & (which == first), weight0, 0.0) + jnp.where(
            (slot == slot1) & (which == second), weight1, 0.0
        )
        for part, value in enumerate(three_parts(mix)):
            mix_ref[part * Q_DEV : (part + 1) * Q_DEV, :] = value.astype(BF16)

    total = stream_ref[...].astype(F32)
    for z in range(NZ):
        moved = dot_nn(mix_ref[...], returned_ref[z])
        total = total + moved[:Q_DEV] + moved[Q_DEV : 2 * Q_DEV] + moved[2 * Q_DEV :]
    out_ref[...] = total.astype(BF16)


def combine(returned, stream, routes):
    return pl.pallas_call(
        combine_kernel,
        grid=(SLICE // C_BLOCK,),
        out_shape=jax.ShapeDtypeStruct((Q_DEV, SLICE), BF16),
        in_specs=[
            pl.BlockSpec((NZ, RCV, C_BLOCK), lambda i: (0, 0, i)),
            pl.BlockSpec((Q_DEV, C_BLOCK), lambda i: (0, i)),
            pl.BlockSpec(routes.shape, lambda i: (0, 0)),
        ],
        out_specs=pl.BlockSpec((Q_DEV, C_BLOCK), lambda i: (0, i)),
        scratch_shapes=[pltpu.VMEM((3 * Q_DEV, RCV), BF16)],
        compiler_params=params(40),
        cost_estimate=pl.CostEstimate(flops=7 * 10**8, bytes_accessed=4 * 10**6, transcendentals=0),
        name="combine",
    )(returned, stream, routes)


def body(
    residual,
    queries,
    new_keys,
    new_values,
    cache_keys,
    cache_values,
    out_weight,
    norm_gain,
    route_ids,
    route_weight,
    gate_weight,
    up_weight,
    down_weight,
):
    core = lax.axis_index("c")
    mine = lax.axis_index(XY) * 2 + core
    depth = lax.axis_index("z")

    far_keys = other_core(cache_keys)
    far_values = other_core(cache_values)
    far_new = other_core(jnp.concatenate([new_keys, new_values], axis=1))
    head_width = HEADS * HD
    weight_t = lax.all_gather(out_weight.T, XY + ("c",), axis=0, tiled=True)
    all_queries = exchange(
        jnp.broadcast_to(queries[None], (PLANE, Q_DEV, head_width)), XY
    ).reshape(PLANE * Q_DEV, head_width)
    place = jnp.stack([core, mine]).astype(jnp.int32)
    partial = attend(
        place, all_queries, cache_keys, far_keys, new_keys, far_new[:, :head_width],
        cache_values, far_values, new_values, far_new[:, head_width:],
    )
    far_gate = other_core(gate_weight)
    far_up = other_core(up_weight)
    far_down = other_core(down_weight)

    tok = residual.shape[0]
    codes = jnp.concatenate(
        [
            route_ids.astype(F32),
            jnp.stack(three_parts(route_weight[:, 0]) + three_parts(route_weight[:, 1]), axis=1),
        ],
        axis=1,
    ).astype(BF16)
    codes = jnp.pad(codes, ((0, 0), (0, PACK - codes.shape[1])))
    own = jnp.transpose(residual.reshape(tok, NZ, SLICE), (1, 0, 2))
    own = jnp.concatenate([own, jnp.broadcast_to(codes[None], (NZ, tok, PACK))], axis=2)
    own = exchange(own, ("z",)).reshape(Q_DEV, SLICE + PACK)
    routes = own[:, SLICE:].astype(F32)
    routes_t = routes[:, :8].T

    parts = exchange(partial.reshape(PLANE, Q_DEV, WIDE), XY)
    heads = exchange(project(parts, weight_t), ("z",))
    gain = lax.dynamic_slice_in_dim(norm_gain, depth * SLICE, SLICE, 0)[None]
    stream, packed = pack(heads, own[:, :SLICE], gain, routes_t)
    copies = jnp.broadcast_to(
        packed.reshape(1, E, 1, ROWS, SLICE), (NZ, E, 2, ROWS, SLICE)
    ).reshape(NZ * PLANE, ROWS, SLICE)
    arrived = exchange(copies, ZXY).reshape(NZ, RCV, SLICE)
    hidden = hidden_units(arrived, gate_weight, far_gate, up_weight, far_up)
    answers = down_units(hidden, down_weight, far_down)
    returned = exchange(answers.reshape(NZ * PLANE, ROWS, SLICE), ZXY).reshape(NZ, RCV, SLICE)
    layer = combine(returned, stream, routes)
    final = exchange(layer.reshape(NZ, tok, SLICE), ("z",))
    return jnp.transpose(final, (1, 0, 2)).reshape(tok, D)


def solution(mesh):
    split = Mesh(mesh.devices.reshape(4, 2, 2, 2, NZ), ("y", "xh", "xl", "c", "z"))
    dp = ("y", "xh", "xl", "c")
    rows = dp + ("z",)
    placed = (
        P(rows, None),
        P(dp, "z"),
        P(dp, "z"),
        P(dp, "z"),
        P(dp, "z"),
        P(dp, "z"),
        P("z", dp),
        P(),
        P(rows, None),
        P(rows, None),
        P(None, rows),
        P(None, rows),
        P(rows, None),
    )
    return jax.shard_map(body, mesh=split, in_specs=placed, out_specs=P(rows, None), check_vma=False)
```

time: 665 us -> 275 us (0.41)
  waiting for transfers between devices: 377 us -> 96.5 us
  matrix products: 72.9 us -> 0 us
  Pallas kernels: 0 us -> 61.4 us
  blocking collectives: 117 us -> 60.8 us
  other arithmetic: 27.3 us -> 2.29 us
  local copies, waits for them, and re-layouts: 30 us -> 11.6 us
  starting transfers between devices: 19 us -> 27.9 us
    ppermute x126 -> x6, waiting for transfers between devices: 243 us -> 0.02 us  [other_core(): return lax.ppermute(block, 'c', [(0, 1), (1, 0)])]
    dot_general x70 -> x0, matrix products: 72.9 us -> none  [the longest x32 21 us: fold_keys(): jnp.einsum('qhc,khc->qhk', query_heads, key_heads, preferred_element_type...]
    pallas_call x0 -> x6, Pallas kernels: none -> 61.4 us  [the longest x1 24.1 us: attend(): pl.pallas_call(attend_kernel, grid=(rows // Q_BLOCK,), out_shape=jax.Shap...]
    all_to_all x1 -> x2, blocking collectives: 117 us -> 60.8 us  [exchange(): return lax.all_to_all(block, axes, split_axis=0, concat_axis=0, tiled=True)]
    reduce_sum x37 -> x0, other arithmetic: 21.2 us -> none  [the longest x32 14.1 us: fold_keys(): new_sum = old_sum * rescale + jnp.sum(weights, axis=2)]
    reduce_scatter x1 -> x0, waiting for transfers between devices: 20.7 us -> none  [body(): lax.psum_scatter(head_terms, 'tensor', scatter_dimension=0, tiled=True)]
    all_to_all x1 -> x5, starting transfers between devices: 6.44 us -> 26.4 us  [exchange(): return lax.all_to_all(block, axes, split_axis=0, concat_axis=0, tiled=True)]
    all_to_all x2 -> x0, local copies, waits for them, and re-layouts: 18.3 us -> none  [the longest x1 9.32 us: body(): lax.all_to_all(copies, ('dp', 'tensor'), split_axis=0, concat_axis=0, til...]
  transfers between devices with their start and end apart: 129 -> 12, of which waited for: 65 -> 4; matrix products, arithmetic and copies ran while one was open for 10% -> 3% of each run, Pallas kernels for 0% -> 18%
where the time goes in v1:
time: 275 us; the launch traced here: 274 us
  waiting for transfers between devices  96.5 us (35%)
  Pallas kernels  61.4 us (22%)
  blocking collectives  60.8 us (22%)
  starting transfers between devices  27.9 us (10%)
  between operations  13.5 us (5%)
  local copies, waits for them, and re-layouts  11.6 us (4%)
    all_to_all x5, waiting for transfers between devices, exchange(): return lax.all_to_all(block, axes, split_axis=0, concat_axis=0, tiled=True)  95.8 us
    all_to_all x2, blocking collectives, exchange(): return lax.all_to_all(block, axes, split_axis=0, concat_axis=0, tiled=True)  60.8 us
    all_to_all x5, starting transfers between devices, exchange(): return lax.all_to_all(block, axes, split_axis=0, concat_axis=0, tiled=True)  26.4 us
    pallas_call x1, Pallas kernels, attend(): pl.pallas_call(attend_kernel, grid=(rows // Q_BLOCK,), out_shape=jax.Shap...  24.1 us
    pallas_call x1, Pallas kernels, hidden_units(): pl.pallas_call(functools.partial(hidden_kernel, steps), grid=(2 * steps,)...  19.7 us
    pallas_call x1, Pallas kernels, down_units(): pl.pallas_call(down_kernel, grid=(NZ,), out_shape=jax.ShapeDtypeStruct((N...  9.21 us
  transfers between devices with their start and end apart: 12, of which 4 were waited for; matrix products, arithmetic and copies ran while one was open for 3% of the time, Pallas kernels for 18%

profile of v1, /device:TPU:0, one launch (start us, length us, event | category | flops | bytes accessed | tf_op | source)
XLA Modules:
  0.0 274.1 jit_solution(11012986538359308273)
XLA Ops:
  7.9 0.9 pad_maximum_fusion
  9.0 2.1 broadcast_in_dim.8
  11.1 7.1 %all-to-all-start = ((bf16[16,64,640]{2,1,0:T(8,128)(2,1)}), bf16[16,64,640]{2,1,0:T(8,128)(2,1)S(1)}, u32[]{:S(2)}, u32[]{:S(2)}) async-start(bf16[16,64,640]{2,1,0:T(8,128)(2,1)} %broadcast_in_dim.8), calls=%async_computation | async-start | bytes 2621440 | tf_op jit(solution)/shard_map/all_to_all | solution.py:40
  21.2 22.0 %all-to-all-done = bf16[16,64,640]{2,1,0:T(8,128)(2,1)S(1)} async-done(((bf16[16,64,640]{2,1,0:T(8,128)(2,1)}), bf16[16,64,640]{2,1,0:T(8,128)(2,1)S(1)}, u32[]{:S(2)}, u32[]{:S(2)}) %all-to-all-start) | async-done | bytes 1310752 | tf_op jit(solution)/shard_map/all_to_all | solution.py:40
  43.1 5.2 %all-to-all-start.3 = ((bf16[4,16,1280]{2,1,0:T(8,128)(2,1)}), bf16[4,16,1280]{2,1,0:T(8,128)(2,1)S(1)}, u32[]{:S(2)}, u32[]{:S(2)}) async-start(bf16[4,16,1280]{2,1,0:T(8,128)(2,1)} %pad_maximum_fusion.1), calls=%async_computation.3 | async-start | bytes 327680 | tf_op jit(solution)/shard_map/all_to_all | solution.py:40
  48.4 1.1 copy-done.5
  49.4 24.1 %attend.1 = bf16[1024,768]{1,0:T(8,128)(2,1)} custom-call(s32[2]{0:T(128)} %pad_add_fusion.place_ref, bf16[1024,640]{1,0:T(8,128)(2,1)} %bitcast.28, bf16[1024,640]{1,0:T(8,128)(2,1)} %ka_ref.1, bf16[1024,640]{1,0:T(8,128)(2,1)} %copy-done.5, bf16[64,640]{1,0:T(8,128)(2,1)} %na_ref.1, bf16[64,640]{1,0:T(8,128)(2,1)} %get-tuple-element.10.nb_ref, ...), custom_call_target="tpu_custom_call" | custom-call | flops 11000000512 | bytes 8000000 | tf_op jit(solution)/shard_map/attend/pallas_call | solution.py:109
  73.5 3.7 %all-to-all-start.1 = ((bf16[16,64,768]{2,1,0:T(8,128)(2,1)}), bf16[16,64,768]{2,1,0:T(8,128)(2,1)S(1)}, u32[]{:S(2)}, u32[]{:S(2)}) async-start(bf16[16,64,768]{2,1,0:T(8,128)(2,1)} %bitcast.27), calls=%async_computation.1 | async-start | bytes 3145728 | tf_op jit(solution)/shard_map/all_to_all | solution.py:40
  77.2 0.8 dynamic_slice.3
  78.0 21.3 %all-to-all-done.1.parts_ref = bf16[16,64,768]{2,1,0:T(8,128)(2,1)S(1)} async-done(((bf16[16,64,768]{2,1,0:T(8,128)(2,1)}), bf16[16,64,768]{2,1,0:T(8,128)(2,1)S(1)}, u32[]{:S(2)}, u32[]{:S(2)}) %all-to-all-start.1) | async-done | bytes 1572896 | tf_op jit(solution)/shard_map/all_to_all | solution.py:40
  99.4 2.7 copy-done
  102.0 4.1 %project.1 = bf16[4,64,1152]{2,1,0:T(8,128)(2,1)} custom-call(bf16[16,64,768]{2,1,0:T(8,128)(2,1)S(1)} %all-to-all-done.1.parts_ref, bf16[4608,640]{1,0:T(8,128)(2,1)S(1)} %copy-done), custom_call_target="tpu_custom_call" | custom-call | flops 400000000 | bytes 8000000 | tf_op jit(solution)/shard_map/project/pallas_call | solution.py:149
  106.1 4.5 %all-to-all-start.2 = ((bf16[4,64,1152]{2,1,0:T(8,128)(2,1)}), bf16[4,64,1152]{2,1,0:T(8,128)(2,1)S(1)}, u32[]{:S(2)}, u32[]{:S(2)}) async-start(bf16[4,64,1152]{2,1,0:T(8,128)(2,1)} %project.1), calls=%async_computation.2 | async-start | bytes 1179648 | tf_op jit(solution)/shard_map/all_to_all | solution.py:40
  110.8 8.4 %all-to-all-done.2.heads_ref = bf16[4,64,1152]{2,1,0:T(8,128)(2,1)S(1)} async-done(((bf16[4,64,1152]{2,1,0:T(8,128)(2,1)}), bf16[4,64,1152]{2,1,0:T(8,128)(2,1)S(1)}, u32[]{:S(2)}, u32[]{:S(2)}) %all-to-all-start.2) | async-done | bytes 589856 | tf_op jit(solution)/shard_map/all_to_all | solution.py:40
  119.1 2.0 pack.1
  121.1 2.1 broadcast_in_dim.11
  123.2 5.8 %all-to-all-start.4 = ((bf16[64,24,1152]{2,1,0:T(8,128)(2,1)}), bf16[64,24,1152]{2,1,0:T(8,128)(2,1)}, u32[]{:S(2)}, u32[]{:S(2)}) async-start(bf16[64,24,1152]{2,1,0:T(8,128)(2,1)} %bitcast.26), calls=%async_computation.4 | async-start | bytes 7077888 | tf_op jit(solution)/shard_map/all_to_all | solution.py:40
  129.0 44.2 %all-to-all-done.4 = bf16[64,24,1152]{2,1,0:T(8,128)(2,1)} async-done(((bf16[64,24,1152]{2,1,0:T(8,128)(2,1)}), bf16[64,24,1152]{2,1,0:T(8,128)(2,1)}, u32[]{:S(2)}, u32[]{:S(2)}) %all-to-all-start.4) | async-done | bytes 3538976 | tf_op jit(solution)/shard_map/all_to_all | solution.py:40
  173.2 19.7 %hidden_units.1.h_ref = bf16[384,1536]{1,0:T(8,128)(2,1)} custom-call(bf16[4,384,1152]{2,1,0:T(8,128)(2,1)} %bitcast.9.x_ref, bf16[4608,768]{1,0:T(8,128)(2,1)} %ga_ref.1, bf16[4608,768]{1,0:T(8,128)(2,1)} %collective-permute-done.3.gb_ref, bf16[4608,768]{1,0:T(8,128)(2,1)} %ua_ref.1, bf16[4608,768]{1,0:T(8,128)(2,1)} %collective-permute-done.4.ub_ref), custom_call_target="tpu_custom_call" | custom-call | flops 11000000512 | bytes 33000000 | tf_op jit(solution)/shard_map/hidden_units/pallas_call | solution.py:263
  192.9 1.3 copy-done.1
  194.2 9.2 %down_units.1 = bf16[4,384,1152]{2,1,0:T(8,128)(2,1)S(1)} custom-call(bf16[384,1536]{1,0:T(8,128)(2,1)S(1)} %copy-done.1, bf16[768,4608]{1,0:T(8,128)(2,1)} %da_ref.1, bf16[768,4608]{1,0:T(8,128)(2,1)} %collective-permute-done.5.db_ref), custom_call_target="tpu_custom_call" | custom-call | flops 5500000256 | bytes 20000000 | tf_op jit(solution)/shard_map/down_units/pallas_call | solution.py:285
  203.4 52.4 %all_to_all.35 = bf16[64,24,1152]{2,1,0:T(8,128)(2,1)S(1)} all-to-all(bf16[64,24,1152]{2,1,0:T(8,128)(2,1)S(1)} %bitcast.24), channel_id=1, replica_groups=mesh['y'=4,'xh'=2,'xl'=2,'c'=2,'z'=4] {'z','y','xh','xl'}, dimensions={0} | all-to-all | bytes 7077888 | tf_op jit(solution)/shard_map/all_to_all | solution.py:40
  255.8 2.3 combine.1
  258.2 8.4 %all_to_all.36 = bf16[4,16,1152]{2,1,0:T(8,128)(2,1)S(1)} all-to-all(bf16[4,16,1152]{2,1,0:T(8,128)(2,1)S(1)} %bitcast.25), channel_id=1, replica_groups=mesh['y'=4,'xh'=2,'xl'=2,'c'=2,'z'=4] {'z'}, dimensions={0} | all-to-all | bytes 294912 | tf_op jit(solution)/shard_map/all_to_all | solution.py:40
  (44 shorter events, 5.2 us)
Async XLA Ops:
  6.5 12.3 %copy-start.4 = (f32[16,2]{0,1:T(2,128)S(1)}, f32[16,2]{0,1:T(2,128)}, u32[]{:S(2)}) copy-start(f32[16,2]{0,1:T(2,128)} %param.22) | copy-start | bytes 388
  6.5 12.3 %copy-start.6 = (s32[16,2]{0,1:T(2,128)S(1)}, s32[16,2]{0,1:T(2,128)}, u32[]{:S(2)}) copy-start(s32[16,2]{0,1:T(2,128)} %param.21) | copy-start | bytes 388
  6.5 12.4 %copy-start.3 = (bf16[16,4608]{1,0:T(8,128)(2,1)S(1)}, bf16[16,4608]{1,0:T(8,128)(2,1)}, u32[]{:S(2)}) copy-start(bf16[16,4608]{1,0:T(8,128)(2,1)} %param.13) | copy-start | bytes 442372
  6.5 92.8 %all-gather.2.cloned.1.call-start = ((), (), s32[]{:S(2)}) async-start(), calls=%async_computation.7 | async-start | bytes 6082560 | tf_op jit(solution)/shard_map/all_gather | solution.py:374
  7.3 41.1 %collective-permute-start = (bf16[1024,640]{1,0:T(8,128)(2,1)}, bf16[1024,640]{1,0:T(8,128)(2,1)S(1)}, u32[]{:S(2)}, u32[]{:S(2)}) collective-permute-start(bf16[1024,640]{1,0:T(8,128)(2,1)} %ka_ref.1), channel_id=1, source_target_pairs={{0,4},{4,0},{1,5},{5,1},{2,6},{6,2},{3,7},{7,3},{8,12},{12,8},{9,1... | collective-permute-start | bytes 3932168 | tf_op jit(solution)/shard_map/ppermute | solution.py:44
  7.4 41.0 %collective-permute-start.2 = (bf16[1024,640]{1,0:T(8,128)(2,1)}, bf16[1024,640]{1,0:T(8,128)(2,1)}, u32[]{:S(2)}, u32[]{:S(2)}) collective-permute-start(bf16[1024,640]{1,0:T(8,128)(2,1)} %va_ref.1), channel_id=1, source_target_pairs={{0,4},{4,0},{1,5},{5,1},{2,6},{6,2},{3,7},{7,3},{8,12},{12,8},{9,1... | collective-permute-start | bytes 3932168 | tf_op jit(solution)/shard_map/ppermute | solution.py:44
  8.8 11.5 %collective-permute-start.1 = (bf16[64,1280]{1,0:T(8,128)(2,1)S(1)}, bf16[64,1280]{1,0:T(8,128)(2,1)S(1)}, u32[]{:S(2)}, u32[]{:S(2)}) collective-permute-start(bf16[64,1280]{1,0:T(8,128)(2,1)S(1)} %pad_maximum_fusion), channel_id=1, source_target_pairs={{0,4},{4,0},{1,5},{5,1},{2,6},{6,2},{3,7},{7,3},{8,12},{12,8},{9,1... | collective-permute-start | bytes 491528 | tf_op jit(solution)/shard_map/ppermute | solution.py:44
  11.1 32.1 %all-to-all-start = ((bf16[16,64,640]{2,1,0:T(8,128)(2,1)}), bf16[16,64,640]{2,1,0:T(8,128)(2,1)S(1)}, u32[]{:S(2)}, u32[]{:S(2)}) async-start(bf16[16,64,640]{2,1,0:T(8,128)(2,1)} %broadcast_in_dim.8), calls=%async_computation | async-start | bytes 2621440 | tf_op jit(solution)/shard_map/all_to_all | solution.py:40
  18.2 110.8 %collective-permute-start.3 = (bf16[4608,768]{1,0:T(8,128)(2,1)}, bf16[4608,768]{1,0:T(8,128)(2,1)}, u32[]{:S(2)}, u32[]{:S(2)}) collective-permute-start(bf16[4608,768]{1,0:T(8,128)(2,1)} %ga_ref.1), channel_id=1, source_target_pairs={{0,4},{4,0},{1,5},{5,1},{2,6},{6,2},{3,7},{7,3},{8,12},{12,8},{9,1... | collective-permute-start | bytes 21233672 | tf_op jit(solution)/shard_map/ppermute | solution.py:44
  18.4 110.6 %collective-permute-start.4 = (bf16[4608,768]{1,0:T(8,128)(2,1)}, bf16[4608,768]{1,0:T(8,128)(2,1)}, u32[]{:S(2)}, u32[]{:S(2)}) collective-permute-start(bf16[4608,768]{1,0:T(8,128)(2,1)} %ua_ref.1), channel_id=1, source_target_pairs={{0,4},{4,0},{1,5},{5,1},{2,6},{6,2},{3,7},{7,3},{8,12},{12,8},{9,1... | collective-permute-start | bytes 21233672 | tf_op jit(solution)/shard_map/ppermute | solution.py:44
  20.3 172.6 %collective-permute-start.5 = (bf16[768,4608]{1,0:T(8,128)(2,1)}, bf16[768,4608]{1,0:T(8,128)(2,1)}, u32[]{:S(2)}, u32[]{:S(2)}) collective-permute-start(bf16[768,4608]{1,0:T(8,128)(2,1)} %da_ref.1), channel_id=1, source_target_pairs={{0,4},{4,0},{1,5},{5,1},{2,6},{6,2},{3,7},{7,3},{8,12},{12,8},{9,1... | collective-permute-start | bytes 21233672 | tf_op jit(solution)/shard_map/ppermute | solution.py:44
  43.1 5.2 %copy-start.2 = (bf16[16,64,640]{2,1,0:T(8,128)(2,1)}, bf16[16,64,640]{2,1,0:T(8,128)(2,1)S(1)}, u32[]{:S(2)}) copy-start(bf16[16,64,640]{2,1,0:T(8,128)(2,1)S(1)} %all-to-all-done) | copy-start | bytes 3932164
  43.1 30.4 %all-to-all-start.3 = ((bf16[4,16,1280]{2,1,0:T(8,128)(2,1)}), bf16[4,16,1280]{2,1,0:T(8,128)(2,1)S(1)}, u32[]{:S(2)}, u32[]{:S(2)}) async-start(bf16[4,16,1280]{2,1,0:T(8,128)(2,1)} %pad_maximum_fusion.1), calls=%async_computation.3 | async-start | bytes 327680 | tf_op jit(solution)/shard_map/all_to_all | solution.py:40
  48.4 1.1 copy-start.5
  73.5 25.8 %all-to-all-start.1 = ((bf16[16,64,768]{2,1,0:T(8,128)(2,1)}), bf16[16,64,768]{2,1,0:T(8,128)(2,1)S(1)}, u32[]{:S(2)}, u32[]{:S(2)}) async-start(bf16[16,64,768]{2,1,0:T(8,128)(2,1)} %bitcast.27), calls=%async_computation.1 | async-start | bytes 3145728 | tf_op jit(solution)/shard_map/all_to_all | solution.py:40
  99.4 2.7 copy-start
  106.1 13.0 %all-to-all-start.2 = ((bf16[4,64,1152]{2,1,0:T(8,128)(2,1)}), bf16[4,64,1152]{2,1,0:T(8,128)(2,1)S(1)}, u32[]{:S(2)}, u32[]{:S(2)}) async-start(bf16[4,64,1152]{2,1,0:T(8,128)(2,1)} %project.1), calls=%async_computation.2 | async-start | bytes 1179648 | tf_op jit(solution)/shard_map/all_to_all | solution.py:40
  123.2 50.0 %all-to-all-start.4 = ((bf16[64,24,1152]{2,1,0:T(8,128)(2,1)}), bf16[64,24,1152]{2,1,0:T(8,128)(2,1)}, u32[]{:S(2)}, u32[]{:S(2)}) async-start(bf16[64,24,1152]{2,1,0:T(8,128)(2,1)} %bitcast.26), calls=%async_computation.4 | async-start | bytes 7077888 | tf_op jit(solution)/shard_map/all_to_all | solution.py:40
  192.9 1.3 copy-start.1
Sparse Core Ops, SparseCore 0:
  9.7 59.7 all-gather.1

commit v2 on v1

v2 whole, which is shorter than its diff:
```python
import functools
import math

import jax
import jax.numpy as jnp
from jax import lax
from jax.experimental import pallas as pl
from jax.experimental.pallas import tpu as pltpu
from jax.sharding import Mesh, PartitionSpec as P

D = 4608
HD = 128
HEADS = 5
E = 8
TOP = 2
CAP = 5
NZ = 4
PLANE = 16
Q_DEV = 64
SLICE = D // NZ
MAIN = 16
OVER = NZ * CAP - MAIN
THIRD = SLICE // 3
CHUNK = SLICE + THIRD
PACK = 128
WIDE = HEADS * HD + PACK
NORM_EPS = 1e-06
NEGATIVE = -1e30
TO_BASE2 = math.log2(math.e) / math.sqrt(HD)

XY = ("y", "xh", "xl")
ZXY = ("z", "y", "xh", "xl")
F32 = jnp.float32
BF16 = jnp.bfloat16


VMEM = pl.BlockSpec(memory_space=pltpu.VMEM)
HBM = pl.BlockSpec(memory_space=pltpu.HBM)


def params(mib):
    return pltpu.CompilerParams(vmem_limit_bytes=mib * 2**20)


def exchange(block, axes):
    return lax.all_to_all(block, axes, split_axis=0, concat_axis=0, tiled=True)


def other_core(block):
    return lax.ppermute(block, "c", [(0, 1), (1, 0)])


def around_z(blocks, depth):
    take = lambda a, i: lax.dynamic_index_in_dim(a, i % NZ, 0, keepdims=False)
    got = [take(blocks, depth)]
    for step in range(1, NZ):
        route = [(i, (i + step) % NZ) for i in range(NZ)]
        got.append(lax.ppermute(take(blocks, depth + step), "z", route))
    got = jnp.stack(got)
    return jnp.stack([take(got, depth - i + NZ) for i in range(NZ)])


def three_parts(value):
    high = value.astype(BF16).astype(F32)
    rest = value - high
    middle = rest.astype(BF16).astype(F32)
    return high, middle, (rest - middle).astype(BF16).astype(F32)


def dot_nt(a, b, **kw):
    return lax.dot_general(a, b, (((1,), (1,)), ((), ())), preferred_element_type=F32, **kw)


def dot_nn(a, b, **kw):
    return lax.dot_general(a, b, (((1,), (0,)), ((), ())), preferred_element_type=F32, **kw)


Q_BLOCKS = 8


def attend_kernel(place_ref, q_ref, ka_ref, kb_ref, na_ref, nb_ref, va_ref, vb_ref, wa_ref, wb_ref, out_ref):
    core, mine = place_ref[0], place_ref[1]
    rows = out_ref.shape[0]
    row = lax.broadcasted_iota(jnp.int32, (rows, HD), 0)
    lane = lax.broadcasted_iota(jnp.int32, (rows, HD), 1)
    block = pl.program_id(0) * Q_BLOCKS + row // Q_DEV
    q_pos = (block * 2 + core) * Q_DEV + row % Q_DEV
    k_pos = jnp.where(lane < Q_DEV, mine * Q_DEV + lane, (mine + 1 - 2 * core) * Q_DEV + lane - Q_DEV)
    allowed = k_pos <= q_pos
    pack = jnp.zeros((rows, PACK), F32)
    for h in range(HEADS):
        cols = slice(h * HD, (h + 1) * HD)
        q = q_ref[:, :, cols].reshape(rows, HD)
        s1 = dot_nt(q, ka_ref[:, cols])
        s2 = dot_nt(q, kb_ref[:, cols])
        fresh = jnp.concatenate([na_ref[:, cols], nb_ref[:, cols]], axis=0)
        s3 = jnp.where(allowed, dot_nt(q, fresh), NEGATIVE)
        top = jnp.maximum(
            jnp.maximum(jnp.max(s1, axis=1, keepdims=True), jnp.max(s2, axis=1, keepdims=True)),
            jnp.max(s3, axis=1, keepdims=True),
        ) * TO_BASE2
        w1 = jnp.exp2(s1 * TO_BASE2 - top)
        w2 = jnp.exp2(s2 * TO_BASE2 - top)
        w3 = jnp.exp2(s3 * TO_BASE2 - top)
        total = (
            jnp.sum(w1, axis=1, keepdims=True)
            + jnp.sum(w2, axis=1, keepdims=True)
            + jnp.sum(w3, axis=1, keepdims=True)
        )
        fresh_v = jnp.concatenate([wa_ref[:, cols], wb_ref[:, cols]], axis=0)
        acc = (
            dot_nn(w1.astype(BF16), va_ref[:, cols])
            + dot_nn(w2.astype(BF16), vb_ref[:, cols])
            + dot_nn(w3.astype(BF16), fresh_v)
        )
        out_ref[:, cols] = (acc / total).astype(BF16)
        for part, value in enumerate(three_parts(top + jnp.log2(total))):
            pack = jnp.where(lane == part * 8 + h, value, pack)
    out_ref[:, HEADS * HD :] = pack.astype(BF16)


def attend(place, q, *keys):
    rows = Q_BLOCKS * Q_DEV
    whole = [pl.BlockSpec(a.shape, lambda i: (0, 0)) for a in keys]
    return pl.pallas_call(
        attend_kernel,
        grid=(PLANE // Q_BLOCKS,),
        out_shape=jax.ShapeDtypeStruct((PLANE * Q_DEV, WIDE), BF16),
        in_specs=[
            pl.BlockSpec(memory_space=pltpu.SMEM),
            pl.BlockSpec((Q_BLOCKS, Q_DEV, HEADS * HD), lambda i: (i, 0, 0)),
            *whole,
        ],
        out_specs=pl.BlockSpec((rows, WIDE), lambda i: (i, 0)),
        compiler_params=params(56),
        cost_estimate=pl.CostEstimate(flops=11 * 10**9, bytes_accessed=10**7, transcendentals=11 * 10**6),
        name="attend",
    )(place, q, *keys)


def merge(parts_ref, out_ref):
    count = parts_ref.shape[0]
    sums = [parts_ref[i, :, HEADS * HD :].astype(F32) for i in range(count)]
    for h in range(HEADS):
        cols = slice(h * HD, (h + 1) * HD)
        logs = [s[:, h : h + 1] + s[:, 8 + h : 9 + h] + s[:, 16 + h : 17 + h] for s in sums]
        top = functools.reduce(jnp.maximum, logs)
        shares = [jnp.exp2(v - top) for v in logs]
        total = functools.reduce(jnp.add, shares)
        acc = functools.reduce(
            jnp.add, [shares[i] * parts_ref[i, :, cols].astype(F32) for i in range(count)]
        )
        out_ref[:, cols] = (acc / total).astype(BF16)


def project_kernel(parts_ref, weight_ref, out_ref, attended_ref):
    @pl.when(pl.program_id(0) == 0)
    def _():
        merge(parts_ref, attended_ref)

    out_ref[0] = dot_nt(attended_ref[...], weight_ref[...]).astype(BF16)


def project(parts, weight):
    width = HEADS * HD
    return pl.pallas_call(
        project_kernel,
        grid=(NZ,),
        out_shape=jax.ShapeDtypeStruct((NZ, Q_DEV, SLICE), BF16),
        in_specs=[
            pl.BlockSpec(parts.shape, lambda i: (0, 0, 0)),
            pl.BlockSpec((SLICE, width), lambda i: (i, 0)),
        ],
        out_specs=pl.BlockSpec((1, Q_DEV, SLICE), lambda i: (i, 0, 0)),
        scratch_shapes=[pltpu.VMEM((Q_DEV, width), BF16)],
        compiler_params=params(58),
        cost_estimate=pl.CostEstimate(flops=4 * 10**8, bytes_accessed=8 * 10**6, transcendentals=0),
        name="project",
    )(parts, weight)


def earlier():
    i = lax.broadcasted_iota(jnp.int32, (Q_DEV, Q_DEV), 0)
    j = lax.broadcasted_iota(jnp.int32, (Q_DEV, Q_DEV), 1)
    return i, j


def pack_kernel(heads_ref, own_ref, gain_ref, stream_ref, routes_ref, chunk_ref, made_ref, sems):
    total = own_ref[:, :SLICE].astype(F32)
    summed = heads_ref[0].astype(F32)
    for z in range(1, NZ):
        summed = summed + heads_ref[z].astype(F32)
    stream = (total + summed).astype(BF16)
    stream_ref[...] = stream
    stream_f = stream.astype(F32)
    squares = stream_f * stream_f
    scaled = (stream_f * gain_ref[...]).astype(BF16)
    routes = own_ref[:, SLICE:]
    routes_ref[...] = routes.astype(F32)
    kind, lane = iotas(8, PACK)
    turned = dot_nt(jnp.where(kind == lane, 1.0, 0.0).astype(BF16), routes)
    first, second = turned[0:1, :], turned[1:2, :]
    expert = lax.broadcasted_iota(jnp.int32, (E, Q_DEV), 0).astype(F32)
    hot0 = jnp.where(expert == first, 1.0, 0.0)
    hot1 = jnp.where(expert == second, 1.0, 0.0)
    j, i = earlier()
    before_t = jnp.where((j < i) & (j // 16 == i // 16), 1.0, 0.0)
    counts = dot_nn((hot0 + hot1).astype(BF16), before_t.astype(BF16))
    base = (lax.broadcasted_iota(jnp.int32, (1, Q_DEV), 1) // 16 * CAP).astype(F32)
    slot0 = jnp.sum(counts * hot0, axis=0, keepdims=True) + base
    slot1 = jnp.sum(counts * hot1, axis=0, keepdims=True) + base

    def placing(slot, which):
        return jnp.where(
            ((slot == slot0) & (which == first)) | ((slot == slot1) & (which == second)), 1.0, 0.0
        )

    line = lax.broadcasted_iota(jnp.int32, (E * MAIN, Q_DEV), 0)
    which = (line // MAIN).astype(F32)
    part = line % MAIN
    main = dot_nn(placing(part.astype(F32), which).astype(BF16), scaled).astype(BF16)
    over = jnp.zeros((E * MAIN, THIRD), F32)
    for t in range(3):
        wanted = jnp.where(part // OVER == t, MAIN + part % OVER, -1).astype(F32)
        over = over + dot_nn(placing(wanted, which).astype(BF16), scaled[:, t * THIRD : (t + 1) * THIRD])
    sums_row = dot_nt(jnp.ones((8, SLICE), F32), squares, precision=lax.Precision.HIGHEST)
    slot = lax.broadcasted_iota(jnp.int32, (HD, Q_DEV), 0).astype(F32)
    row = lax.broadcasted_iota(jnp.int32, (MAIN, HD), 0)
    for e in range(E):
        placed = dot_nt(sums_row, placing(slot, float(e)), precision=lax.Precision.HIGHEST)[0:1, :]
        high, middle, low = three_parts(placed)
        extra = jnp.where(
            row == 3 * OVER,
            high,
            jnp.where(row == 3 * OVER + 1, middle, jnp.where(row == 3 * OVER + 2, low, 0.0)),
        )
        here = slice(e * MAIN, (e + 1) * MAIN)
        begin = (over[here, :HD] + extra).astype(BF16)
        rest = over[here, HD:].astype(BF16)
        made_ref[e, :, :SLICE] = main[here]
        made_ref[e, :, SLICE : SLICE + HD] = begin
        made_ref[e, :, SLICE + HD :] = rest
    copies = [
        pltpu.make_async_copy(made_ref, chunk_ref.at[z, :, x], sems.at[z, x])
        for z in range(NZ)
        for x in range(2)
    ]
    for copy in copies:
        copy.start()
    for copy in copies:
        copy.wait()


def pack(heads, own, gain):
    return pl.pallas_call(
        pack_kernel,
        out_shape=(
            jax.ShapeDtypeStruct((Q_DEV, SLICE), BF16),
            jax.ShapeDtypeStruct((Q_DEV, PACK), F32),
            jax.ShapeDtypeStruct((NZ, E, 2, MAIN, CHUNK), BF16),
        ),
        in_specs=[VMEM] * 3,
        out_specs=(VMEM, VMEM, HBM),
        scratch_shapes=[pltpu.VMEM((E, MAIN, CHUNK), BF16), pltpu.SemaphoreType.DMA((NZ, 2))],
        compiler_params=params(40),
        cost_estimate=pl.CostEstimate(flops=3 * 10**7, bytes_accessed=5 * 10**6, transcendentals=0),
        name="pack",
    )(heads, own, gain)


RCV = PLANE * MAIN
F_BLOCK = 256
EXT = PLANE * OVER
ALL = RCV + EXT
def iotas(rows, cols):
    return (
        lax.broadcasted_iota(jnp.int32, (rows, cols), 0),
        lax.broadcasted_iota(jnp.int32, (rows, cols), 1),
    )


def unpack(x_ref, rows_ref):
    over_row, line = iotas(EXT, RCV)
    extra_sum = jnp.zeros((RCV, HD), F32)
    for z in range(NZ):
        rows_ref[:RCV, z * SLICE : (z + 1) * SLICE] = x_ref[z, :, :SLICE]
        over = x_ref[z, :, SLICE:]
        extra_sum = extra_sum + over[:, :HD].astype(F32)
        for t in range(3):
            pick = (line // MAIN == over_row // OVER) & (line % MAIN == t * OVER + over_row % OVER)
            rows_ref[RCV:, z * SLICE + t * THIRD : z * SLICE + (t + 1) * THIRD] = dot_nn(
                jnp.where(pick, 1.0, 0.0).astype(BF16), over
            ).astype(BF16)

    source, line = iotas(PLANE, RCV)
    part = line % MAIN
    pick = (line // MAIN == source) & (part >= 3 * OVER) & (part < 3 * OVER + 3)
    sums = dot_nn(jnp.where(pick, 1.0, 0.0), extra_sum, precision=lax.Precision.HIGHEST)
    row, source = iotas(ALL, PLANE)
    owner = jnp.where(row < RCV, row // MAIN, (row - RCV) // OVER)
    spread = dot_nn(jnp.where(owner == source, 1.0, 0.0), sums, precision=lax.Precision.HIGHEST)
    row, lane = iotas(ALL, HD)
    slot = jnp.where(row < RCV, row % MAIN, MAIN + (row - RCV) % OVER)
    column = jnp.sum(jnp.where(lane == slot, spread, 0.0), axis=1, keepdims=True)
    return lax.rsqrt(column * (1.0 / D) + NORM_EPS)


def repack(answer, made_ref, z):
    width = answer.shape[1]
    made_ref[z, :, :width] = answer[:RCV]
    line, over_row = iotas(RCV, EXT)
    for third in range(width // THIRD):
        over = jnp.zeros((RCV, HD), F32)
        for t in range(3):
            pick = (line // MAIN == over_row // OVER) & (line % MAIN == t * OVER + over_row % OVER)
            at = third * THIRD + t * HD
            over = over + dot_nn(jnp.where(pick, 1.0, 0.0).astype(BF16), answer[RCV:, at : at + HD])
        made_ref[z, :, width + third * HD : width + (third + 1) * HD] = over.astype(BF16)


AHEAD = 2
SLOTS = AHEAD + 1


def experts_kernel(
    x_ref, ga_hbm, gb_hbm, ua_hbm, ub_hbm, da_hbm, db_hbm, out_hbm,
    made_ref, rows_ref, scale_ref, hidden_ref, gate_ref, up_ref, down_ref, weight_sem, down_sem, out_sem,
):
    steps = ga_hbm.shape[1] // F_BLOCK

    def weight_copies(step, gate_hbm, up_hbm, block):
        cols = pl.ds(pl.multiple_of(block * F_BLOCK, F_BLOCK), F_BLOCK)
        slot = lax.rem(step, SLOTS)
        return (
            pltpu.make_async_copy(gate_hbm.at[:, cols], gate_ref.at[slot], weight_sem.at[0, slot]),
            pltpu.make_async_copy(up_hbm.at[:, cols], up_ref.at[slot], weight_sem.at[1, slot]),
        )

    def down_copies():
        return [
            [
                pltpu.make_async_copy(
                    hbm.at[:, z * SLICE : (z + 1) * SLICE], down_ref.at[side, z], down_sem.at[side, z]
                )
                for side, hbm in enumerate((da_hbm, db_hbm))
            ]
            for z in range(NZ)
        ]

    for step in range(AHEAD):
        for copy in weight_copies(step, ga_hbm, ua_hbm, step):
            copy.start()
    scale_ref[...] = jnp.broadcast_to(unpack(x_ref, rows_ref), (ALL, HD))

    @pl.loop(0, 2 * steps)
    def _(step):
        later = step + AHEAD

        @pl.when(later < steps)
        def _():
            for copy in weight_copies(later, ga_hbm, ua_hbm, later):
                copy.start()

        @pl.when((later >= steps) & (later < 2 * steps))
        def _():
            for copy in weight_copies(later, gb_hbm, ub_hbm, later - steps):
                copy.start()

        @pl.when(later == 2 * steps)
        def _():
            for pair in down_copies():
                for copy in pair:
                    copy.start()

        for copy in weight_copies(step, ga_hbm, ua_hbm, 0):
            copy.wait()
        slot = lax.rem(step, SLOTS)
        gate = dot_nn(rows_ref[...], gate_ref[slot]) * scale_ref[:, :1]
        up = dot_nn(rows_ref[...], up_ref[slot]) * scale_ref[:, :1]
        to = pl.ds(pl.multiple_of(step * F_BLOCK, F_BLOCK), F_BLOCK)
        hidden_ref[:, to] = (gate / (1.0 + jnp.exp(-gate)) * up).astype(BF16)

    half = da_hbm.shape[0]
    sent = []
    for z, pair in enumerate(down_copies()):
        for copy in pair:
            copy.wait()
        answer = dot_nn(hidden_ref[:, :half], down_ref[0, z]) + dot_nn(hidden_ref[:, half:], down_ref[1, z])
        repack(answer.astype(BF16), made_ref, z)
        sent.append(pltpu.make_async_copy(made_ref.at[z], out_hbm.at[z], out_sem.at[z]))
        sent[-1].start()
    for copy in sent:
        copy.wait()


def experts(x, ga, gb, ua, ub, da, db):
    width = ga.shape[1]
    return pl.pallas_call(
        experts_kernel,
        out_shape=jax.ShapeDtypeStruct(x.shape, BF16),
        in_specs=[VMEM] + [HBM] * 6,
        out_specs=HBM,
        scratch_shapes=[
            pltpu.VMEM(x.shape, BF16),
            pltpu.VMEM((ALL, D), BF16),
            pltpu.VMEM((ALL, HD), F32),
            pltpu.VMEM((ALL, 2 * width), BF16),
            pltpu.VMEM((SLOTS, D, F_BLOCK), BF16),
            pltpu.VMEM((SLOTS, D, F_BLOCK), BF16),
            pltpu.VMEM((2, NZ, width, SLICE), BF16),
            pltpu.SemaphoreType.DMA((2, SLOTS)),
            pltpu.SemaphoreType.DMA((2, NZ)),
            pltpu.SemaphoreType.DMA((NZ,)),
        ],
        compiler_params=params(56),
        cost_estimate=pl.CostEstimate(flops=14 * 10**9, bytes_accessed=48 * 10**6, transcendentals=10**6),
        name="experts",
    )(x, ga, gb, ua, ub, da, db)


def mixing_kernel(routes_ref, mix_ref):
    first, second = routes_ref[:, 0:1], routes_ref[:, 1:2]
    weight0 = routes_ref[:, 2:3] + routes_ref[:, 3:4] + routes_ref[:, 4:5]
    weight1 = routes_ref[:, 5:6] + routes_ref[:, 6:7] + routes_ref[:, 7:8]
    expert = lax.broadcasted_iota(jnp.int32, (Q_DEV, HD), 1).astype(F32)
    hot0 = jnp.where(expert == first, 1.0, 0.0)
    hot1 = jnp.where(expert == second, 1.0, 0.0)
    i, j = earlier()
    before = jnp.where((j < i) & (j // 16 == i // 16), 1.0, 0.0)
    counts = dot_nn(before.astype(BF16), (hot0 + hot1).astype(BF16))
    base = (lax.broadcasted_iota(jnp.int32, (Q_DEV, 1), 0) // 16 * CAP).astype(F32)
    slot0 = jnp.sum(counts * hot0, axis=1, keepdims=True) + base
    slot1 = jnp.sum(counts * hot1, axis=1, keepdims=True) + base
    col = lax.broadcasted_iota(jnp.int32, (Q_DEV, RCV), 1)
    part = col % MAIN
    which = (col // (2 * MAIN)).astype(F32)
    for kind in range(4):
        slot = part if kind == 0 else jnp.where(part // OVER == kind - 1, MAIN + part % OVER, -1)
        slot = slot.astype(F32)
        mix = jnp.where((slot == slot0) & (which == first), weight0, 0.0) + jnp.where(
            (slot == slot1) & (which == second), weight1, 0.0
        )
        for at, value in enumerate(three_parts(mix)):
            mix_ref[kind, at * Q_DEV : (at + 1) * Q_DEV, :] = value.astype(BF16)


def mixing(routes):
    return pl.pallas_call(
        mixing_kernel,
        out_shape=jax.ShapeDtypeStruct((4, 3 * Q_DEV, RCV), BF16),
        compiler_params=params(30),
        cost_estimate=pl.CostEstimate(flops=10**6, bytes_accessed=4 * 10**5, transcendentals=0),
        name="mixing",
    )(routes)


def combine_kernel(returned_hbm, stream_ref, mix_ref, out_ref, returned_ref, sems):
    copies = [
        pltpu.make_async_copy(returned_hbm.at[z], returned_ref.at[z], sems.at[z]) for z in range(NZ)
    ]
    for copy in copies:
        copy.start()

    def fold(kind, block):
        moved = dot_nn(mix_ref[kind], block)
        return moved[:Q_DEV] + moved[Q_DEV : 2 * Q_DEV] + moved[2 * Q_DEV :]

    total = stream_ref[...].astype(F32)
    extra = [jnp.zeros((Q_DEV, HD), F32)] * (SLICE // HD)
    for z in range(NZ):
        copies[z].wait()
        total = total + fold(0, returned_ref[z, :, :SLICE])
        for at in range(SLICE // HD):
            lanes = slice(SLICE + at // 3 * HD, SLICE + (at // 3 + 1) * HD)
            extra[at] = extra[at] + fold(at % 3 + 1, returned_ref[z, :, lanes])
    for at, part in enumerate(extra):
        cols = slice(at * HD, (at + 1) * HD)
        out_ref[:, cols] = (total[:, cols] + part).astype(BF16)


def combine(returned, stream, mix):
    return pl.pallas_call(
        combine_kernel,
        out_shape=jax.ShapeDtypeStruct((Q_DEV, SLICE), BF16),
        in_specs=[HBM, VMEM, VMEM],
        out_specs=VMEM,
        scratch_shapes=[pltpu.VMEM(returned.shape, BF16), pltpu.SemaphoreType.DMA((NZ,))],
        compiler_params=params(40),
        cost_estimate=pl.CostEstimate(flops=7 * 10**8, bytes_accessed=5 * 10**6, transcendentals=0),
        name="combine",
    )(returned, stream, mix)


def body(
    residual,
    queries,
    new_keys,
    new_values,
    cache_keys,
    cache_values,
    out_weight,
    norm_gain,
    route_ids,
    route_weight,
    gate_weight,
    up_weight,
    down_weight,
):
    core = lax.axis_index("c")
    mine = lax.axis_index(XY) * 2 + core
    depth = lax.axis_index("z")

    head_width = HEADS * HD
    far_keys = other_core(cache_keys)
    far_values = other_core(cache_values)
    far_new_keys = other_core(new_keys)
    far_new_values = other_core(new_values)
    weight_t = lax.all_gather(out_weight.T, XY + ("c",), axis=0, tiled=True)
    all_queries = exchange(jnp.broadcast_to(queries[None], (PLANE, Q_DEV, head_width)), XY)
    tok = residual.shape[0]
    codes = jnp.concatenate(
        [
            route_ids.astype(F32),
            jnp.stack(three_parts(route_weight[:, 0]) + three_parts(route_weight[:, 1]), axis=1),
        ],
        axis=1,
    ).astype(BF16)
    codes = jnp.pad(codes, ((0, 0), (0, PACK - codes.shape[1])))
    own = jnp.transpose(residual.reshape(tok, NZ, SLICE), (1, 0, 2))
    own = jnp.concatenate([own, jnp.broadcast_to(codes[None], (NZ, tok, PACK))], axis=2)
    own = around_z(own, depth).reshape(Q_DEV, SLICE + PACK)
    own, all_queries = lax.optimization_barrier((own, all_queries))

    place = jnp.stack([core, mine]).astype(jnp.int32)
    partial = attend(
        place, all_queries, cache_keys, far_keys, new_keys, far_new_keys,
        cache_values, far_values, new_values, far_new_values,
    )
    after = lax.optimization_barrier((gate_weight, up_weight, down_weight, all_queries))
    far_gate, far_up, far_down = (other_core(w) for w in after[:3])
    parts = exchange(partial.reshape(PLANE, Q_DEV, WIDE), XY)
    heads = exchange(project(parts, weight_t), ("z",))
    gain = lax.dynamic_slice_in_dim(norm_gain, depth * SLICE, SLICE, 0)[None]
    stream, routes, chunks = pack(heads, own, gain)
    mix = mixing(routes)
    arrived = exchange(chunks.reshape(NZ * PLANE, MAIN, CHUNK), ZXY).reshape(NZ, RCV, CHUNK)
    answers = experts(arrived, gate_weight, far_gate, up_weight, far_up, down_weight, far_down)
    returned = exchange(answers.reshape(NZ * PLANE, MAIN, CHUNK), ZXY).reshape(NZ, RCV, CHUNK)
    layer = combine(returned, stream, mix)
    final = exchange(layer.reshape(NZ, tok, SLICE), ("z",))
    return jnp.transpose(final, (1, 0, 2)).reshape(tok, D)


def solution(mesh):
    split = Mesh(mesh.devices.reshape(4, 2, 2, 2, NZ), ("y", "xh", "xl", "c", "z"))
    dp = ("y", "xh", "xl", "c")
    rows = dp + ("z",)
    placed = (
        P(rows, None),
        P(dp, "z"),
        P(dp, "z"),
        P(dp, "z"),
        P(dp, "z"),
        P(dp, "z"),
        P("z", dp),
        P(),
        P(rows, None),
        P(rows, None),
        P(None, rows),
        P(None, rows),
        P(rows, None),
    )
    return jax.shard_map(body, mesh=split, in_specs=placed, out_specs=P(rows, None), check_vma=False)
```

time: 275 us -> 256 us (0.931)
  blocking collectives: 60.8 us -> 36.4 us
  waiting for transfers between devices: 96.5 us -> 105 us
  starting transfers between devices: 27.9 us -> 32.5 us
  local copies, waits for them, and re-layouts: 11.6 us -> 8.44 us
  Pallas kernels: 61.4 us -> 58.6 us
    all_to_all x2, blocking collectives: 60.8 us -> 36.4 us  [exchange(): return lax.all_to_all(block, axes, split_axis=0, concat_axis=0, tiled=True)]
    pallas_call x4, Pallas kernels: 55.3 us -> 47.7 us  [the longest x1 23.2 us: experts(): pl.pallas_call(experts_kernel, out_shape=jax.ShapeDtypeStruct(x.shape, BF...]
    ppermute x0 -> x3, starting transfers between devices: none -> 6.58 us  [around_z(): got.append(lax.ppermute(take(blocks, depth + step), 'z', route))]
    all_to_all x5 -> x4, waiting for transfers between devices: 95.8 us -> 102 us  [exchange(): return lax.all_to_all(block, axes, split_axis=0, concat_axis=0, tiled=True)]
    all_to_all x5 -> x4, starting transfers between devices: 26.4 us -> 24.5 us  [exchange(): return lax.all_to_all(block, axes, split_axis=0, concat_axis=0, tiled=True)]
  transfers between devices with their start and end apart: 12 -> 15, of which waited for: 4 -> 6; matrix products, arithmetic and copies ran while one was open for 3% -> 1% of each run, Pallas kernels for 18% -> 13%
where the time goes in v2:
time: 256 us; the launch traced here: 255 us
  waiting for transfers between devices  105 us (41%)
  Pallas kernels  58.6 us (23%)
  blocking collectives  36.4 us (14%)
  starting transfers between devices  32.5 us (13%)
  between operations  13.7 us (5%)
  local copies, waits for them, and re-layouts  8.44 us (3%)
    all_to_all x4, waiting for transfers between devices, exchange(): return lax.all_to_all(block, axes, split_axis=0, concat_axis=0, tiled=True)  102 us
    all_to_all x2, blocking collectives, exchange(): return lax.all_to_all(block, axes, split_axis=0, concat_axis=0, tiled=True)  36.4 us
    all_to_all x4, starting transfers between devices, exchange(): return lax.all_to_all(block, axes, split_axis=0, concat_axis=0, tiled=True)  24.5 us
    pallas_call x1, Pallas kernels, experts(): pl.pallas_call(experts_kernel, out_shape=jax.ShapeDtypeStruct(x.shape, BF...  23.2 us
    pallas_call x1, Pallas kernels, attend(): pl.pallas_call(attend_kernel, grid=(PLANE // Q_BLOCKS,), out_shape=jax.Sh...  21.8 us
    pallas_call x1, Pallas kernels, project(): pl.pallas_call(project_kernel, grid=(NZ,), out_shape=jax.ShapeDtypeStruct...  6.84 us
    ppermute x3, starting transfers between devices, around_z(): got.append(lax.ppermute(take(blocks, depth + step), 'z', route))  6.58 us
  transfers between devices with their start and end apart: 15, of which 6 were waited for; matrix products, arithmetic and copies ran while one was open for 1% of the time, Pallas kernels for 13%

profile of v2, /device:TPU:0, one launch (start us, length us, event | category | flops | bytes accessed | tf_op | source)
XLA Modules:
  0.0 255.2 jit_solution(3239533366605918450)
XLA Ops:
  7.3 2.1 broadcast_in_dim.7
  9.4 7.1 %all-to-all-start = ((bf16[16,64,640]{2,1,0:T(8,128)(2,1)}), bf16[16,64,640]{2,1,0:T(8,128)(2,1)S(1)}, u32[]{:S(2)}, u32[]{:S(2)}) async-start(bf16[16,64,640]{2,1,0:T(8,128)(2,1)} %broadcast_in_dim.7), calls=%async_computation | async-start | bytes 2621440 | tf_op jit(solution)/shard_map/all_to_all | solution.py:46
  16.9 2.0 collective-permute-start
  18.8 3.6 %collective-permute-start.1 = (bf16[16,1280]{1,0:T(8,128)(2,1)S(1)}, bf16[16,1280]{1,0:T(8,128)(2,1)S(1)}, u32[]{:S(2)}, u32[]{:S(2)}) collective-permute-start(bf16[16,1280]{1,0:T(8,128)(2,1)S(1)} %get-tuple-element.27), channel_id=1, source_target_pairs={{0,2},{1,3},{2,0},{3,1},{4,6},{5,7},{6,4},{7,5},{8,10},{9,11},{10,... | collective-permute-start | bytes 122888 | tf_op jit(solution)/shard_map/ppermute | solution.py:58
  22.4 1.0 collective-permute-start.2
  24.0 0.8 collective-permute-done.1
  24.9 1.6 collective-permute-done.2
  26.5 12.4 %all-to-all-done.q_ref = bf16[16,64,640]{2,1,0:T(8,128)(2,1)S(1)} async-done(((bf16[16,64,640]{2,1,0:T(8,128)(2,1)}), bf16[16,64,640]{2,1,0:T(8,128)(2,1)S(1)}, u32[]{:S(2)}, u32[]{:S(2)}) %all-to-all-start) | async-done | bytes 1310752 | tf_op jit(solution)/shard_map/all_to_all | solution.py:46
  40.4 21.8 %attend.1 = bf16[1024,768]{1,0:T(8,128)(2,1)} custom-call(s32[2]{0:T(128)} %pad_add_fusion.place_ref, bf16[16,64,640]{2,1,0:T(8,128)(2,1)} %copy-done.5, bf16[1024,640]{1,0:T(8,128)(2,1)} %ka_ref.1, bf16[1024,640]{1,0:T(8,128)(2,1)} %collective-permute-done.3.kb_ref, bf16[64,640]{1,0:T(8,128)(2,1)} %na_ref.1, bf16[64,640]{1,0:T(8,128)(2,1)} %copy-done.11, ...), custom_call_target="tpu_custom_call" | custom-call | flops 11000000512 | bytes 10000000 | tf_op jit(solution)/shard_map/attend/pallas_call | solution.py:125
  62.2 27.9 %all_to_all.30.parts_ref = bf16[16,64,768]{2,1,0:T(8,128)(2,1)} all-to-all(bf16[16,64,768]{2,1,0:T(8,128)(2,1)} %bitcast.34), channel_id=1, replica_groups=mesh['y'=4,'xh'=2,'xl'=2,'c'=2,'z'=4] {'y','xh','xl'}, dimensions={0} | all-to-all | bytes 3145728 | tf_op jit(solution)/shard_map/all_to_all | solution.py:46
  90.1 6.8 %project.1 = bf16[4,64,1152]{2,1,0:T(8,128)(2,1)} custom-call(bf16[16,64,768]{2,1,0:T(8,128)(2,1)} %all_to_all.30.parts_ref, bf16[4608,640]{1,0:T(8,128)(2,1)} %all-gather.2.cloned.1.call-done.weight_ref), custom_call_target="tpu_custom_call" | custom-call | flops 400000000 | bytes 8000000 | tf_op jit(solution)/shard_map/project/pallas_call | solution.py:166
  97.0 5.8 %all-to-all-start.2 = ((bf16[4,64,1152]{2,1,0:T(8,128)(2,1)}), bf16[4,64,1152]{2,1,0:T(8,128)(2,1)S(1)}, u32[]{:S(2)}, u32[]{:S(2)}) async-start(bf16[4,64,1152]{2,1,0:T(8,128)(2,1)} %project.1), calls=%async_computation.2 | async-start | bytes 1179648 | tf_op jit(solution)/shard_map/all_to_all | solution.py:46
  102.8 0.8 dynamic_slice.36
  103.6 8.7 %all-to-all-done.2.heads_ref = bf16[4,64,1152]{2,1,0:T(8,128)(2,1)S(1)} async-done(((bf16[4,64,1152]{2,1,0:T(8,128)(2,1)}), bf16[4,64,1152]{2,1,0:T(8,128)(2,1)S(1)}, u32[]{:S(2)}, u32[]{:S(2)}) %all-to-all-start.2) | async-done | bytes 589856 | tf_op jit(solution)/shard_map/all_to_all | solution.py:46
  112.2 4.0 %pack.1 = (bf16[64,1152]{1,0:T(8,128)(2,1)S(1)}, f32[64,128]{1,0:T(8,128)S(1)}, bf16[4,8,2,16,1536]{4,3,2,1,0:T(8,128)(2,1)}) custom-call(bf16[4,64,1152]{2,1,0:T(8,128)(2,1)S(1)} %all-to-all-done.2.heads_ref, bf16[64,1280]{1,0:T(8,128)(2,1)S(1)} %bitcast.30, f32[1,1152]{1,0:T(1,128)S(1)} %broadcast_in_dim.8.gain_ref), custom_call_target="tpu_custom_call" | custom-call | flops 30000000 | bytes 5000000 | tf_op jit(solution)/shard_map/pack/pallas_call | solution.py:255
  117.5 4.9 %all-to-all-start.3 = ((bf16[64,16,1536]{2,1,0:T(8,128)(2,1)}), bf16[64,16,1536]{2,1,0:T(8,128)(2,1)S(1)}, u32[]{:S(2)}, u32[]{:S(2)}) async-start(bf16[64,16,1536]{2,1,0:T(8,128)(2,1)} %bitcast.12), calls=%async_computation.3 | async-start | bytes 6291456 | tf_op jit(solution)/shard_map/all_to_all | solution.py:46
  122.5 40.3 %all-to-all-done.3 = bf16[64,16,1536]{2,1,0:T(8,128)(2,1)S(1)} async-done(((bf16[64,16,1536]{2,1,0:T(8,128)(2,1)}), bf16[64,16,1536]{2,1,0:T(8,128)(2,1)S(1)}, u32[]{:S(2)}, u32[]{:S(2)}) %all-to-all-start.3) | async-done | bytes 3145760 | tf_op jit(solution)/shard_map/all_to_all | solution.py:46
  162.8 1.8 copy-done.4
  164.5 23.2 %experts.1 = bf16[4,256,1536]{2,1,0:T(8,128)(2,1)} custom-call(bf16[4,256,1536]{2,1,0:T(8,128)(2,1)} %bitcast.32, bf16[4608,768]{1,0:T(8,128)(2,1)} %ga_hbm.1, bf16[4608,768]{1,0:T(8,128)(2,1)} %collective-permute-done.7.gb_hbm, bf16[4608,768]{1,0:T(8,128)(2,1)} %ua_hbm.1, bf16[4608,768]{1,0:T(8,128)(2,1)} %collective-permute-done.8.ub_hbm, ...), custom_call_target="tpu_custom_call" | custom-call | flops 14000000000 | bytes 48000000 | tf_op jit(solution)/shard_map/experts/pallas_call | solution.py:398
  187.7 6.7 %all-to-all-start.4 = ((bf16[64,16,1536]{2,1,0:T(8,128)(2,1)}), bf16[64,16,1536]{2,1,0:T(8,128)(2,1)S(1)}, u32[]{:S(2)}, u32[]{:S(2)}) async-start(bf16[64,16,1536]{2,1,0:T(8,128)(2,1)} %bitcast.33), calls=%async_computation.4 | async-start | bytes 6291456 | tf_op jit(solution)/shard_map/all_to_all | solution.py:46
  195.5 40.4 %all-to-all-done.4 = bf16[64,16,1536]{2,1,0:T(8,128)(2,1)S(1)} async-done(((bf16[64,16,1536]{2,1,0:T(8,128)(2,1)}), bf16[64,16,1536]{2,1,0:T(8,128)(2,1)S(1)}, u32[]{:S(2)}, u32[]{:S(2)}) %all-to-all-start.4) | async-done | bytes 3145760 | tf_op jit(solution)/shard_map/all_to_all | solution.py:46
  235.9 0.9 copy-done.1
  236.8 2.4 combine.1
  239.2 8.4 %all_to_all.31 = bf16[4,16,1152]{2,1,0:T(8,128)(2,1)S(1)} all-to-all(bf16[4,16,1152]{2,1,0:T(8,128)(2,1)S(1)} %bitcast.31), channel_id=1, replica_groups=mesh['y'=4,'xh'=2,'xl'=2,'c'=2,'z'=4] {'z'}, dimensions={0} | all-to-all | bytes 294912 | tf_op jit(solution)/shard_map/all_to_all | solution.py:46
  (60 shorter events, 6.1 us)
Async XLA Ops:
  6.5 10.0 %copy-start.7 = (f32[16,2]{0,1:T(2,128)S(1)}, f32[16,2]{0,1:T(2,128)}, u32[]{:S(2)}) copy-start(f32[16,2]{0,1:T(2,128)} %param.22) | copy-start | bytes 388
  6.5 10.0 %copy-start.13 = (s32[16,2]{0,1:T(2,128)S(1)}, s32[16,2]{0,1:T(2,128)}, u32[]{:S(2)}) copy-start(s32[16,2]{0,1:T(2,128)} %param.21) | copy-start | bytes 388
  6.5 10.2 %copy-start.6 = (bf16[16,4608]{1,0:T(8,128)(2,1)S(1)}, bf16[16,4608]{1,0:T(8,128)(2,1)}, u32[]{:S(2)}) copy-start(bf16[16,4608]{1,0:T(8,128)(2,1)} %param.13) | copy-start | bytes 442372
  6.5 16.9 %copy-start.8 = (bf16[1024,640]{1,0:T(8,128)(2,1)S(1)}, bf16[1024,640]{1,0:T(8,128)(2,1)}, u32[]{:S(2)}) copy-start(bf16[1024,640]{1,0:T(8,128)(2,1)} %ka_ref.1) | copy-start | bytes 3932164
  6.5 17.4 %copy-start.9 = (bf16[64,640]{1,0:T(8,128)(2,1)S(1)}, bf16[64,640]{1,0:T(8,128)(2,1)}, u32[]{:S(2)}) copy-start(bf16[64,640]{1,0:T(8,128)(2,1)} %na_ref.1) | copy-start | bytes 245764
  6.6 18.3 %copy-start.10 = (bf16[64,640]{1,0:T(8,128)(2,1)S(1)}, bf16[64,640]{1,0:T(8,128)(2,1)}, u32[]{:S(2)}) copy-start(bf16[64,640]{1,0:T(8,128)(2,1)} %wa_ref.1) | copy-start | bytes 245764
  6.6 83.6 %all-gather.2.cloned.1.call-start = ((), (), s32[]{:S(2)}) async-start(), calls=%async_computation.6 | async-start | bytes 6082560 | tf_op jit(solution)/shard_map/all_gather | solution.py:518
  9.4 29.5 %all-to-all-start = ((bf16[16,64,640]{2,1,0:T(8,128)(2,1)}), bf16[16,64,640]{2,1,0:T(8,128)(2,1)S(1)}, u32[]{:S(2)}, u32[]{:S(2)}) async-start(bf16[16,64,640]{2,1,0:T(8,128)(2,1)} %broadcast_in_dim.7), calls=%async_computation | async-start | bytes 2621440 | tf_op jit(solution)/shard_map/all_to_all | solution.py:46
  16.9 7.1 %collective-permute-start = (bf16[16,1280]{1,0:T(8,128)(2,1)S(1)}, bf16[16,1280]{1,0:T(8,128)(2,1)S(1)}, u32[]{:S(2)}, u32[]{:S(2)}) collective-permute-start(bf16[16,1280]{1,0:T(8,128)(2,1)S(1)} %get-tuple-element.26), channel_id=1, source_target_pairs={{0,1},{1,2},{2,3},{3,0},{4,5},{5,6},{6,7},{7,4},{8,9},{9,10},{10,1... | collective-permute-start | bytes 122888 | tf_op jit(solution)/shard_map/ppermute | solution.py:58
  18.8 6.0 %collective-permute-start.1 = (bf16[16,1280]{1,0:T(8,128)(2,1)S(1)}, bf16[16,1280]{1,0:T(8,128)(2,1)S(1)}, u32[]{:S(2)}, u32[]{:S(2)}) collective-permute-start(bf16[16,1280]{1,0:T(8,128)(2,1)S(1)} %get-tuple-element.27), channel_id=1, source_target_pairs={{0,2},{1,3},{2,0},{3,1},{4,6},{5,7},{6,4},{7,5},{8,10},{9,11},{10,... | collective-permute-start | bytes 122888 | tf_op jit(solution)/shard_map/ppermute | solution.py:58
  22.4 4.0 %collective-permute-start.2 = (bf16[16,1280]{1,0:T(8,128)(2,1)S(1)}, bf16[16,1280]{1,0:T(8,128)(2,1)S(1)}, u32[]{:S(2)}, u32[]{:S(2)}) collective-permute-start(bf16[16,1280]{1,0:T(8,128)(2,1)S(1)} %get-tuple-element.28), channel_id=1, source_target_pairs={{0,3},{1,0},{2,1},{3,2},{4,7},{5,4},{6,5},{7,6},{8,11},{9,8},{10,9... | collective-permute-start | bytes 122888 | tf_op jit(solution)/shard_map/ppermute | solution.py:58
  23.4 16.9 %collective-permute-start.3 = (bf16[1024,640]{1,0:T(8,128)(2,1)S(1)}, bf16[1024,640]{1,0:T(8,128)(2,1)}, u32[]{:S(2)}, u32[]{:S(2)}) collective-permute-start(bf16[1024,640]{1,0:T(8,128)(2,1)S(1)} %copy-done.8), channel_id=1, source_target_pairs={{0,4},{4,0},{1,5},{5,1},{2,6},{6,2},{3,7},{7,3},{8,12},{12,8},{9,1... | collective-permute-start | bytes 3932168 | tf_op jit(solution)/shard_map/ppermute | solution.py:50
  23.4 16.9 %collective-permute-start.5 = (bf16[1024,640]{1,0:T(8,128)(2,1)}, bf16[1024,640]{1,0:T(8,128)(2,1)}, u32[]{:S(2)}, u32[]{:S(2)}) collective-permute-start(bf16[1024,640]{1,0:T(8,128)(2,1)} %va_ref.1), channel_id=1, source_target_pairs={{0,4},{4,0},{1,5},{5,1},{2,6},{6,2},{3,7},{7,3},{8,12},{12,8},{9,1... | collective-permute-start | bytes 3932168 | tf_op jit(solution)/shard_map/ppermute | solution.py:50
  24.0 15.0 %collective-permute-start.4 = (bf16[64,640]{1,0:T(8,128)(2,1)S(1)}, bf16[64,640]{1,0:T(8,128)(2,1)S(1)}, u32[]{:S(2)}, u32[]{:S(2)}) collective-permute-start(bf16[64,640]{1,0:T(8,128)(2,1)S(1)} %copy-done.9), channel_id=1, source_target_pairs={{0,4},{4,0},{1,5},{5,1},{2,6},{6,2},{3,7},{7,3},{8,12},{12,8},{9,1... | collective-permute-start | bytes 245768 | tf_op jit(solution)/shard_map/ppermute | solution.py:50
  24.9 14.6 %collective-permute-start.6 = (bf16[64,640]{1,0:T(8,128)(2,1)S(1)}, bf16[64,640]{1,0:T(8,128)(2,1)S(1)}, u32[]{:S(2)}, u32[]{:S(2)}) collective-permute-start(bf16[64,640]{1,0:T(8,128)(2,1)S(1)} %copy-done.10), channel_id=1, source_target_pairs={{0,4},{4,0},{1,5},{5,1},{2,6},{6,2},{3,7},{7,3},{8,12},{12,8},{9,1... | collective-permute-start | bytes 245768 | tf_op jit(solution)/shard_map/ppermute | solution.py:50
  38.9 1.5 copy-start.5
  38.9 83.5 %collective-permute-start.7 = (bf16[4608,768]{1,0:T(8,128)(2,1)}, bf16[4608,768]{1,0:T(8,128)(2,1)}, u32[]{:S(2)}, u32[]{:S(2)}) collective-permute-start(bf16[4608,768]{1,0:T(8,128)(2,1)} %ga_hbm.1), channel_id=1, source_target_pairs={{0,4},{4,0},{1,5},{5,1},{2,6},{6,2},{3,7},{7,3},{8,12},{12,8},{9,1... | collective-permute-start | bytes 21233672 | tf_op jit(solution)/shard_map/ppermute | solution.py:50
  38.9 1.5 copy-start.11
  38.9 83.5 %collective-permute-start.8 = (bf16[4608,768]{1,0:T(8,128)(2,1)}, bf16[4608,768]{1,0:T(8,128)(2,1)}, u32[]{:S(2)}, u32[]{:S(2)}) collective-permute-start(bf16[4608,768]{1,0:T(8,128)(2,1)} %ua_hbm.1), channel_id=1, source_target_pairs={{0,4},{4,0},{1,5},{5,1},{2,6},{6,2},{3,7},{7,3},{8,12},{12,8},{9,1... | collective-permute-start | bytes 21233672 | tf_op jit(solution)/shard_map/ppermute | solution.py:50
  39.4 83.0 %collective-permute-start.9 = (bf16[768,4608]{1,0:T(8,128)(2,1)}, bf16[768,4608]{1,0:T(8,128)(2,1)}, u32[]{:S(2)}, u32[]{:S(2)}) collective-permute-start(bf16[768,4608]{1,0:T(8,128)(2,1)} %da_hbm.1), channel_id=1, source_target_pairs={{0,4},{4,0},{1,5},{5,1},{2,6},{6,2},{3,7},{7,3},{8,12},{12,8},{9,1... | collective-permute-start | bytes 21233672 | tf_op jit(solution)/shard_map/ppermute | solution.py:50
  97.0 15.3 %all-to-all-start.2 = ((bf16[4,64,1152]{2,1,0:T(8,128)(2,1)}), bf16[4,64,1152]{2,1,0:T(8,128)(2,1)S(1)}, u32[]{:S(2)}, u32[]{:S(2)}) async-start(bf16[4,64,1152]{2,1,0:T(8,128)(2,1)} %project.1), calls=%async_computation.2 | async-start | bytes 1179648 | tf_op jit(solution)/shard_map/all_to_all | solution.py:46
  117.5 45.3 %all-to-all-start.3 = ((bf16[64,16,1536]{2,1,0:T(8,128)(2,1)}), bf16[64,16,1536]{2,1,0:T(8,128)(2,1)S(1)}, u32[]{:S(2)}, u32[]{:S(2)}) async-start(bf16[64,16,1536]{2,1,0:T(8,128)(2,1)} %bitcast.12), calls=%async_computation.3 | async-start | bytes 6291456 | tf_op jit(solution)/shard_map/all_to_all | solution.py:46
  162.8 1.8 copy-start.4
  187.7 48.2 %all-to-all-start.4 = ((bf16[64,16,1536]{2,1,0:T(8,128)(2,1)}), bf16[64,16,1536]{2,1,0:T(8,128)(2,1)S(1)}, u32[]{:S(2)}, u32[]{:S(2)}) async-start(bf16[64,16,1536]{2,1,0:T(8,128)(2,1)} %bitcast.33), calls=%async_computation.4 | async-start | bytes 6291456 | tf_op jit(solution)/shard_map/all_to_all | solution.py:46
  (5 other events, 3.9 us)
Sparse Core Ops, SparseCore 0:
  9.7 64.8 all-gather.1

commit v3 on v2

--- a/solution.py
+++ b/solution.py
@@ -23,7 +23,7 @@
 THIRD = SLICE // 3
 CHUNK = SLICE + THIRD
 PACK = 128
-WIDE = HEADS * HD + PACK
+LINES = HEADS * Q_DEV + 8
 NORM_EPS = 1e-06
 NEGATIVE = -1e30
 TO_BASE2 = math.log2(math.e) / math.sqrt(HD)
@@ -36,6 +36,7 @@
 
 VMEM = pl.BlockSpec(memory_space=pltpu.VMEM)
 HBM = pl.BlockSpec(memory_space=pltpu.HBM)
+ANY = pl.BlockSpec(memory_space=pl.ANY)
 
 
 def params(mib):
@@ -80,7 +81,7 @@
 
 def attend_kernel(place_ref, q_ref, ka_ref, kb_ref, na_ref, nb_ref, va_ref, vb_ref, wa_ref, wb_ref, out_ref):
     core, mine = place_ref[0], place_ref[1]
-    rows = out_ref.shape[0]
+    rows = Q_BLOCKS * Q_DEV
     row = lax.broadcasted_iota(jnp.int32, (rows, HD), 0)
     lane = lax.broadcasted_iota(jnp.int32, (rows, HD), 1)
     block = pl.program_id(0) * Q_BLOCKS + row // Q_DEV
@@ -88,6 +89,7 @@
     k_pos = jnp.where(lane < Q_DEV, mine * Q_DEV + lane, (mine + 1 - 2 * core) * Q_DEV + lane - Q_DEV)
     allowed = k_pos <= q_pos
     pack = jnp.zeros((rows, PACK), F32)
+    group = row % Q_DEV // 8 * 16
     for h in range(HEADS):
         cols = slice(h * HD, (h + 1) * HD)
         q = q_ref[:, :, cols].reshape(rows, HD)
@@ -113,25 +115,27 @@
             + dot_nn(w2.astype(BF16), vb_ref[:, cols])
             + dot_nn(w3.astype(BF16), fresh_v)
         )
-        out_ref[:, cols] = (acc / total).astype(BF16)
+        out_ref[:, h * Q_DEV : (h + 1) * Q_DEV, :] = (
+            (acc / total).astype(BF16).reshape(Q_BLOCKS, Q_DEV, HD)
+        )
         for part, value in enumerate(three_parts(top + jnp.log2(total))):
-            pack = jnp.where(lane == part * 8 + h, value, pack)
-    out_ref[:, HEADS * HD :] = pack.astype(BF16)
+            pack = jnp.where(lane == group + part * HEADS + h, value, pack)
+    folded = jnp.sum(pack.reshape(Q_BLOCKS, 8, 8, PACK), axis=1)
+    out_ref[:, HEADS * Q_DEV :, :] = folded.astype(BF16)
 
 
 def attend(place, q, *keys):
-    rows = Q_BLOCKS * Q_DEV
     whole = [pl.BlockSpec(a.shape, lambda i: (0, 0)) for a in keys]
     return pl.pallas_call(
         attend_kernel,
         grid=(PLANE // Q_BLOCKS,),
-        out_shape=jax.ShapeDtypeStruct((PLANE * Q_DEV, WIDE), BF16),
+        out_shape=jax.ShapeDtypeStruct((PLANE, LINES, HD), BF16),
         in_specs=[
             pl.BlockSpec(memory_space=pltpu.SMEM),
             pl.BlockSpec((Q_BLOCKS, Q_DEV, HEADS * HD), lambda i: (i, 0, 0)),
             *whole,
         ],
-        out_specs=pl.BlockSpec((rows, WIDE), lambda i: (i, 0)),
+        out_specs=pl.BlockSpec((Q_BLOCKS, LINES, HD), lambda i: (i, 0, 0)),
         compiler_params=params(56),
         cost_estimate=pl.CostEstimate(flops=11 * 10**9, bytes_accessed=10**7, transcendentals=11 * 10**6),
         name="attend",
@@ -140,17 +144,25 @@
 
 def merge(parts_ref, out_ref):
     count = parts_ref.shape[0]
-    sums = [parts_ref[i, :, HEADS * HD :].astype(F32) for i in range(count)]
+    sums = [parts_ref[i, HEADS * Q_DEV :, :].astype(F32) for i in range(count)]
+    sums = [
+        s + pltpu.roll(s, PACK - HEADS, axis=1) + pltpu.roll(s, PACK - 2 * HEADS, axis=1) for s in sums
+    ]
     for h in range(HEADS):
-        cols = slice(h * HD, (h + 1) * HD)
-        logs = [s[:, h : h + 1] + s[:, 8 + h : 9 + h] + s[:, 16 + h : 17 + h] for s in sums]
+        logs = [
+            jnp.concatenate([s[:, g * 16 + h : g * 16 + h + 1] for g in range(8)], axis=0) for s in sums
+        ]
         top = functools.reduce(jnp.maximum, logs)
         shares = [jnp.exp2(v - top) for v in logs]
         total = functools.reduce(jnp.add, shares)
         acc = functools.reduce(
-            jnp.add, [shares[i] * parts_ref[i, :, cols].astype(F32) for i in range(count)]
+            jnp.add,
+            [
+                shares[i] * parts_ref[i, h * Q_DEV : (h + 1) * Q_DEV, :].astype(F32)
+                for i in range(count)
+            ],
         )
-        out_ref[:, cols] = (acc / total).astype(BF16)
+        out_ref[:, h * HD : (h + 1) * HD] = (acc / total).astype(BF16)
 
 
 def project_kernel(parts_ref, weight_ref, out_ref, attended_ref):
@@ -185,50 +197,26 @@
     return i, j
 
 
-def pack_kernel(heads_ref, own_ref, gain_ref, stream_ref, routes_ref, chunk_ref, made_ref, sems):
-    total = own_ref[:, :SLICE].astype(F32)
+def pack_kernel(heads_ref, own_ref, gain_ref, main_ref, over_ref, spread_ref, stream_ref, chunk_ref, made_ref, sems):
     summed = heads_ref[0].astype(F32)
     for z in range(1, NZ):
         summed = summed + heads_ref[z].astype(F32)
-    stream = (total + summed).astype(BF16)
+    stream = (own_ref[:, :SLICE].astype(F32) + summed).astype(BF16)
     stream_ref[...] = stream
     stream_f = stream.astype(F32)
     squares = stream_f * stream_f
     scaled = (stream_f * gain_ref[...]).astype(BF16)
-    routes = own_ref[:, SLICE:]
-    routes_ref[...] = routes.astype(F32)
-    kind, lane = iotas(8, PACK)
-    turned = dot_nt(jnp.where(kind == lane, 1.0, 0.0).astype(BF16), routes)
-    first, second = turned[0:1, :], turned[1:2, :]
-    expert = lax.broadcasted_iota(jnp.int32, (E, Q_DEV), 0).astype(F32)
-    hot0 = jnp.where(expert == first, 1.0, 0.0)
-    hot1 = jnp.where(expert == second, 1.0, 0.0)
-    j, i = earlier()
-    before_t = jnp.where((j < i) & (j // 16 == i // 16), 1.0, 0.0)
-    counts = dot_nn((hot0 + hot1).astype(BF16), before_t.astype(BF16))
-    base = (lax.broadcasted_iota(jnp.int32, (1, Q_DEV), 1) // 16 * CAP).astype(F32)
-    slot0 = jnp.sum(counts * hot0, axis=0, keepdims=True) + base
-    slot1 = jnp.sum(counts * hot1, axis=0, keepdims=True) + base
-
-    def placing(slot, which):
-        return jnp.where(
-            ((slot == slot0) & (which == first)) | ((slot == slot1) & (which == second)), 1.0, 0.0
-        )
-
-    line = lax.broadcasted_iota(jnp.int32, (E * MAIN, Q_DEV), 0)
-    which = (line // MAIN).astype(F32)
-    part = line % MAIN
-    main = dot_nn(placing(part.astype(F32), which).astype(BF16), scaled).astype(BF16)
+    main = dot_nn(main_ref[...], scaled).astype(BF16)
     over = jnp.zeros((E * MAIN, THIRD), F32)
     for t in range(3):
-        wanted = jnp.where(part // OVER == t, MAIN + part % OVER, -1).astype(F32)
-        over = over + dot_nn(placing(wanted, which).astype(BF16), scaled[:, t * THIRD : (t + 1) * THIRD])
+        over = over + dot_nn(over_ref[t], scaled[:, t * THIRD : (t + 1) * THIRD])
     sums_row = dot_nt(jnp.ones((8, SLICE), F32), squares, precision=lax.Precision.HIGHEST)
-    slot = lax.broadcasted_iota(jnp.int32, (HD, Q_DEV), 0).astype(F32)
+    parts = jnp.concatenate(three_parts(sums_row), axis=0).astype(BF16)
+    placed = dot_nt(parts, spread_ref[...])
     row = lax.broadcasted_iota(jnp.int32, (MAIN, HD), 0)
     for e in range(E):
-        placed = dot_nt(sums_row, placing(slot, float(e)), precision=lax.Precision.HIGHEST)[0:1, :]
-        high, middle, low = three_parts(placed)
+        lanes = slice(e * HD, (e + 1) * HD)
+        high, middle, low = placed[0:1, lanes], placed[8:9, lanes], placed[16:17, lanes]
         extra = jnp.where(
             row == 3 * OVER,
             high,
@@ -251,21 +239,20 @@
         copy.wait()
 
 
-def pack(heads, own, gain):
+def pack(heads, own, gain, main, over, spread):
     return pl.pallas_call(
         pack_kernel,
         out_shape=(
             jax.ShapeDtypeStruct((Q_DEV, SLICE), BF16),
-            jax.ShapeDtypeStruct((Q_DEV, PACK), F32),
             jax.ShapeDtypeStruct((NZ, E, 2, MAIN, CHUNK), BF16),
         ),
-        in_specs=[VMEM] * 3,
-        out_specs=(VMEM, VMEM, HBM),
+        in_specs=[VMEM] * 6,
+        out_specs=(VMEM, HBM),
         scratch_shapes=[pltpu.VMEM((E, MAIN, CHUNK), BF16), pltpu.SemaphoreType.DMA((NZ, 2))],
         compiler_params=params(40),
         cost_estimate=pl.CostEstimate(flops=3 * 10**7, bytes_accessed=5 * 10**6, transcendentals=0),
         name="pack",
-    )(heads, own, gain)
+    )(heads, own, gain, main, over, spread)
 
 
 RCV = PLANE * MAIN
@@ -323,8 +310,8 @@
 
 
 def experts_kernel(
-    x_ref, ga_hbm, gb_hbm, ua_hbm, ub_hbm, da_hbm, db_hbm, out_hbm,
-    made_ref, rows_ref, scale_ref, hidden_ref, gate_ref, up_ref, down_ref, weight_sem, down_sem, out_sem,
+    x_any, ga_hbm, gb_hbm, ua_hbm, ub_hbm, da_hbm, db_hbm, out_hbm,
+    made_ref, rows_ref, scale_ref, hidden_ref, gate_ref, up_ref, down_ref, x_sem, weight_sem, down_sem, out_sem,
 ):
     steps = ga_hbm.shape[1] // F_BLOCK
 
@@ -347,10 +334,13 @@
             for z in range(NZ)
         ]
 
+    arrive = pltpu.make_async_copy(x_any, made_ref, x_sem)
+    arrive.start()
     for step in range(AHEAD):
         for copy in weight_copies(step, ga_hbm, ua_hbm, step):
             copy.start()
-    scale_ref[...] = jnp.broadcast_to(unpack(x_ref, rows_ref), (ALL, HD))
+    arrive.wait()
+    scale_ref[...] = jnp.broadcast_to(unpack(made_ref, rows_ref), (ALL, HD))
 
     @pl.loop(0, 2 * steps)
     def _(step):
@@ -398,7 +388,7 @@
     return pl.pallas_call(
         experts_kernel,
         out_shape=jax.ShapeDtypeStruct(x.shape, BF16),
-        in_specs=[VMEM] + [HBM] * 6,
+        in_specs=[ANY] + [HBM] * 6,
         out_specs=HBM,
         scratch_shapes=[
             pltpu.VMEM(x.shape, BF16),
@@ -408,6 +398,7 @@
             pltpu.VMEM((SLOTS, D, F_BLOCK), BF16),
             pltpu.VMEM((SLOTS, D, F_BLOCK), BF16),
             pltpu.VMEM((2, NZ, width, SLICE), BF16),
+            pltpu.SemaphoreType.DMA,
             pltpu.SemaphoreType.DMA((2, SLOTS)),
             pltpu.SemaphoreType.DMA((2, NZ)),
             pltpu.SemaphoreType.DMA((NZ,)),
@@ -418,7 +409,38 @@
     )(x, ga, gb, ua, ub, da, db)
 
 
-def mixing_kernel(routes_ref, mix_ref):
+def place_rows(codes, main_ref, over_ref, spread_ref):
+    kind, lane = iotas(8, PACK)
+    turned = dot_nt(jnp.where(kind == lane, 1.0, 0.0).astype(BF16), codes)
+    first, second = turned[0:1, :], turned[1:2, :]
+    expert = lax.broadcasted_iota(jnp.int32, (E, Q_DEV), 0).astype(F32)
+    hot0 = jnp.where(expert == first, 1.0, 0.0)
+    hot1 = jnp.where(expert == second, 1.0, 0.0)
+    j, i = earlier()
+    before_t = jnp.where((j < i) & (j // 16 == i // 16), 1.0, 0.0)
+    counts = dot_nn((hot0 + hot1).astype(BF16), before_t.astype(BF16))
+    base = (lax.broadcasted_iota(jnp.int32, (1, Q_DEV), 1) // 16 * CAP).astype(F32)
+    slot0 = jnp.sum(counts * hot0, axis=0, keepdims=True) + base
+    slot1 = jnp.sum(counts * hot1, axis=0, keepdims=True) + base
+
+    def placing(slot, which):
+        hit = ((slot == slot0) & (which == first)) | ((slot == slot1) & (which == second))
+        return jnp.where(hit, 1.0, 0.0).astype(BF16)
+
+    line = lax.broadcasted_iota(jnp.int32, (E * MAIN, Q_DEV), 0)
+    which = (line // MAIN).astype(F32)
+    part = line % MAIN
+    main_ref[...] = placing(part.astype(F32), which)
+    for t in range(3):
+        over_ref[t] = placing(jnp.where(part // OVER == t, MAIN + part % OVER, -1).astype(F32), which)
+    line = lax.broadcasted_iota(jnp.int32, (E * HD, Q_DEV), 0)
+    spread_ref[...] = placing((line % HD).astype(F32), (line // HD).astype(F32))
+
+
+def routing_kernel(own_ref, main_ref, over_ref, spread_ref, mix_ref):
+    codes = own_ref[:, SLICE:]
+    place_rows(codes, main_ref, over_ref, spread_ref)
+    routes_ref = codes.astype(F32)
     first, second = routes_ref[:, 0:1], routes_ref[:, 1:2]
     weight0 = routes_ref[:, 2:3] + routes_ref[:, 3:4] + routes_ref[:, 4:5]
     weight1 = routes_ref[:, 5:6] + routes_ref[:, 6:7] + routes_ref[:, 7:8]
@@ -444,14 +466,19 @@
             mix_ref[kind, at * Q_DEV : (at + 1) * Q_DEV, :] = value.astype(BF16)
 
 
-def mixing(routes):
+def routing(own):
     return pl.pallas_call(
-        mixing_kernel,
-        out_shape=jax.ShapeDtypeStruct((4, 3 * Q_DEV, RCV), BF16),
+        routing_kernel,
+        out_shape=(
+            jax.ShapeDtypeStruct((E * MAIN, Q_DEV), BF16),
+            jax.ShapeDtypeStruct((3, E * MAIN, Q_DEV), BF16),
+            jax.ShapeDtypeStruct((E * HD, Q_DEV), BF16),
+            jax.ShapeDtypeStruct((4, 3 * Q_DEV, RCV), BF16),
+        ),
         compiler_params=params(30),
-        cost_estimate=pl.CostEstimate(flops=10**6, bytes_accessed=4 * 10**5, transcendentals=0),
-        name="mixing",
-    )(routes)
+        cost_estimate=pl.CostEstimate(flops=10**6, bytes_accessed=10**6, transcendentals=0),
+        name="routing",
+    )(own)
 
 
 def combine_kernel(returned_hbm, stream_ref, mix_ref, out_ref, returned_ref, sems):
@@ -482,7 +509,7 @@
     return pl.pallas_call(
         combine_kernel,
         out_shape=jax.ShapeDtypeStruct((Q_DEV, SLICE), BF16),
-        in_specs=[HBM, VMEM, VMEM],
+        in_specs=[ANY, VMEM, VMEM],
         out_specs=VMEM,
         scratch_shapes=[pltpu.VMEM(returned.shape, BF16), pltpu.SemaphoreType.DMA((NZ,))],
         compiler_params=params(40),
@@ -529,7 +556,8 @@
     own = jnp.transpose(residual.reshape(tok, NZ, SLICE), (1, 0, 2))
     own = jnp.concatenate([own, jnp.broadcast_to(codes[None], (NZ, tok, PACK))], axis=2)
     own = around_z(own, depth).reshape(Q_DEV, SLICE + PACK)
-    own, all_queries = lax.optimization_barrier((own, all_queries))
+    main, over, spread, mix = routing(own)
+    mix, all_queries = lax.optimization_barrier((mix, all_queries))
 
     place = jnp.stack([core, mine]).astype(jnp.int32)
     partial = attend(
@@ -538,11 +566,10 @@
     )
     after = lax.optimization_barrier((gate_weight, up_weight, down_weight, all_queries))
     far_gate, far_up, far_down = (other_core(w) for w in after[:3])
-    parts = exchange(partial.reshape(PLANE, Q_DEV, WIDE), XY)
+    parts = exchange(partial, XY)
     heads = exchange(project(parts, weight_t), ("z",))
     gain = lax.dynamic_slice_in_dim(norm_gain, depth * SLICE, SLICE, 0)[None]
-    stream, routes, chunks = pack(heads, own, gain)
-    mix = mixing(routes)
+    stream, chunks = pack(heads, own, gain, main, over, spread)
     arrived = exchange(chunks.reshape(NZ * PLANE, MAIN, CHUNK), ZXY).reshape(NZ, RCV, CHUNK)
     answers = experts(arrived, gate_weight, far_gate, up_weight, far_up, down_weight, far_down)
     returned = exchange(answers.reshape(NZ * PLANE, MAIN, CHUNK), ZXY).reshape(NZ, RCV, CHUNK)

time: 256 us -> 248 us (0.969)
  blocking collectives: 36.4 us -> 80.5 us
  waiting for transfers between devices: 105 us -> 62.7 us
  starting transfers between devices: 32.5 us -> 26.8 us
  local copies, waits for them, and re-layouts: 8.44 us -> 3.77 us
    all_to_all x2 -> x3, blocking collectives: 36.4 us -> 80.5 us  [exchange(): return lax.all_to_all(block, axes, split_axis=0, concat_axis=0, tiled=True)]
    all_to_all x4 -> x3, waiting for transfers between devices: 102 us -> 59.7 us  [exchange(): return lax.all_to_all(block, axes, split_axis=0, concat_axis=0, tiled=True)]
    all_to_all x4 -> x3, starting transfers between devices: 24.5 us -> 18.8 us  [exchange(): return lax.all_to_all(block, axes, split_axis=0, concat_axis=0, tiled=True)]
    unnamed x29 -> x17, local copies, waits for them, and re-layouts: 4.8 us -> 0.12 us
  transfers between devices with their start and end apart: 15 -> 14, of which waited for: 6 -> 5; matrix products, arithmetic and copies ran while one was open for 1% -> 2% of each run, Pallas kernels for 13% -> 13%
where the time goes in v3:
time: 248 us; the launch traced here: 247 us
  blocking collectives  80.5 us (32%)
  waiting for transfers between devices  62.7 us (25%)
  Pallas kernels  59.1 us (24%)
  starting transfers between devices  26.8 us (11%)
  between operations  13.7 us (6%)
  local copies, waits for them, and re-layouts  3.77 us (2%)
    all_to_all x3, blocking collectives, exchange(): return lax.all_to_all(block, axes, split_axis=0, concat_axis=0, tiled=True)  80.5 us
    all_to_all x3, waiting for transfers between devices, exchange(): return lax.all_to_all(block, axes, split_axis=0, concat_axis=0, tiled=True)  59.7 us
    pallas_call x1, Pallas kernels, experts(): pl.pallas_call(experts_kernel, out_shape=jax.ShapeDtypeStruct(x.shape, BF...  24 us
    pallas_call x1, Pallas kernels, attend(): pl.pallas_call(attend_kernel, grid=(PLANE // Q_BLOCKS,), out_shape=jax.Sh...  22.2 us
    all_to_all x3, starting transfers between devices, exchange(): return lax.all_to_all(block, axes, split_axis=0, concat_axis=0, tiled=True)  18.8 us
    pallas_call x1, Pallas kernels, project(): pl.pallas_call(project_kernel, grid=(NZ,), out_shape=jax.ShapeDtypeStruct...  6.81 us
    ppermute x3, starting transfers between devices, around_z(): got.append(lax.ppermute(take(blocks, depth + step), 'z', route))  6.58 us
  transfers between devices with their start and end apart: 14, of which 5 were waited for; matrix products, arithmetic and copies ran while one was open for 2% of the time, Pallas kernels for 13%

profile of v3, /device:TPU:0, one launch (start us, length us, event | category | flops | bytes accessed | tf_op | source)
XLA Modules:
  0.0 247.2 jit_solution(8047431882663942816)
XLA Ops:
  6.6 0.7 all-gather.2.cloned.1.call-update
  7.3 2.1 broadcast_in_dim.7
  9.4 7.1 %all-to-all-start = ((bf16[16,64,640]{2,1,0:T(8,128)(2,1)}), bf16[16,64,640]{2,1,0:T(8,128)(2,1)S(1)}, u32[]{:S(2)}, u32[]{:S(2)}) async-start(bf16[16,64,640]{2,1,0:T(8,128)(2,1)} %broadcast_in_dim.7), calls=%async_computation | async-start | bytes 2621440 | tf_op jit(solution)/shard_map/all_to_all | solution.py:47
  16.9 2.0 collective-permute-start
  18.8 3.6 %collective-permute-start.1 = (bf16[16,1280]{1,0:T(8,128)(2,1)S(1)}, bf16[16,1280]{1,0:T(8,128)(2,1)S(1)}, u32[]{:S(2)}, u32[]{:S(2)}) collective-permute-start(bf16[16,1280]{1,0:T(8,128)(2,1)S(1)} %get-tuple-element.33), channel_id=1, source_target_pairs={{0,2},{1,3},{2,0},{3,1},{4,6},{5,7},{6,4},{7,5},{8,10},{9,11},{10,... | collective-permute-start | bytes 122888 | tf_op jit(solution)/shard_map/ppermute | solution.py:59
  22.4 1.0 collective-permute-start.2
  24.0 0.8 collective-permute-done.1
  24.8 1.6 collective-permute-done.2
  26.5 1.0 routing.1
  27.5 11.4 %all-to-all-done.q_ref = bf16[16,64,640]{2,1,0:T(8,128)(2,1)S(1)} async-done(((bf16[16,64,640]{2,1,0:T(8,128)(2,1)}), bf16[16,64,640]{2,1,0:T(8,128)(2,1)S(1)}, u32[]{:S(2)}, u32[]{:S(2)}) %all-to-all-start) | async-done | bytes 1310752 | tf_op jit(solution)/shard_map/all_to_all | solution.py:47
  40.3 22.2 %attend.1 = bf16[16,328,128]{2,1,0:T(8,128)(2,1)} custom-call(s32[2]{0:T(128)} %pad_add_fusion.place_ref, bf16[16,64,640]{2,1,0:T(8,128)(2,1)} %copy-done, bf16[1024,640]{1,0:T(8,128)(2,1)} %ka_ref.1, bf16[1024,640]{1,0:T(8,128)(2,1)} %collective-permute-done.3.kb_ref, bf16[64,640]{1,0:T(8,128)(2,1)} %na_ref.1, bf16[64,640]{1,0:T(8,128)(2,1)} %copy-done.5, ...), custom_call_target="tpu_custom_call" | custom-call | flops 11000000512 | bytes 10000000 | tf_op jit(solution)/shard_map/attend/pallas_call | solution.py:129
  62.6 25.4 %all_to_all.30.parts_ref = bf16[16,328,128]{2,1,0:T(8,128)(2,1)} all-to-all(bf16[16,328,128]{2,1,0:T(8,128)(2,1)} %attend.1), channel_id=1, replica_groups=mesh['y'=4,'xh'=2,'xl'=2,'c'=2,'z'=4] {'y','xh','xl'}, dimensions={0} | all-to-all | bytes 2686976 | tf_op jit(solution)/shard_map/all_to_all | solution.py:47
  88.0 6.8 %project.1 = bf16[4,64,1152]{2,1,0:T(8,128)(2,1)} custom-call(bf16[16,328,128]{2,1,0:T(8,128)(2,1)} %all_to_all.30.parts_ref, bf16[4608,640]{1,0:T(8,128)(2,1)} %all-gather.2.cloned.1.call-done.weight_ref), custom_call_target="tpu_custom_call" | custom-call | flops 400000000 | bytes 8000000 | tf_op jit(solution)/shard_map/project/pallas_call | solution.py:178
  94.8 5.8 %all-to-all-start.2 = ((bf16[4,64,1152]{2,1,0:T(8,128)(2,1)}), bf16[4,64,1152]{2,1,0:T(8,128)(2,1)S(1)}, u32[]{:S(2)}, u32[]{:S(2)}) async-start(bf16[4,64,1152]{2,1,0:T(8,128)(2,1)} %project.1), calls=%async_computation.2 | async-start | bytes 1179648 | tf_op jit(solution)/shard_map/all_to_all | solution.py:47
  100.6 0.8 dynamic_slice.36
  101.4 8.7 %all-to-all-done.2.heads_ref = bf16[4,64,1152]{2,1,0:T(8,128)(2,1)S(1)} async-done(((bf16[4,64,1152]{2,1,0:T(8,128)(2,1)}), bf16[4,64,1152]{2,1,0:T(8,128)(2,1)S(1)}, u32[]{:S(2)}, u32[]{:S(2)}) %all-to-all-start.2) | async-done | bytes 589856 | tf_op jit(solution)/shard_map/all_to_all | solution.py:47
  110.1 2.7 %pack.1 = (bf16[64,1152]{1,0:T(8,128)(2,1)S(1)}, bf16[4,8,2,16,1536]{4,3,2,1,0:T(8,128)(2,1)}) custom-call(bf16[4,64,1152]{2,1,0:T(8,128)(2,1)S(1)} %all-to-all-done.2.heads_ref, bf16[64,1280]{1,0:T(8,128)(2,1)S(1)} %bitcast.30, f32[1,1152]{1,0:T(1,128)S(1)} %broadcast_in_dim.8.gain_ref, bf16[128,64]{1,0:T(8,128)(2,1)S(1)} %get-tuple-element.18.main_ref, ...), custom_call_target="tpu_custom_call" | custom-call | flops 30000000 | bytes 5000000 | tf_op jit(solution)/shard_map/pack/pallas_call | solution.py:243
  112.8 5.8 %all-to-all-start.3 = ((bf16[64,16,1536]{2,1,0:T(8,128)(2,1)}), bf16[64,16,1536]{2,1,0:T(8,128)(2,1)}, u32[]{:S(2)}, u32[]{:S(2)}) async-start(bf16[64,16,1536]{2,1,0:T(8,128)(2,1)} %bitcast.11), calls=%async_computation.3 | async-start | bytes 6291456 | tf_op jit(solution)/shard_map/all_to_all | solution.py:47
  118.7 39.5 %all-to-all-done.3 = bf16[64,16,1536]{2,1,0:T(8,128)(2,1)} async-done(((bf16[64,16,1536]{2,1,0:T(8,128)(2,1)}), bf16[64,16,1536]{2,1,0:T(8,128)(2,1)}, u32[]{:S(2)}, u32[]{:S(2)}) %all-to-all-start.3) | async-done | bytes 3145760 | tf_op jit(solution)/shard_map/all_to_all | solution.py:47
  158.2 24.0 %experts.1 = bf16[4,256,1536]{2,1,0:T(8,128)(2,1)} custom-call(bf16[4,256,1536]{2,1,0:T(8,128)(2,1)} %bitcast.12.x_any, bf16[4608,768]{1,0:T(8,128)(2,1)} %ga_hbm.1, bf16[4608,768]{1,0:T(8,128)(2,1)} %collective-permute-done.7.gb_hbm, bf16[4608,768]{1,0:T(8,128)(2,1)} %ua_hbm.1, bf16[4608,768]{1,0:T(8,128)(2,1)} %collective-permute-done.8.ub_hbm, ...), custom_call_target="tpu_custom_call" | custom-call | flops 14000000000 | bytes 48000000 | tf_op jit(solution)/shard_map/experts/pallas_call | solution.py:388
  182.2 46.7 %all_to_all.31 = bf16[64,16,1536]{2,1,0:T(8,128)(2,1)S(1)} all-to-all(bf16[64,16,1536]{2,1,0:T(8,128)(2,1)} %bitcast.32), channel_id=1, replica_groups=mesh['y'=4,'xh'=2,'xl'=2,'c'=2,'z'=4] {'z','y','xh','xl'}, dimensions={0} | all-to-all | bytes 6291456 | tf_op jit(solution)/shard_map/all_to_all | solution.py:47
  228.9 2.4 combine.1
  231.3 8.4 %all_to_all.32 = bf16[4,16,1152]{2,1,0:T(8,128)(2,1)S(1)} all-to-all(bf16[4,16,1152]{2,1,0:T(8,128)(2,1)S(1)} %bitcast.31), channel_id=1, replica_groups=mesh['y'=4,'xh'=2,'xl'=2,'c'=2,'z'=4] {'z'}, dimensions={0} | all-to-all | bytes 294912 | tf_op jit(solution)/shard_map/all_to_all | solution.py:47
  239.7 0.7 copy.19
  (47 shorter events, 2.3 us)
Async XLA Ops:
  6.5 10.0 %copy-start.2 = (f32[16,2]{0,1:T(2,128)S(1)}, f32[16,2]{0,1:T(2,128)}, u32[]{:S(2)}) copy-start(f32[16,2]{0,1:T(2,128)} %param.22) | copy-start | bytes 388
  6.5 10.0 %copy-start.7 = (s32[16,2]{0,1:T(2,128)S(1)}, s32[16,2]{0,1:T(2,128)}, u32[]{:S(2)}) copy-start(s32[16,2]{0,1:T(2,128)} %param.21) | copy-start | bytes 388
  6.5 10.2 %copy-start.1 = (bf16[16,4608]{1,0:T(8,128)(2,1)S(1)}, bf16[16,4608]{1,0:T(8,128)(2,1)}, u32[]{:S(2)}) copy-start(bf16[16,4608]{1,0:T(8,128)(2,1)} %param.13) | copy-start | bytes 442372
  6.5 16.9 %copy-start.3 = (bf16[64,640]{1,0:T(8,128)(2,1)S(1)}, bf16[64,640]{1,0:T(8,128)(2,1)}, u32[]{:S(2)}) copy-start(bf16[64,640]{1,0:T(8,128)(2,1)} %na_ref.1) | copy-start | bytes 245764
  6.5 16.9 %copy-start.4 = (bf16[64,640]{1,0:T(8,128)(2,1)S(1)}, bf16[64,640]{1,0:T(8,128)(2,1)}, u32[]{:S(2)}) copy-start(bf16[64,640]{1,0:T(8,128)(2,1)} %wa_ref.1) | copy-start | bytes 245764
  6.6 81.4 %all-gather.2.cloned.1.call-start = ((), (), s32[]{:S(2)}) async-start(), calls=%async_computation.6 | async-start | bytes 6082560 | tf_op jit(solution)/shard_map/all_gather | solution.py:545
  9.4 29.5 %all-to-all-start = ((bf16[16,64,640]{2,1,0:T(8,128)(2,1)}), bf16[16,64,640]{2,1,0:T(8,128)(2,1)S(1)}, u32[]{:S(2)}, u32[]{:S(2)}) async-start(bf16[16,64,640]{2,1,0:T(8,128)(2,1)} %broadcast_in_dim.7), calls=%async_computation | async-start | bytes 2621440 | tf_op jit(solution)/shard_map/all_to_all | solution.py:47
  16.9 7.1 %collective-permute-start = (bf16[16,1280]{1,0:T(8,128)(2,1)S(1)}, bf16[16,1280]{1,0:T(8,128)(2,1)S(1)}, u32[]{:S(2)}, u32[]{:S(2)}) collective-permute-start(bf16[16,1280]{1,0:T(8,128)(2,1)S(1)} %get-tuple-element.32), channel_id=1, source_target_pairs={{0,1},{1,2},{2,3},{3,0},{4,5},{5,6},{6,7},{7,4},{8,9},{9,10},{10,1... | collective-permute-start | bytes 122888 | tf_op jit(solution)/shard_map/ppermute | solution.py:59
  18.8 6.0 %collective-permute-start.1 = (bf16[16,1280]{1,0:T(8,128)(2,1)S(1)}, bf16[16,1280]{1,0:T(8,128)(2,1)S(1)}, u32[]{:S(2)}, u32[]{:S(2)}) collective-permute-start(bf16[16,1280]{1,0:T(8,128)(2,1)S(1)} %get-tuple-element.33), channel_id=1, source_target_pairs={{0,2},{1,3},{2,0},{3,1},{4,6},{5,7},{6,4},{7,5},{8,10},{9,11},{10,... | collective-permute-start | bytes 122888 | tf_op jit(solution)/shard_map/ppermute | solution.py:59
  22.4 4.0 %collective-permute-start.2 = (bf16[16,1280]{1,0:T(8,128)(2,1)S(1)}, bf16[16,1280]{1,0:T(8,128)(2,1)S(1)}, u32[]{:S(2)}, u32[]{:S(2)}) collective-permute-start(bf16[16,1280]{1,0:T(8,128)(2,1)S(1)} %get-tuple-element.34), channel_id=1, source_target_pairs={{0,3},{1,0},{2,1},{3,2},{4,7},{5,4},{6,5},{7,6},{8,11},{9,8},{10,9... | collective-permute-start | bytes 122888 | tf_op jit(solution)/shard_map/ppermute | solution.py:59
  23.4 15.5 %collective-permute-start.4 = (bf16[64,640]{1,0:T(8,128)(2,1)S(1)}, bf16[64,640]{1,0:T(8,128)(2,1)S(1)}, u32[]{:S(2)}, u32[]{:S(2)}) collective-permute-start(bf16[64,640]{1,0:T(8,128)(2,1)S(1)} %copy-done.3), channel_id=1, source_target_pairs={{0,4},{4,0},{1,5},{5,1},{2,6},{6,2},{3,7},{7,3},{8,12},{12,8},{9,1... | collective-permute-start | bytes 245768 | tf_op jit(solution)/shard_map/ppermute | solution.py:51
  23.4 16.0 %collective-permute-start.6 = (bf16[64,640]{1,0:T(8,128)(2,1)S(1)}, bf16[64,640]{1,0:T(8,128)(2,1)S(1)}, u32[]{:S(2)}, u32[]{:S(2)}) collective-permute-start(bf16[64,640]{1,0:T(8,128)(2,1)S(1)} %copy-done.4), channel_id=1, source_target_pairs={{0,4},{4,0},{1,5},{5,1},{2,6},{6,2},{3,7},{7,3},{8,12},{12,8},{9,1... | collective-permute-start | bytes 245768 | tf_op jit(solution)/shard_map/ppermute | solution.py:51
  24.0 16.4 %collective-permute-start.3 = (bf16[1024,640]{1,0:T(8,128)(2,1)}, bf16[1024,640]{1,0:T(8,128)(2,1)}, u32[]{:S(2)}, u32[]{:S(2)}) collective-permute-start(bf16[1024,640]{1,0:T(8,128)(2,1)} %ka_ref.1), channel_id=1, source_target_pairs={{0,4},{4,0},{1,5},{5,1},{2,6},{6,2},{3,7},{7,3},{8,12},{12,8},{9,1... | collective-permute-start | bytes 3932168 | tf_op jit(solution)/shard_map/ppermute | solution.py:51
  24.8 15.5 %collective-permute-start.5 = (bf16[1024,640]{1,0:T(8,128)(2,1)}, bf16[1024,640]{1,0:T(8,128)(2,1)}, u32[]{:S(2)}, u32[]{:S(2)}) collective-permute-start(bf16[1024,640]{1,0:T(8,128)(2,1)} %va_ref.1), channel_id=1, source_target_pairs={{0,4},{4,0},{1,5},{5,1},{2,6},{6,2},{3,7},{7,3},{8,12},{12,8},{9,1... | collective-permute-start | bytes 3932168 | tf_op jit(solution)/shard_map/ppermute | solution.py:51
  38.9 1.4 copy-start
  38.9 79.7 %collective-permute-start.7 = (bf16[4608,768]{1,0:T(8,128)(2,1)}, bf16[4608,768]{1,0:T(8,128)(2,1)}, u32[]{:S(2)}, u32[]{:S(2)}) collective-permute-start(bf16[4608,768]{1,0:T(8,128)(2,1)} %ga_hbm.1), channel_id=1, source_target_pairs={{0,4},{4,0},{1,5},{5,1},{2,6},{6,2},{3,7},{7,3},{8,12},{12,8},{9,1... | collective-permute-start | bytes 21233672 | tf_op jit(solution)/shard_map/ppermute | solution.py:51
  38.9 1.4 copy-start.5
  39.0 79.7 %collective-permute-start.8 = (bf16[4608,768]{1,0:T(8,128)(2,1)}, bf16[4608,768]{1,0:T(8,128)(2,1)}, u32[]{:S(2)}, u32[]{:S(2)}) collective-permute-start(bf16[4608,768]{1,0:T(8,128)(2,1)} %ua_hbm.1), channel_id=1, source_target_pairs={{0,4},{4,0},{1,5},{5,1},{2,6},{6,2},{3,7},{7,3},{8,12},{12,8},{9,1... | collective-permute-start | bytes 21233672 | tf_op jit(solution)/shard_map/ppermute | solution.py:51
  39.5 0.9 copy-start.6
  39.5 79.2 %collective-permute-start.9 = (bf16[768,4608]{1,0:T(8,128)(2,1)}, bf16[768,4608]{1,0:T(8,128)(2,1)}, u32[]{:S(2)}, u32[]{:S(2)}) collective-permute-start(bf16[768,4608]{1,0:T(8,128)(2,1)} %da_hbm.1), channel_id=1, source_target_pairs={{0,4},{4,0},{1,5},{5,1},{2,6},{6,2},{3,7},{7,3},{8,12},{12,8},{9,1... | collective-permute-start | bytes 21233672 | tf_op jit(solution)/shard_map/ppermute | solution.py:51
  94.8 15.3 %all-to-all-start.2 = ((bf16[4,64,1152]{2,1,0:T(8,128)(2,1)}), bf16[4,64,1152]{2,1,0:T(8,128)(2,1)S(1)}, u32[]{:S(2)}, u32[]{:S(2)}) async-start(bf16[4,64,1152]{2,1,0:T(8,128)(2,1)} %project.1), calls=%async_computation.2 | async-start | bytes 1179648 | tf_op jit(solution)/shard_map/all_to_all | solution.py:47
  112.8 45.4 %all-to-all-start.3 = ((bf16[64,16,1536]{2,1,0:T(8,128)(2,1)}), bf16[64,16,1536]{2,1,0:T(8,128)(2,1)}, u32[]{:S(2)}, u32[]{:S(2)}) async-start(bf16[64,16,1536]{2,1,0:T(8,128)(2,1)} %bitcast.11), calls=%async_computation.3 | async-start | bytes 6291456 | tf_op jit(solution)/shard_map/all_to_all | solution.py:47
Sparse Core Ops, SparseCore 0:
  9.7 64.8 all-gather.1

commit v4 on v3

--- a/solution.py
+++ b/solution.py
@@ -165,27 +165,34 @@
         out_ref[:, h * HD : (h + 1) * HD] = (acc / total).astype(BF16)
 
 
-def project_kernel(parts_ref, weight_ref, out_ref, attended_ref):
-    @pl.when(pl.program_id(0) == 0)
-    def _():
-        merge(parts_ref, attended_ref)
-
-    out_ref[0] = dot_nt(attended_ref[...], weight_ref[...]).astype(BF16)
+def project_kernel(parts_ref, weight_hbm, out_ref, attended_ref, weight_ref, sems):
+    pieces = [
+        pltpu.make_async_copy(
+            weight_hbm.at[z * SLICE : (z + 1) * SLICE, :], weight_ref.at[z], sems.at[z]
+        )
+        for z in range(NZ)
+    ]
+    for piece in pieces:
+        piece.start()
+    merge(parts_ref, attended_ref)
+    for z, piece in enumerate(pieces):
+        piece.wait()
+        out_ref[z] = dot_nt(attended_ref[...], weight_ref[z]).astype(BF16)
 
 
 def project(parts, weight):
     width = HEADS * HD
     return pl.pallas_call(
         project_kernel,
-        grid=(NZ,),
         out_shape=jax.ShapeDtypeStruct((NZ, Q_DEV, SLICE), BF16),
-        in_specs=[
-            pl.BlockSpec(parts.shape, lambda i: (0, 0, 0)),
-            pl.BlockSpec((SLICE, width), lambda i: (i, 0)),
+        in_specs=[VMEM, HBM],
+        out_specs=VMEM,
+        scratch_shapes=[
+            pltpu.VMEM((Q_DEV, width), BF16),
+            pltpu.VMEM((NZ, SLICE, width), BF16),
+            pltpu.SemaphoreType.DMA((NZ,)),
         ],
-        out_specs=pl.BlockSpec((1, Q_DEV, SLICE), lambda i: (i, 0, 0)),
-        scratch_shapes=[pltpu.VMEM((Q_DEV, width), BF16)],
-        compiler_params=params(58),
+        compiler_params=params(56),
         cost_estimate=pl.CostEstimate(flops=4 * 10**8, bytes_accessed=8 * 10**6, transcendentals=0),
         name="project",
     )(parts, weight)
@@ -311,23 +318,26 @@
 
 def experts_kernel(
     x_any, ga_hbm, gb_hbm, ua_hbm, ub_hbm, da_hbm, db_hbm, out_hbm,
-    made_ref, rows_ref, scale_ref, hidden_ref, gate_ref, up_ref, down_ref, x_sem, weight_sem, down_sem, out_sem,
+    made_ref, rows_ref, scale_ref, hidden_ref, both_ref, down_ref, x_sem, weight_sem, down_sem, out_sem,
 ):
-    steps = ga_hbm.shape[1] // F_BLOCK
+    half = da_hbm.shape[0]
+    steps = half // F_BLOCK
 
     def weight_copies(step, gate_hbm, up_hbm, block):
         cols = pl.ds(pl.multiple_of(block * F_BLOCK, F_BLOCK), F_BLOCK)
         slot = lax.rem(step, SLOTS)
         return (
-            pltpu.make_async_copy(gate_hbm.at[:, cols], gate_ref.at[slot], weight_sem.at[0, slot]),
-            pltpu.make_async_copy(up_hbm.at[:, cols], up_ref.at[slot], weight_sem.at[1, slot]),
+            pltpu.make_async_copy(gate_hbm.at[:, cols], both_ref.at[slot, :, :F_BLOCK], weight_sem.at[0, slot]),
+            pltpu.make_async_copy(up_hbm.at[:, cols], both_ref.at[slot, :, F_BLOCK:], weight_sem.at[1, slot]),
         )
 
     def down_copies():
         return [
             [
                 pltpu.make_async_copy(
-                    hbm.at[:, z * SLICE : (z + 1) * SLICE], down_ref.at[side, z], down_sem.at[side, z]
+                    hbm.at[:, z * SLICE : (z + 1) * SLICE],
+                    down_ref.at[z, side * half : (side + 1) * half, :],
+                    down_sem.at[side, z],
                 )
                 for side, hbm in enumerate((da_hbm, db_hbm))
             ]
@@ -365,18 +375,16 @@
         for copy in weight_copies(step, ga_hbm, ua_hbm, 0):
             copy.wait()
         slot = lax.rem(step, SLOTS)
-        gate = dot_nn(rows_ref[...], gate_ref[slot]) * scale_ref[:, :1]
-        up = dot_nn(rows_ref[...], up_ref[slot]) * scale_ref[:, :1]
+        both = dot_nn(rows_ref[...], both_ref[slot]) * scale_ref[:, :1]
+        gate, up = both[:, :F_BLOCK], both[:, F_BLOCK:]
         to = pl.ds(pl.multiple_of(step * F_BLOCK, F_BLOCK), F_BLOCK)
         hidden_ref[:, to] = (gate / (1.0 + jnp.exp(-gate)) * up).astype(BF16)
 
-    half = da_hbm.shape[0]
     sent = []
     for z, pair in enumerate(down_copies()):
         for copy in pair:
             copy.wait()
-        answer = dot_nn(hidden_ref[:, :half], down_ref[0, z]) + dot_nn(hidden_ref[:, half:], down_ref[1, z])
-        repack(answer.astype(BF16), made_ref, z)
+        repack(dot_nn(hidden_ref[...], down_ref[z]).astype(BF16), made_ref, z)
         sent.append(pltpu.make_async_copy(made_ref.at[z], out_hbm.at[z], out_sem.at[z]))
         sent[-1].start()
     for copy in sent:
@@ -395,9 +403,8 @@
             pltpu.VMEM((ALL, D), BF16),
             pltpu.VMEM((ALL, HD), F32),
             pltpu.VMEM((ALL, 2 * width), BF16),
-            pltpu.VMEM((SLOTS, D, F_BLOCK), BF16),
-            pltpu.VMEM((SLOTS, D, F_BLOCK), BF16),
-            pltpu.VMEM((2, NZ, width, SLICE), BF16),
+            pltpu.VMEM((SLOTS, D, 2 * F_BLOCK), BF16),
+            pltpu.VMEM((NZ, 2 * width, SLICE), BF16),
             pltpu.SemaphoreType.DMA,
             pltpu.SemaphoreType.DMA((2, SLOTS)),
             pltpu.SemaphoreType.DMA((2, NZ)),

time: 248 us -> 247 us (level)
  no operation moved by 1% of the time
where the time goes in v4:
time: 247 us; the launch traced here: 246 us
  blocking collectives  80.5 us (33%)
  waiting for transfers between devices  62.7 us (25%)
  Pallas kernels  58.2 us (24%)
  starting transfers between devices  26.6 us (11%)
  between operations  13.7 us (6%)
  local copies, waits for them, and re-layouts  3.77 us (2%)
    all_to_all x3, blocking collectives, exchange(): return lax.all_to_all(block, axes, split_axis=0, concat_axis=0, tiled=True)  80.5 us
    all_to_all x3, waiting for transfers between devices, exchange(): return lax.all_to_all(block, axes, split_axis=0, concat_axis=0, tiled=True)  59.7 us
    pallas_call x1, Pallas kernels, experts(): pl.pallas_call(experts_kernel, out_shape=jax.ShapeDtypeStruct(x.shape, BF...  23.9 us
    pallas_call x1, Pallas kernels, attend(): pl.pallas_call(attend_kernel, grid=(PLANE // Q_BLOCKS,), out_shape=jax.Sh...  22.2 us
    all_to_all x3, starting transfers between devices, exchange(): return lax.all_to_all(block, axes, split_axis=0, concat_axis=0, tiled=True)  18.6 us
    ppermute x3, starting transfers between devices, around_z(): got.append(lax.ppermute(take(blocks, depth + step), 'z', route))  6.58 us
    pallas_call x1, Pallas kernels, project(): pl.pallas_call(project_kernel, out_shape=jax.ShapeDtypeStruct((NZ, Q_DEV,...  5.98 us
  transfers between devices with their start and end apart: 14, of which 5 were waited for; matrix products, arithmetic and copies ran while one was open for 2% of the time, Pallas kernels for 13%

profile of v4, /device:TPU:0, one launch (start us, length us, event | category | flops | bytes accessed | tf_op | source)
XLA Modules:
  0.0 246.1 jit_solution(7040577996831797992)
XLA Ops:
  6.6 0.7 all-gather.2.cloned.1.call-update
  7.3 2.1 broadcast_in_dim.7
  9.4 7.1 %all-to-all-start = ((bf16[16,64,640]{2,1,0:T(8,128)(2,1)}), bf16[16,64,640]{2,1,0:T(8,128)(2,1)S(1)}, u32[]{:S(2)}, u32[]{:S(2)}) async-start(bf16[16,64,640]{2,1,0:T(8,128)(2,1)} %broadcast_in_dim.7), calls=%async_computation | async-start | bytes 2621440 | tf_op jit(solution)/shard_map/all_to_all | solution.py:47
  16.9 2.0 collective-permute-start
  18.8 3.6 %collective-permute-start.1 = (bf16[16,1280]{1,0:T(8,128)(2,1)S(1)}, bf16[16,1280]{1,0:T(8,128)(2,1)S(1)}, u32[]{:S(2)}, u32[]{:S(2)}) collective-permute-start(bf16[16,1280]{1,0:T(8,128)(2,1)S(1)} %get-tuple-element.33), channel_id=1, source_target_pairs={{0,2},{1,3},{2,0},{3,1},{4,6},{5,7},{6,4},{7,5},{8,10},{9,11},{10,... | collective-permute-start | bytes 122888 | tf_op jit(solution)/shard_map/ppermute | solution.py:59
  22.4 1.0 collective-permute-start.2
  24.0 0.8 collective-permute-done.1
  24.8 1.6 collective-permute-done.2
  26.5 1.0 routing.1
  27.5 11.4 %all-to-all-done.q_ref = bf16[16,64,640]{2,1,0:T(8,128)(2,1)S(1)} async-done(((bf16[16,64,640]{2,1,0:T(8,128)(2,1)}), bf16[16,64,640]{2,1,0:T(8,128)(2,1)S(1)}, u32[]{:S(2)}, u32[]{:S(2)}) %all-to-all-start) | async-done | bytes 1310752 | tf_op jit(solution)/shard_map/all_to_all | solution.py:47
  40.3 22.2 %attend.1 = bf16[16,328,128]{2,1,0:T(8,128)(2,1)} custom-call(s32[2]{0:T(128)} %pad_add_fusion.place_ref, bf16[16,64,640]{2,1,0:T(8,128)(2,1)} %copy-done, bf16[1024,640]{1,0:T(8,128)(2,1)} %ka_ref.1, bf16[1024,640]{1,0:T(8,128)(2,1)} %collective-permute-done.3.kb_ref, bf16[64,640]{1,0:T(8,128)(2,1)} %na_ref.1, bf16[64,640]{1,0:T(8,128)(2,1)} %copy-done.5, ...), custom_call_target="tpu_custom_call" | custom-call | flops 11000000512 | bytes 10000000 | tf_op jit(solution)/shard_map/attend/pallas_call | solution.py:129
  62.6 25.4 %all_to_all.30.parts_ref = bf16[16,328,128]{2,1,0:T(8,128)(2,1)} all-to-all(bf16[16,328,128]{2,1,0:T(8,128)(2,1)} %attend.1), channel_id=1, replica_groups=mesh['y'=4,'xh'=2,'xl'=2,'c'=2,'z'=4] {'y','xh','xl'}, dimensions={0} | all-to-all | bytes 2686976 | tf_op jit(solution)/shard_map/all_to_all | solution.py:47
  88.0 6.0 %project.1 = bf16[4,64,1152]{2,1,0:T(8,128)(2,1)} custom-call(bf16[16,328,128]{2,1,0:T(8,128)(2,1)} %all_to_all.30.parts_ref, bf16[4608,640]{1,0:T(8,128)(2,1)} %all-gather.2.cloned.1.call-done.weight_hbm), custom_call_target="tpu_custom_call" | custom-call | flops 400000000 | bytes 8000000 | tf_op jit(solution)/shard_map/project/pallas_call | solution.py:185
  94.0 5.8 %all-to-all-start.2 = ((bf16[4,64,1152]{2,1,0:T(8,128)(2,1)}), bf16[4,64,1152]{2,1,0:T(8,128)(2,1)S(1)}, u32[]{:S(2)}, u32[]{:S(2)}) async-start(bf16[4,64,1152]{2,1,0:T(8,128)(2,1)} %project.1), calls=%async_computation.2 | async-start | bytes 1179648 | tf_op jit(solution)/shard_map/all_to_all | solution.py:47
  99.8 0.8 dynamic_slice.36
  100.6 8.7 %all-to-all-done.2.heads_ref = bf16[4,64,1152]{2,1,0:T(8,128)(2,1)S(1)} async-done(((bf16[4,64,1152]{2,1,0:T(8,128)(2,1)}), bf16[4,64,1152]{2,1,0:T(8,128)(2,1)S(1)}, u32[]{:S(2)}, u32[]{:S(2)}) %all-to-all-start.2) | async-done | bytes 589856 | tf_op jit(solution)/shard_map/all_to_all | solution.py:47
  109.3 2.7 %pack.1 = (bf16[64,1152]{1,0:T(8,128)(2,1)S(1)}, bf16[4,8,2,16,1536]{4,3,2,1,0:T(8,128)(2,1)}) custom-call(bf16[4,64,1152]{2,1,0:T(8,128)(2,1)S(1)} %all-to-all-done.2.heads_ref, bf16[64,1280]{1,0:T(8,128)(2,1)S(1)} %bitcast.30, f32[1,1152]{1,0:T(1,128)S(1)} %broadcast_in_dim.8.gain_ref, bf16[128,64]{1,0:T(8,128)(2,1)S(1)} %get-tuple-element.18.main_ref, ...), custom_call_target="tpu_custom_call" | custom-call | flops 30000000 | bytes 5000000 | tf_op jit(solution)/shard_map/pack/pallas_call | solution.py:250
  112.0 5.6 %all-to-all-start.3 = ((bf16[64,16,1536]{2,1,0:T(8,128)(2,1)}), bf16[64,16,1536]{2,1,0:T(8,128)(2,1)}, u32[]{:S(2)}, u32[]{:S(2)}) async-start(bf16[64,16,1536]{2,1,0:T(8,128)(2,1)} %bitcast.11), calls=%async_computation.3 | async-start | bytes 6291456 | tf_op jit(solution)/shard_map/all_to_all | solution.py:47
  117.6 39.5 %all-to-all-done.3 = bf16[64,16,1536]{2,1,0:T(8,128)(2,1)} async-done(((bf16[64,16,1536]{2,1,0:T(8,128)(2,1)}), bf16[64,16,1536]{2,1,0:T(8,128)(2,1)}, u32[]{:S(2)}, u32[]{:S(2)}) %all-to-all-start.3) | async-done | bytes 3145760 | tf_op jit(solution)/shard_map/all_to_all | solution.py:47
  157.2 23.9 %experts.1 = bf16[4,256,1536]{2,1,0:T(8,128)(2,1)} custom-call(bf16[4,256,1536]{2,1,0:T(8,128)(2,1)} %bitcast.12.x_any, bf16[4608,768]{1,0:T(8,128)(2,1)} %ga_hbm.1, bf16[4608,768]{1,0:T(8,128)(2,1)} %collective-permute-done.7.gb_hbm, bf16[4608,768]{1,0:T(8,128)(2,1)} %ua_hbm.1, bf16[4608,768]{1,0:T(8,128)(2,1)} %collective-permute-done.8.ub_hbm, ...), custom_call_target="tpu_custom_call" | custom-call | flops 14000000000 | bytes 48000000 | tf_op jit(solution)/shard_map/experts/pallas_call | solution.py:396
  181.1 46.7 %all_to_all.31 = bf16[64,16,1536]{2,1,0:T(8,128)(2,1)S(1)} all-to-all(bf16[64,16,1536]{2,1,0:T(8,128)(2,1)} %bitcast.32), channel_id=1, replica_groups=mesh['y'=4,'xh'=2,'xl'=2,'c'=2,'z'=4] {'z','y','xh','xl'}, dimensions={0} | all-to-all | bytes 6291456 | tf_op jit(solution)/shard_map/all_to_all | solution.py:47
  227.8 2.4 combine.1
  230.2 8.4 %all_to_all.32 = bf16[4,16,1152]{2,1,0:T(8,128)(2,1)S(1)} all-to-all(bf16[4,16,1152]{2,1,0:T(8,128)(2,1)S(1)} %bitcast.31), channel_id=1, replica_groups=mesh['y'=4,'xh'=2,'xl'=2,'c'=2,'z'=4] {'z'}, dimensions={0} | all-to-all | bytes 294912 | tf_op jit(solution)/shard_map/all_to_all | solution.py:47
  238.6 0.7 copy.19
  (47 shorter events, 2.3 us)
Async XLA Ops:
  6.5 10.0 %copy-start.2 = (f32[16,2]{0,1:T(2,128)S(1)}, f32[16,2]{0,1:T(2,128)}, u32[]{:S(2)}) copy-start(f32[16,2]{0,1:T(2,128)} %param.22) | copy-start | bytes 388
  6.5 10.0 %copy-start.7 = (s32[16,2]{0,1:T(2,128)S(1)}, s32[16,2]{0,1:T(2,128)}, u32[]{:S(2)}) copy-start(s32[16,2]{0,1:T(2,128)} %param.21) | copy-start | bytes 388
  6.5 10.2 %copy-start.1 = (bf16[16,4608]{1,0:T(8,128)(2,1)S(1)}, bf16[16,4608]{1,0:T(8,128)(2,1)}, u32[]{:S(2)}) copy-start(bf16[16,4608]{1,0:T(8,128)(2,1)} %param.13) | copy-start | bytes 442372
  6.5 16.9 %copy-start.3 = (bf16[64,640]{1,0:T(8,128)(2,1)S(1)}, bf16[64,640]{1,0:T(8,128)(2,1)}, u32[]{:S(2)}) copy-start(bf16[64,640]{1,0:T(8,128)(2,1)} %na_ref.1) | copy-start | bytes 245764
  6.5 16.9 %copy-start.4 = (bf16[64,640]{1,0:T(8,128)(2,1)S(1)}, bf16[64,640]{1,0:T(8,128)(2,1)}, u32[]{:S(2)}) copy-start(bf16[64,640]{1,0:T(8,128)(2,1)} %wa_ref.1) | copy-start | bytes 245764
  6.6 81.4 %all-gather.2.cloned.1.call-start = ((), (), s32[]{:S(2)}) async-start(), calls=%async_computation.6 | async-start | bytes 6082560 | tf_op jit(solution)/shard_map/all_gather | solution.py:552
  9.4 29.5 %all-to-all-start = ((bf16[16,64,640]{2,1,0:T(8,128)(2,1)}), bf16[16,64,640]{2,1,0:T(8,128)(2,1)S(1)}, u32[]{:S(2)}, u32[]{:S(2)}) async-start(bf16[16,64,640]{2,1,0:T(8,128)(2,1)} %broadcast_in_dim.7), calls=%async_computation | async-start | bytes 2621440 | tf_op jit(solution)/shard_map/all_to_all | solution.py:47
  16.9 7.1 %collective-permute-start = (bf16[16,1280]{1,0:T(8,128)(2,1)S(1)}, bf16[16,1280]{1,0:T(8,128)(2,1)S(1)}, u32[]{:S(2)}, u32[]{:S(2)}) collective-permute-start(bf16[16,1280]{1,0:T(8,128)(2,1)S(1)} %get-tuple-element.32), channel_id=1, source_target_pairs={{0,1},{1,2},{2,3},{3,0},{4,5},{5,6},{6,7},{7,4},{8,9},{9,10},{10,1... | collective-permute-start | bytes 122888 | tf_op jit(solution)/shard_map/ppermute | solution.py:59
  18.8 6.0 %collective-permute-start.1 = (bf16[16,1280]{1,0:T(8,128)(2,1)S(1)}, bf16[16,1280]{1,0:T(8,128)(2,1)S(1)}, u32[]{:S(2)}, u32[]{:S(2)}) collective-permute-start(bf16[16,1280]{1,0:T(8,128)(2,1)S(1)} %get-tuple-element.33), channel_id=1, source_target_pairs={{0,2},{1,3},{2,0},{3,1},{4,6},{5,7},{6,4},{7,5},{8,10},{9,11},{10,... | collective-permute-start | bytes 122888 | tf_op jit(solution)/shard_map/ppermute | solution.py:59
  22.4 4.0 %collective-permute-start.2 = (bf16[16,1280]{1,0:T(8,128)(2,1)S(1)}, bf16[16,1280]{1,0:T(8,128)(2,1)S(1)}, u32[]{:S(2)}, u32[]{:S(2)}) collective-permute-start(bf16[16,1280]{1,0:T(8,128)(2,1)S(1)} %get-tuple-element.34), channel_id=1, source_target_pairs={{0,3},{1,0},{2,1},{3,2},{4,7},{5,4},{6,5},{7,6},{8,11},{9,8},{10,9... | collective-permute-start | bytes 122888 | tf_op jit(solution)/shard_map/ppermute | solution.py:59
  23.4 15.5 %collective-permute-start.4 = (bf16[64,640]{1,0:T(8,128)(2,1)S(1)}, bf16[64,640]{1,0:T(8,128)(2,1)S(1)}, u32[]{:S(2)}, u32[]{:S(2)}) collective-permute-start(bf16[64,640]{1,0:T(8,128)(2,1)S(1)} %copy-done.3), channel_id=1, source_target_pairs={{0,4},{4,0},{1,5},{5,1},{2,6},{6,2},{3,7},{7,3},{8,12},{12,8},{9,1... | collective-permute-start | bytes 245768 | tf_op jit(solution)/shard_map/ppermute | solution.py:51
  23.4 16.0 %collective-permute-start.6 = (bf16[64,640]{1,0:T(8,128)(2,1)S(1)}, bf16[64,640]{1,0:T(8,128)(2,1)S(1)}, u32[]{:S(2)}, u32[]{:S(2)}) collective-permute-start(bf16[64,640]{1,0:T(8,128)(2,1)S(1)} %copy-done.4), channel_id=1, source_target_pairs={{0,4},{4,0},{1,5},{5,1},{2,6},{6,2},{3,7},{7,3},{8,12},{12,8},{9,1... | collective-permute-start | bytes 245768 | tf_op jit(solution)/shard_map/ppermute | solution.py:51
  24.0 16.4 %collective-permute-start.3 = (bf16[1024,640]{1,0:T(8,128)(2,1)}, bf16[1024,640]{1,0:T(8,128)(2,1)}, u32[]{:S(2)}, u32[]{:S(2)}) collective-permute-start(bf16[1024,640]{1,0:T(8,128)(2,1)} %ka_ref.1), channel_id=1, source_target_pairs={{0,4},{4,0},{1,5},{5,1},{2,6},{6,2},{3,7},{7,3},{8,12},{12,8},{9,1... | collective-permute-start | bytes 3932168 | tf_op jit(solution)/shard_map/ppermute | solution.py:51
  24.8 15.5 %collective-permute-start.5 = (bf16[1024,640]{1,0:T(8,128)(2,1)}, bf16[1024,640]{1,0:T(8,128)(2,1)}, u32[]{:S(2)}, u32[]{:S(2)}) collective-permute-start(bf16[1024,640]{1,0:T(8,128)(2,1)} %va_ref.1), channel_id=1, source_target_pairs={{0,4},{4,0},{1,5},{5,1},{2,6},{6,2},{3,7},{7,3},{8,12},{12,8},{9,1... | collective-permute-start | bytes 3932168 | tf_op jit(solution)/shard_map/ppermute | solution.py:51
  38.9 1.4 copy-start
  38.9 78.7 %collective-permute-start.7 = (bf16[4608,768]{1,0:T(8,128)(2,1)}, bf16[4608,768]{1,0:T(8,128)(2,1)}, u32[]{:S(2)}, u32[]{:S(2)}) collective-permute-start(bf16[4608,768]{1,0:T(8,128)(2,1)} %ga_hbm.1), channel_id=1, source_target_pairs={{0,4},{4,0},{1,5},{5,1},{2,6},{6,2},{3,7},{7,3},{8,12},{12,8},{9,1... | collective-permute-start | bytes 21233672 | tf_op jit(solution)/shard_map/ppermute | solution.py:51
  38.9 1.4 copy-start.5
  39.0 78.6 %collective-permute-start.8 = (bf16[4608,768]{1,0:T(8,128)(2,1)}, bf16[4608,768]{1,0:T(8,128)(2,1)}, u32[]{:S(2)}, u32[]{:S(2)}) collective-permute-start(bf16[4608,768]{1,0:T(8,128)(2,1)} %ua_hbm.1), channel_id=1, source_target_pairs={{0,4},{4,0},{1,5},{5,1},{2,6},{6,2},{3,7},{7,3},{8,12},{12,8},{9,1... | collective-permute-start | bytes 21233672 | tf_op jit(solution)/shard_map/ppermute | solution.py:51
  39.5 0.9 copy-start.6
  39.5 78.2 %collective-permute-start.9 = (bf16[768,4608]{1,0:T(8,128)(2,1)}, bf16[768,4608]{1,0:T(8,128)(2,1)}, u32[]{:S(2)}, u32[]{:S(2)}) collective-permute-start(bf16[768,4608]{1,0:T(8,128)(2,1)} %da_hbm.1), channel_id=1, source_target_pairs={{0,4},{4,0},{1,5},{5,1},{2,6},{6,2},{3,7},{7,3},{8,12},{12,8},{9,1... | collective-permute-start | bytes 21233672 | tf_op jit(solution)/shard_map/ppermute | solution.py:51
  94.0 15.4 %all-to-all-start.2 = ((bf16[4,64,1152]{2,1,0:T(8,128)(2,1)}), bf16[4,64,1152]{2,1,0:T(8,128)(2,1)S(1)}, u32[]{:S(2)}, u32[]{:S(2)}) async-start(bf16[4,64,1152]{2,1,0:T(8,128)(2,1)} %project.1), calls=%async_computation.2 | async-start | bytes 1179648 | tf_op jit(solution)/shard_map/all_to_all | solution.py:47
  112.0 45.2 %all-to-all-start.3 = ((bf16[64,16,1536]{2,1,0:T(8,128)(2,1)}), bf16[64,16,1536]{2,1,0:T(8,128)(2,1)}, u32[]{:S(2)}, u32[]{:S(2)}) async-start(bf16[64,16,1536]{2,1,0:T(8,128)(2,1)} %bitcast.11), calls=%async_computation.3 | async-start | bytes 6291456 | tf_op jit(solution)/shard_map/all_to_all | solution.py:47
Sparse Core Ops, SparseCore 0:
  9.7 64.8 all-gather.1

commit v5 on v4

--- a/solution.py
+++ b/solution.py
@@ -346,10 +346,10 @@
 
     arrive = pltpu.make_async_copy(x_any, made_ref, x_sem)
     arrive.start()
+    arrive.wait()
     for step in range(AHEAD):
         for copy in weight_copies(step, ga_hbm, ua_hbm, step):
             copy.start()
-    arrive.wait()
     scale_ref[...] = jnp.broadcast_to(unpack(made_ref, rows_ref), (ALL, HD))
 
     @pl.loop(0, 2 * steps)

time: 247 us -> 246 us (level)
  no operation moved by 1% of the time
where the time goes in v5:
time: 246 us; the launch traced here: 245 us
  blocking collectives  80.5 us (33%)
  waiting for transfers between devices  62.7 us (25%)
  Pallas kernels  57.4 us (23%)
  starting transfers between devices  26.6 us (11%)
  between operations  13.7 us (6%)
  local copies, waits for them, and re-layouts  3.77 us (2%)
    all_to_all x3, blocking collectives, exchange(): return lax.all_to_all(block, axes, split_axis=0, concat_axis=0, tiled=True)  80.5 us
    all_to_all x3, waiting for transfers between devices, exchange(): return lax.all_to_all(block, axes, split_axis=0, concat_axis=0, tiled=True)  59.7 us
    pallas_call x1, Pallas kernels, experts(): pl.pallas_call(experts_kernel, out_shape=jax.ShapeDtypeStruct(x.shape, BF...  23.1 us
    pallas_call x1, Pallas kernels, attend(): pl.pallas_call(attend_kernel, grid=(PLANE // Q_BLOCKS,), out_shape=jax.Sh...  22.2 us
    all_to_all x3, starting transfers between devices, exchange(): return lax.all_to_all(block, axes, split_axis=0, concat_axis=0, tiled=True)  18.6 us
    ppermute x3, starting transfers between devices, around_z(): got.append(lax.ppermute(take(blocks, depth + step), 'z', route))  6.58 us
    pallas_call x1, Pallas kernels, project(): pl.pallas_call(project_kernel, out_shape=jax.ShapeDtypeStruct((NZ, Q_DEV,...  5.98 us
  transfers between devices with their start and end apart: 14, of which 5 were waited for; matrix products, arithmetic and copies ran while one was open for 2% of the time, Pallas kernels for 13%

profile of v5, /device:TPU:0, one launch (start us, length us, event | category | flops | bytes accessed | tf_op | source)
XLA Modules:
  0.0 245.3 jit_solution(15539886048973794468)
XLA Ops:
  6.6 0.7 all-gather.2.cloned.1.call-update
  7.3 2.1 broadcast_in_dim.7
  9.4 7.1 %all-to-all-start = ((bf16[16,64,640]{2,1,0:T(8,128)(2,1)}), bf16[16,64,640]{2,1,0:T(8,128)(2,1)S(1)}, u32[]{:S(2)}, u32[]{:S(2)}) async-start(bf16[16,64,640]{2,1,0:T(8,128)(2,1)} %broadcast_in_dim.7), calls=%async_computation | async-start | bytes 2621440 | tf_op jit(solution)/shard_map/all_to_all | solution.py:47
  16.9 2.0 collective-permute-start
  18.8 3.6 %collective-permute-start.1 = (bf16[16,1280]{1,0:T(8,128)(2,1)S(1)}, bf16[16,1280]{1,0:T(8,128)(2,1)S(1)}, u32[]{:S(2)}, u32[]{:S(2)}) collective-permute-start(bf16[16,1280]{1,0:T(8,128)(2,1)S(1)} %get-tuple-element.33), channel_id=1, source_target_pairs={{0,2},{1,3},{2,0},{3,1},{4,6},{5,7},{6,4},{7,5},{8,10},{9,11},{10,... | collective-permute-start | bytes 122888 | tf_op jit(solution)/shard_map/ppermute | solution.py:59
  22.4 1.0 collective-permute-start.2
  24.0 0.8 collective-permute-done.1
  24.8 1.6 collective-permute-done.2
  26.5 1.0 routing.1
  27.5 11.4 %all-to-all-done.q_ref = bf16[16,64,640]{2,1,0:T(8,128)(2,1)S(1)} async-done(((bf16[16,64,640]{2,1,0:T(8,128)(2,1)}), bf16[16,64,640]{2,1,0:T(8,128)(2,1)S(1)}, u32[]{:S(2)}, u32[]{:S(2)}) %all-to-all-start) | async-done | bytes 1310752 | tf_op jit(solution)/shard_map/all_to_all | solution.py:47
  40.3 22.2 %attend.1 = bf16[16,328,128]{2,1,0:T(8,128)(2,1)} custom-call(s32[2]{0:T(128)} %pad_add_fusion.place_ref, bf16[16,64,640]{2,1,0:T(8,128)(2,1)} %copy-done, bf16[1024,640]{1,0:T(8,128)(2,1)} %ka_ref.1, bf16[1024,640]{1,0:T(8,128)(2,1)} %collective-permute-done.3.kb_ref, bf16[64,640]{1,0:T(8,128)(2,1)} %na_ref.1, bf16[64,640]{1,0:T(8,128)(2,1)} %copy-done.5, ...), custom_call_target="tpu_custom_call" | custom-call | flops 11000000512 | bytes 10000000 | tf_op jit(solution)/shard_map/attend/pallas_call | solution.py:129
  62.6 25.4 %all_to_all.30.parts_ref = bf16[16,328,128]{2,1,0:T(8,128)(2,1)} all-to-all(bf16[16,328,128]{2,1,0:T(8,128)(2,1)} %attend.1), channel_id=1, replica_groups=mesh['y'=4,'xh'=2,'xl'=2,'c'=2,'z'=4] {'y','xh','xl'}, dimensions={0} | all-to-all | bytes 2686976 | tf_op jit(solution)/shard_map/all_to_all | solution.py:47
  88.0 6.0 %project.1 = bf16[4,64,1152]{2,1,0:T(8,128)(2,1)} custom-call(bf16[16,328,128]{2,1,0:T(8,128)(2,1)} %all_to_all.30.parts_ref, bf16[4608,640]{1,0:T(8,128)(2,1)} %all-gather.2.cloned.1.call-done.weight_hbm), custom_call_target="tpu_custom_call" | custom-call | flops 400000000 | bytes 8000000 | tf_op jit(solution)/shard_map/project/pallas_call | solution.py:185
  94.0 5.8 %all-to-all-start.2 = ((bf16[4,64,1152]{2,1,0:T(8,128)(2,1)}), bf16[4,64,1152]{2,1,0:T(8,128)(2,1)S(1)}, u32[]{:S(2)}, u32[]{:S(2)}) async-start(bf16[4,64,1152]{2,1,0:T(8,128)(2,1)} %project.1), calls=%async_computation.2 | async-start | bytes 1179648 | tf_op jit(solution)/shard_map/all_to_all | solution.py:47
  99.8 0.8 dynamic_slice.36
  100.6 8.7 %all-to-all-done.2.heads_ref = bf16[4,64,1152]{2,1,0:T(8,128)(2,1)S(1)} async-done(((bf16[4,64,1152]{2,1,0:T(8,128)(2,1)}), bf16[4,64,1152]{2,1,0:T(8,128)(2,1)S(1)}, u32[]{:S(2)}, u32[]{:S(2)}) %all-to-all-start.2) | async-done | bytes 589856 | tf_op jit(solution)/shard_map/all_to_all | solution.py:47
  109.3 2.7 %pack.1 = (bf16[64,1152]{1,0:T(8,128)(2,1)S(1)}, bf16[4,8,2,16,1536]{4,3,2,1,0:T(8,128)(2,1)}) custom-call(bf16[4,64,1152]{2,1,0:T(8,128)(2,1)S(1)} %all-to-all-done.2.heads_ref, bf16[64,1280]{1,0:T(8,128)(2,1)S(1)} %bitcast.30, f32[1,1152]{1,0:T(1,128)S(1)} %broadcast_in_dim.8.gain_ref, bf16[128,64]{1,0:T(8,128)(2,1)S(1)} %get-tuple-element.18.main_ref, ...), custom_call_target="tpu_custom_call" | custom-call | flops 30000000 | bytes 5000000 | tf_op jit(solution)/shard_map/pack/pallas_call | solution.py:250
  112.0 5.6 %all-to-all-start.3 = ((bf16[64,16,1536]{2,1,0:T(8,128)(2,1)}), bf16[64,16,1536]{2,1,0:T(8,128)(2,1)}, u32[]{:S(2)}, u32[]{:S(2)}) async-start(bf16[64,16,1536]{2,1,0:T(8,128)(2,1)} %bitcast.11), calls=%async_computation.3 | async-start | bytes 6291456 | tf_op jit(solution)/shard_map/all_to_all | solution.py:47
  117.6 39.5 %all-to-all-done.3 = bf16[64,16,1536]{2,1,0:T(8,128)(2,1)} async-done(((bf16[64,16,1536]{2,1,0:T(8,128)(2,1)}), bf16[64,16,1536]{2,1,0:T(8,128)(2,1)}, u32[]{:S(2)}, u32[]{:S(2)}) %all-to-all-start.3) | async-done | bytes 3145760 | tf_op jit(solution)/shard_map/all_to_all | solution.py:47
  157.2 23.1 %experts.1 = bf16[4,256,1536]{2,1,0:T(8,128)(2,1)} custom-call(bf16[4,256,1536]{2,1,0:T(8,128)(2,1)} %bitcast.12.x_any, bf16[4608,768]{1,0:T(8,128)(2,1)} %ga_hbm.1, bf16[4608,768]{1,0:T(8,128)(2,1)} %collective-permute-done.7.gb_hbm, bf16[4608,768]{1,0:T(8,128)(2,1)} %ua_hbm.1, bf16[4608,768]{1,0:T(8,128)(2,1)} %collective-permute-done.8.ub_hbm, ...), custom_call_target="tpu_custom_call" | custom-call | flops 14000000000 | bytes 48000000 | tf_op jit(solution)/shard_map/experts/pallas_call | solution.py:396
  180.3 46.7 %all_to_all.31 = bf16[64,16,1536]{2,1,0:T(8,128)(2,1)S(1)} all-to-all(bf16[64,16,1536]{2,1,0:T(8,128)(2,1)} %bitcast.32), channel_id=1, replica_groups=mesh['y'=4,'xh'=2,'xl'=2,'c'=2,'z'=4] {'z','y','xh','xl'}, dimensions={0} | all-to-all | bytes 6291456 | tf_op jit(solution)/shard_map/all_to_all | solution.py:47
  227.0 2.4 combine.1
  229.4 8.4 %all_to_all.32 = bf16[4,16,1152]{2,1,0:T(8,128)(2,1)S(1)} all-to-all(bf16[4,16,1152]{2,1,0:T(8,128)(2,1)S(1)} %bitcast.31), channel_id=1, replica_groups=mesh['y'=4,'xh'=2,'xl'=2,'c'=2,'z'=4] {'z'}, dimensions={0} | all-to-all | bytes 294912 | tf_op jit(solution)/shard_map/all_to_all | solution.py:47
  237.8 0.7 copy.19
  (47 shorter events, 2.3 us)
Async XLA Ops:
  6.5 10.0 %copy-start.2 = (f32[16,2]{0,1:T(2,128)S(1)}, f32[16,2]{0,1:T(2,128)}, u32[]{:S(2)}) copy-start(f32[16,2]{0,1:T(2,128)} %param.22) | copy-start | bytes 388
  6.5 10.0 %copy-start.7 = (s32[16,2]{0,1:T(2,128)S(1)}, s32[16,2]{0,1:T(2,128)}, u32[]{:S(2)}) copy-start(s32[16,2]{0,1:T(2,128)} %param.21) | copy-start | bytes 388
  6.5 10.2 %copy-start.1 = (bf16[16,4608]{1,0:T(8,128)(2,1)S(1)}, bf16[16,4608]{1,0:T(8,128)(2,1)}, u32[]{:S(2)}) copy-start(bf16[16,4608]{1,0:T(8,128)(2,1)} %param.13) | copy-start | bytes 442372
  6.5 16.9 %copy-start.3 = (bf16[64,640]{1,0:T(8,128)(2,1)S(1)}, bf16[64,640]{1,0:T(8,128)(2,1)}, u32[]{:S(2)}) copy-start(bf16[64,640]{1,0:T(8,128)(2,1)} %na_ref.1) | copy-start | bytes 245764
  6.5 16.9 %copy-start.4 = (bf16[64,640]{1,0:T(8,128)(2,1)S(1)}, bf16[64,640]{1,0:T(8,128)(2,1)}, u32[]{:S(2)}) copy-start(bf16[64,640]{1,0:T(8,128)(2,1)} %wa_ref.1) | copy-start | bytes 245764
  6.6 81.4 %all-gather.2.cloned.1.call-start = ((), (), s32[]{:S(2)}) async-start(), calls=%async_computation.6 | async-start | bytes 6082560 | tf_op jit(solution)/shard_map/all_gather | solution.py:552
  9.4 29.5 %all-to-all-start = ((bf16[16,64,640]{2,1,0:T(8,128)(2,1)}), bf16[16,64,640]{2,1,0:T(8,128)(2,1)S(1)}, u32[]{:S(2)}, u32[]{:S(2)}) async-start(bf16[16,64,640]{2,1,0:T(8,128)(2,1)} %broadcast_in_dim.7), calls=%async_computation | async-start | bytes 2621440 | tf_op jit(solution)/shard_map/all_to_all | solution.py:47
  16.9 7.1 %collective-permute-start = (bf16[16,1280]{1,0:T(8,128)(2,1)S(1)}, bf16[16,1280]{1,0:T(8,128)(2,1)S(1)}, u32[]{:S(2)}, u32[]{:S(2)}) collective-permute-start(bf16[16,1280]{1,0:T(8,128)(2,1)S(1)} %get-tuple-element.32), channel_id=1, source_target_pairs={{0,1},{1,2},{2,3},{3,0},{4,5},{5,6},{6,7},{7,4},{8,9},{9,10},{10,1... | collective-permute-start | bytes 122888 | tf_op jit(solution)/shard_map/ppermute | solution.py:59
  18.8 6.0 %collective-permute-start.1 = (bf16[16,1280]{1,0:T(8,128)(2,1)S(1)}, bf16[16,1280]{1,0:T(8,128)(2,1)S(1)}, u32[]{:S(2)}, u32[]{:S(2)}) collective-permute-start(bf16[16,1280]{1,0:T(8,128)(2,1)S(1)} %get-tuple-element.33), channel_id=1, source_target_pairs={{0,2},{1,3},{2,0},{3,1},{4,6},{5,7},{6,4},{7,5},{8,10},{9,11},{10,... | collective-permute-start | bytes 122888 | tf_op jit(solution)/shard_map/ppermute | solution.py:59
  22.4 4.0 %collective-permute-start.2 = (bf16[16,1280]{1,0:T(8,128)(2,1)S(1)}, bf16[16,1280]{1,0:T(8,128)(2,1)S(1)}, u32[]{:S(2)}, u32[]{:S(2)}) collective-permute-start(bf16[16,1280]{1,0:T(8,128)(2,1)S(1)} %get-tuple-element.34), channel_id=1, source_target_pairs={{0,3},{1,0},{2,1},{3,2},{4,7},{5,4},{6,5},{7,6},{8,11},{9,8},{10,9... | collective-permute-start | bytes 122888 | tf_op jit(solution)/shard_map/ppermute | solution.py:59
  23.4 15.5 %collective-permute-start.4 = (bf16[64,640]{1,0:T(8,128)(2,1)S(1)}, bf16[64,640]{1,0:T(8,128)(2,1)S(1)}, u32[]{:S(2)}, u32[]{:S(2)}) collective-permute-start(bf16[64,640]{1,0:T(8,128)(2,1)S(1)} %copy-done.3), channel_id=1, source_target_pairs={{0,4},{4,0},{1,5},{5,1},{2,6},{6,2},{3,7},{7,3},{8,12},{12,8},{9,1... | collective-permute-start | bytes 245768 | tf_op jit(solution)/shard_map/ppermute | solution.py:51
  23.4 16.0 %collective-permute-start.6 = (bf16[64,640]{1,0:T(8,128)(2,1)S(1)}, bf16[64,640]{1,0:T(8,128)(2,1)S(1)}, u32[]{:S(2)}, u32[]{:S(2)}) collective-permute-start(bf16[64,640]{1,0:T(8,128)(2,1)S(1)} %copy-done.4), channel_id=1, source_target_pairs={{0,4},{4,0},{1,5},{5,1},{2,6},{6,2},{3,7},{7,3},{8,12},{12,8},{9,1... | collective-permute-start | bytes 245768 | tf_op jit(solution)/shard_map/ppermute | solution.py:51
  24.0 16.4 %collective-permute-start.3 = (bf16[1024,640]{1,0:T(8,128)(2,1)}, bf16[1024,640]{1,0:T(8,128)(2,1)}, u32[]{:S(2)}, u32[]{:S(2)}) collective-permute-start(bf16[1024,640]{1,0:T(8,128)(2,1)} %ka_ref.1), channel_id=1, source_target_pairs={{0,4},{4,0},{1,5},{5,1},{2,6},{6,2},{3,7},{7,3},{8,12},{12,8},{9,1... | collective-permute-start | bytes 3932168 | tf_op jit(solution)/shard_map/ppermute | solution.py:51
  24.8 15.5 %collective-permute-start.5 = (bf16[1024,640]{1,0:T(8,128)(2,1)}, bf16[1024,640]{1,0:T(8,128)(2,1)}, u32[]{:S(2)}, u32[]{:S(2)}) collective-permute-start(bf16[1024,640]{1,0:T(8,128)(2,1)} %va_ref.1), channel_id=1, source_target_pairs={{0,4},{4,0},{1,5},{5,1},{2,6},{6,2},{3,7},{7,3},{8,12},{12,8},{9,1... | collective-permute-start | bytes 3932168 | tf_op jit(solution)/shard_map/ppermute | solution.py:51
  38.9 1.4 copy-start
  38.9 78.7 %collective-permute-start.7 = (bf16[4608,768]{1,0:T(8,128)(2,1)}, bf16[4608,768]{1,0:T(8,128)(2,1)}, u32[]{:S(2)}, u32[]{:S(2)}) collective-permute-start(bf16[4608,768]{1,0:T(8,128)(2,1)} %ga_hbm.1), channel_id=1, source_target_pairs={{0,4},{4,0},{1,5},{5,1},{2,6},{6,2},{3,7},{7,3},{8,12},{12,8},{9,1... | collective-permute-start | bytes 21233672 | tf_op jit(solution)/shard_map/ppermute | solution.py:51
  38.9 1.4 copy-start.5
  39.0 78.6 %collective-permute-start.8 = (bf16[4608,768]{1,0:T(8,128)(2,1)}, bf16[4608,768]{1,0:T(8,128)(2,1)}, u32[]{:S(2)}, u32[]{:S(2)}) collective-permute-start(bf16[4608,768]{1,0:T(8,128)(2,1)} %ua_hbm.1), channel_id=1, source_target_pairs={{0,4},{4,0},{1,5},{5,1},{2,6},{6,2},{3,7},{7,3},{8,12},{12,8},{9,1... | collective-permute-start | bytes 21233672 | tf_op jit(solution)/shard_map/ppermute | solution.py:51
  39.5 0.9 copy-start.6
  39.5 78.2 %collective-permute-start.9 = (bf16[768,4608]{1,0:T(8,128)(2,1)}, bf16[768,4608]{1,0:T(8,128)(2,1)}, u32[]{:S(2)}, u32[]{:S(2)}) collective-permute-start(bf16[768,4608]{1,0:T(8,128)(2,1)} %da_hbm.1), channel_id=1, source_target_pairs={{0,4},{4,0},{1,5},{5,1},{2,6},{6,2},{3,7},{7,3},{8,12},{12,8},{9,1... | collective-permute-start | bytes 21233672 | tf_op jit(solution)/shard_map/ppermute | solution.py:51
  94.0 15.4 %all-to-all-start.2 = ((bf16[4,64,1152]{2,1,0:T(8,128)(2,1)}), bf16[4,64,1152]{2,1,0:T(8,128)(2,1)S(1)}, u32[]{:S(2)}, u32[]{:S(2)}) async-start(bf16[4,64,1152]{2,1,0:T(8,128)(2,1)} %project.1), calls=%async_computation.2 | async-start | bytes 1179648 | tf_op jit(solution)/shard_map/all_to_all | solution.py:47
  112.0 45.2 %all-to-all-start.3 = ((bf16[64,16,1536]{2,1,0:T(8,128)(2,1)}), bf16[64,16,1536]{2,1,0:T(8,128)(2,1)}, u32[]{:S(2)}, u32[]{:S(2)}) async-start(bf16[64,16,1536]{2,1,0:T(8,128)(2,1)} %bitcast.11), calls=%async_computation.3 | async-start | bytes 6291456 | tf_op jit(solution)/shard_map/all_to_all | solution.py:47
Sparse Core Ops, SparseCore 0:
  9.7 64.8 all-gather.1
